TPU v7x, 512 devices: a whole 4x4x16 slice. The times are simulated.
512 devices in a mesh: ctx: 64 (over z, x), tp: 8 (over y, core).
Axes of the slice: x: 4, y: 4, z: 16, core: 2. Of those that a mesh axis runs over, the one named last changes fastest.
Arguments:
- tokens: bfloat16 [8192, 3072], P('ctx'), may hold values from -6 to 6
- w_qkv: bfloat16 [3072, 3, 3072], P('ctx', None, 'tp'), may hold values from -0.109375 to 0.109375
- w_rate: bfloat16 [3072, 48], P('ctx', 'tp'), may hold values from -0.109375 to 0.109375
- layer_one: float32 [48, 64, 256], P('tp'), may hold values from -0.75 to 0.75
- layer_two: float32 [48, 64, 256], P('tp'), may hold values from -0.375 to 0.375
- bias_one: float32 [48, 256], P('tp'), may hold values from -3 to 3
- bias_two: float32 [48, 64], P('tp'), may hold values from -3 to 3
- inner_gain: float32 [48, 64], P('tp'), may hold values from 0.3 to 3
- inner_bias: float32 [48, 64], P('tp'), may hold values from -3 to 3
- inner_rate: float32 [48], P('tp'), may hold values from 0.03 to 0.3
- out_gain: float32 [3072], P('tp'), may hold values from 0.25 to 1.75
Outputs:
- mixed: bfloat16 [8192, 3072], P('ctx', 'tp')
All inputs are finite; a program needn't handle non-finite values.
Results may differ from a plain program's by a relative error of at most 0.0045.
Values may be sent and summed in bfloat16 or wider, within the bound.
No kernel may reach another device: no remote copies, remote signals or barrier semaphores. Data moves between devices by JAX's collectives and lax.ppermute only.
A program may use at most 64 MiB of HBM per device.

v0:
```python
import jax
import jax.numpy as jnp
from jax import lax
from jax.sharding import PartitionSpec as P

D = 3072
HD = 64
STEPS = 4
CHAIN = 8


def passed_along(x, axis, by):
    size = lax.axis_size(axis)
    pairs = [(i, i + by) for i in range(size) if 0 <= i + by < size]
    return lax.ppermute(x, axis, pairs)


def head_forward(inner_state, inputs, gain_row, bias_row):
    first_w, second_w, first_b, second_b = inner_state
    hidden = jnp.dot(inputs, first_w, precision=lax.Precision.HIGHEST) + first_b
    active = jax.nn.gelu(hidden, approximate=True)
    mapped = (
        lax.dot_general(active, second_w, (((1,), (1,)), ((), ())), precision=lax.Precision.HIGHEST)
        + second_b
    )
    centre = mapped - jnp.mean(mapped, -1, keepdims=True)
    spread = jnp.mean(centre * centre, -1, keepdims=True)
    return gain_row * centre * lax.rsqrt(spread + 1e-06) + bias_row


def inner_step(inner_state, mini_batch, gain_row, bias_row):
    key_rows, value_rows, query_rows, rate_rows = mini_batch
    target = value_rows - key_rows

    def recon_loss(params):
        residual = head_forward(params, key_rows, gain_row, bias_row) - target
        return 0.5 * jnp.sum(rate_rows[:, None] * residual * residual) / key_rows.shape[0]

    gradient = jax.grad(recon_loss)(inner_state)
    updated = jax.tree.map(lambda tensor, slope: tensor - slope, inner_state, gradient)
    return (updated, query_rows + head_forward(updated, query_rows, gain_row, bias_row))


def head_run(inner_state, key_rows, value_rows, query_rows, rate_rows, gain_row, bias_row):

    def advance(state_now, mini_batch):
        return inner_step(state_now, mini_batch, gain_row, bias_row)

    return lax.scan(advance, inner_state, (key_rows, value_rows, query_rows, rate_rows))


def pack_state(first_w, second_w, first_b, second_b):
    padding = jnp.zeros(
        second_b.shape[:-1] + (first_w.shape[-1] - second_b.shape[-1],), second_b.dtype
    )
    wide_b = jnp.concatenate([second_b, padding], -1)
    return jnp.concatenate([first_w, second_w, first_b[..., None, :], wide_b[..., None, :]], -2)


def unpack(packed):
    return (
        packed[..., :HD, :],
        packed[..., HD : 2 * HD, :],
        packed[..., 2 * HD, :],
        packed[..., 2 * HD + 1, :HD],
    )


def local(
    tokens,
    w_qkv,
    w_rate,
    layer_one,
    layer_two,
    bias_one,
    bias_two,
    inner_gain,
    inner_bias,
    inner_rate,
    out_gain,
):
    tok_count = tokens.shape[0]
    head_count = w_rate.shape[1]
    proj_width = w_qkv.shape[1] * w_qkv.shape[2]
    batch_rows = tok_count // STEPS
    weight_piece = lax.all_gather(w_qkv, "ctx", axis=0, tiled=True)
    rate_piece = lax.all_gather(w_rate, "ctx", axis=0, tiled=True)
    row_count = weight_piece.shape[0]
    proj_sum = jnp.dot(
        tokens, weight_piece.reshape(row_count, proj_width), preferred_element_type=jnp.float32
    )
    logit_sum = jnp.dot(tokens, rate_piece, preferred_element_type=jnp.float32)
    proj_sum, logit_sum = (proj_sum, logit_sum)
    projected = lax.optimization_barrier(proj_sum.astype(jnp.bfloat16)).reshape(
        tok_count, 3, head_count, HD
    )
    rate_vals = inner_rate * jax.nn.sigmoid(logit_sum)

    def arrange(part):
        return jnp.transpose(
            part.astype(jnp.float32).reshape(STEPS, batch_rows, head_count, HD), (2, 0, 1, 3)
        )

    queries = arrange(projected[:, 0])
    key_rows = arrange(projected[:, 1])
    values = arrange(projected[:, 2])
    rate_blocks = jnp.transpose(rate_vals.reshape(STEPS, batch_rows, head_count), (2, 0, 1))
    position = lax.axis_index("ctx") % CHAIN
    initial = pack_state(layer_one, layer_two, bias_one, bias_two)
    results = jnp.zeros((head_count, STEPS, batch_rows, HD), jnp.float32)

    def advance_all(start_state):
        updated, head_outs = jax.vmap(head_run)(
            unpack(start_state), key_rows, values, queries, rate_blocks, inner_gain, inner_bias
        )
        return (pack_state(*updated), head_outs)

    def advance_section(turn_index, carried):
        outgoing, finished = carried
        received = passed_along(outgoing, "ctx", 1)
        start_state = jnp.where(position == 0, initial, received)
        return lax.cond(
            position == turn_index, lambda: advance_all(start_state), lambda: (outgoing, finished)
        )

    _, results = lax.fori_loop(0, CHAIN, advance_section, (initial, results))
    joined = jnp.transpose(results, (1, 2, 0, 3)).reshape(tok_count, head_count * HD)
    feature_sum = lax.psum(jnp.sum(joined, -1), "tp")
    centre = joined - (feature_sum / D)[:, None]
    square_sum = lax.psum(jnp.sum(centre * centre, -1), "tp")
    variance = square_sum / D
    return (centre * lax.rsqrt(variance + 1e-05)[:, None] * out_gain).astype(jnp.bfloat16)


def solution(mesh):
    placed = (
        P("ctx", None),
        P("ctx", None, "tp"),
        P("ctx", "tp"),
        P("tp", None, None),
        P("tp", None, None),
        P("tp", None),
        P("tp", None),
        P("tp", None),
        P("tp", None),
        P("tp"),
        P("tp"),
    )
    return jax.shard_map(
        local, mesh=mesh, in_specs=placed, out_specs=P("ctx", "tp"), check_vma=False
    )
```

profile of v0, /device:TPU:103, one launch (start us, length us, event | category | flops | bytes accessed | tf_op | source)
XLA Modules:
  0.0 532.2 jit_solution(11847672398214245231)
XLA Ops:
  6.5 0.7 all-gather.3.cloned.1.call-update
  7.3 0.7 broadcast_in_dim.52
  8.0 0.7 concatenate.12
  8.7 79.0 %all-gather = bf16[64,48,6]{1,2,0:T(8,128)(2,1)S(1)} all-gather(bf16[1,48,6]{1,2,0:T(8,128)(2,1)} %bitcast.105), channel_id=1, replica_groups=mesh['ctx'=64,'tp'=8] {'ctx'}, dimensions={0}, use_global_device_ids=true | all-gather | bytes 37440 | tf_op jit(solution)/shard_map/all_gather | solution.py:87
  87.9 1.0 fusion.42
  89.0 1.0 pad_maximum_fusion.1
  90.0 2.4 copy.42
  92.4 64.7 %all-gather.3.cloned.1.call-done = bf16[3072,3,384]{2,0,1:T(8,128)(2,1)} async-done(((bf16[48,3,384]{2,0,1:T(8,128)(2,1)}), bf16[3072,3,384]{2,0,1:T(8,128)(2,1)}) %all-gather.3.cloned.1.call-update) | async-done | bytes 7077904 | tf_op jit(solution)/shard_map/all_gather | solution.py:86
  157.1 10.1 %copy.36 = bf16[3072,3,384]{0,2,1:T(8,128)(2,1)} copy(bf16[3072,3,384]{2,0,1:T(8,128)(2,1)} %all-gather.3.cloned.1.call-done) | data formatting | bytes 14155776 | tf_op jit(solution)/shard_map/all_gather | solution.py:86
  167.2 5.4 %convolution_convert_fusion = bf16[128,1152]{1,0:T(8,128)(2,1)S(1)} fusion(bf16[128,3072]{1,0:T(8,128)(2,1)S(1)} %copy-done, bf16[3072,1152]{0,1:T(8,128)(2,1)} %bitcast.99), kind=kOutput, calls=%fused_computation.68 | convolution fusion | flops 906117120 | bytes 8159232 | tf_op jit(solution)/shard_map/dot_general | solution.py:89
  173.4 0.8 broadcast_in_dim.54
  174.2 307.1 %while.36 = (s32[]{:T(128)}, f32[6,130,256]{2,1,0:T(8,128)}, f32[6,4,32,64]{3,2,0,1:T(8,128)}, s32[]{:T(128)}, pred[]{:T(512)}, /*index=5*/f32[6,130,256]{2,0,1:...) while((s32[]{:T(128)}, f32[6,130,256]{2,1,0:T(8,128)}, ...), condition=%wide.region_13.14_spmd, body=%wide.region_0.13_spmd.sunk | while | flops 268076736 | bytes 16762433 | solution.py:126
  174.2 5.2 collective-permute-start
  179.5 10.1 %collective-permute-done = f32[6,130,256]{2,1,0:T(8,128)} collective-permute-done((f32[6,130,256]{2,1,0:T(8,128)}, f32[6,130,256]{2,1,0:T(8,128)}, u32[]{:S(2)}, u32[]{:S(2)}) %collective-permute-start) | collective-permute-done | bytes 798752 | tf_op jit(solution)/shard_map/while/body/eval_jaxpr/ppermute | solution.py:15
  189.5 32.6 %collective-permute-start = (f32[6,130,256]{2,1,0:T(8,128)}, f32[6,130,256]{2,1,0:T(8,128)}, u32[]{:S(2)}, u32[]{:S(2)}) collective-permute-start(f32[6,130,256]{2,1,0:T(8,128)} %get-tuple-element.807), channel_id=1, source_target_pairs={{0,8},{8,16},{16,24},{24,32},{32,40},{40,48},{48,56},{56,64},{64,7... | collective-permute-start | bytes 2396168 | tf_op jit(solution)/shard_map/while/body/eval_jaxpr/ppermute | solution.py:15
  222.2 9.7 %collective-permute-done = f32[6,130,256]{2,1,0:T(8,128)} collective-permute-done((f32[6,130,256]{2,1,0:T(8,128)}, f32[6,130,256]{2,1,0:T(8,128)}, u32[]{:S(2)}, u32[]{:S(2)}) %collective-permute-start) | collective-permute-done | bytes 798752 | tf_op jit(solution)/shard_map/while/body/eval_jaxpr/ppermute | solution.py:15
  231.9 7.1 %collective-permute-start = (f32[6,130,256]{2,1,0:T(8,128)}, f32[6,130,256]{2,1,0:T(8,128)}, u32[]{:S(2)}, u32[]{:S(2)}) collective-permute-start(f32[6,130,256]{2,1,0:T(8,128)} %get-tuple-element.807), channel_id=1, source_target_pairs={{0,8},{8,16},{16,24},{24,32},{32,40},{40,48},{48,56},{56,64},{64,7... | collective-permute-start | bytes 2396168 | tf_op jit(solution)/shard_map/while/body/eval_jaxpr/ppermute | solution.py:15
  239.0 11.3 %collective-permute-done = f32[6,130,256]{2,1,0:T(8,128)} collective-permute-done((f32[6,130,256]{2,1,0:T(8,128)}, f32[6,130,256]{2,1,0:T(8,128)}, u32[]{:S(2)}, u32[]{:S(2)}) %collective-permute-start) | collective-permute-done | bytes 798752 | tf_op jit(solution)/shard_map/while/body/eval_jaxpr/ppermute | solution.py:15
  250.4 21.9 %collective-permute-start = (f32[6,130,256]{2,1,0:T(8,128)}, f32[6,130,256]{2,1,0:T(8,128)}, u32[]{:S(2)}, u32[]{:S(2)}) collective-permute-start(f32[6,130,256]{2,1,0:T(8,128)} %get-tuple-element.807), channel_id=1, source_target_pairs={{0,8},{8,16},{16,24},{24,32},{32,40},{40,48},{48,56},{56,64},{64,7... | collective-permute-start | bytes 2396168 | tf_op jit(solution)/shard_map/while/body/eval_jaxpr/ppermute | solution.py:15
  272.3 9.7 %collective-permute-done = f32[6,130,256]{2,1,0:T(8,128)} collective-permute-done((f32[6,130,256]{2,1,0:T(8,128)}, f32[6,130,256]{2,1,0:T(8,128)}, u32[]{:S(2)}, u32[]{:S(2)}) %collective-permute-start) | collective-permute-done | bytes 798752 | tf_op jit(solution)/shard_map/while/body/eval_jaxpr/ppermute | solution.py:15
  282.0 9.6 %collective-permute-start = (f32[6,130,256]{2,1,0:T(8,128)}, f32[6,130,256]{2,1,0:T(8,128)}, u32[]{:S(2)}, u32[]{:S(2)}) collective-permute-start(f32[6,130,256]{2,1,0:T(8,128)} %get-tuple-element.807), channel_id=1, source_target_pairs={{0,8},{8,16},{16,24},{24,32},{32,40},{40,48},{48,56},{56,64},{64,7... | collective-permute-start | bytes 2396168 | tf_op jit(solution)/shard_map/while/body/eval_jaxpr/ppermute | solution.py:15
  291.6 16.3 %collective-permute-done = f32[6,130,256]{2,1,0:T(8,128)} collective-permute-done((f32[6,130,256]{2,1,0:T(8,128)}, f32[6,130,256]{2,1,0:T(8,128)}, u32[]{:S(2)}, u32[]{:S(2)}) %collective-permute-start) | collective-permute-done | bytes 798752 | tf_op jit(solution)/shard_map/while/body/eval_jaxpr/ppermute | solution.py:15
  307.9 14.5 %collective-permute-start = (f32[6,130,256]{2,1,0:T(8,128)}, f32[6,130,256]{2,1,0:T(8,128)}, u32[]{:S(2)}, u32[]{:S(2)}) collective-permute-start(f32[6,130,256]{2,1,0:T(8,128)} %get-tuple-element.807), channel_id=1, source_target_pairs={{0,8},{8,16},{16,24},{24,32},{32,40},{40,48},{48,56},{56,64},{64,7... | collective-permute-start | bytes 2396168 | tf_op jit(solution)/shard_map/while/body/eval_jaxpr/ppermute | solution.py:15
  322.4 10.0 %collective-permute-done = f32[6,130,256]{2,1,0:T(8,128)} collective-permute-done((f32[6,130,256]{2,1,0:T(8,128)}, f32[6,130,256]{2,1,0:T(8,128)}, u32[]{:S(2)}, u32[]{:S(2)}) %collective-permute-start) | collective-permute-done | bytes 798752 | tf_op jit(solution)/shard_map/while/body/eval_jaxpr/ppermute | solution.py:15
  332.4 17.6 %collective-permute-start = (f32[6,130,256]{2,1,0:T(8,128)}, f32[6,130,256]{2,1,0:T(8,128)}, u32[]{:S(2)}, u32[]{:S(2)}) collective-permute-start(f32[6,130,256]{2,1,0:T(8,128)} %get-tuple-element.807), channel_id=1, source_target_pairs={{0,8},{8,16},{16,24},{24,32},{32,40},{40,48},{48,56},{56,64},{64,7... | collective-permute-start | bytes 2396168 | tf_op jit(solution)/shard_map/while/body/eval_jaxpr/ppermute | solution.py:15
  349.9 17.9 %collective-permute-done = f32[6,130,256]{2,1,0:T(8,128)} collective-permute-done((f32[6,130,256]{2,1,0:T(8,128)}, f32[6,130,256]{2,1,0:T(8,128)}, u32[]{:S(2)}, u32[]{:S(2)}) %collective-permute-start) | collective-permute-done | bytes 798752 | tf_op jit(solution)/shard_map/while/body/eval_jaxpr/ppermute | solution.py:15
  367.9 7.1 %collective-permute-start = (f32[6,130,256]{2,1,0:T(8,128)}, f32[6,130,256]{2,1,0:T(8,128)}, u32[]{:S(2)}, u32[]{:S(2)}) collective-permute-start(f32[6,130,256]{2,1,0:T(8,128)} %get-tuple-element.807), channel_id=1, source_target_pairs={{0,8},{8,16},{16,24},{24,32},{32,40},{40,48},{48,56},{56,64},{64,7... | collective-permute-start | bytes 2396168 | tf_op jit(solution)/shard_map/while/body/eval_jaxpr/ppermute | solution.py:15
  375.0 81.5 %collective-permute-done = f32[6,130,256]{2,1,0:T(8,128)} collective-permute-done((f32[6,130,256]{2,1,0:T(8,128)}, f32[6,130,256]{2,1,0:T(8,128)}, u32[]{:S(2)}, u32[]{:S(2)}) %collective-permute-start) | collective-permute-done | bytes 798752 | tf_op jit(solution)/shard_map/while/body/eval_jaxpr/ppermute | solution.py:15
  456.5 24.9 %conditional.2 = ((f32[6,130,256]{2,1,0:T(8,128)}, f32[6,4,32,64]{3,2,0,1:T(8,128)})) conditional(s32[]{:T(128)} %convert_element_type.52, (f32[6,130,256]{2,1,0:T(8,128)}, f32[6,4,32,64]{3,2,0,1:T(8,128)}) %tuple.81, (pred[]{:T(512)}, f32[6,130,256]{2,0,1:T(8,128)}, f32[6,130,256]{2,1,0:T(8,128)}, f32[4,32,6,64]{3,1,2,0:T(8,128)S(1)}, ...), branch_computations={%region_1.1_spmd, %region_2.12_spmd} | conditional | flops 268076736 | bytes 13567278 | solution.py:122
  456.5 1.5 copy_select_fusion
  458.3 22.0 %while.35 = (s32[]{:T(128)}, f32[6,64,256]{2,1,0:T(8,128)S(1)}, f32[6,64,256]{2,1,0:T(8,128)S(1)}, f32[6,256]{1,0:T(8,128)S(1)}, f32[6,64]{1,0:T(8,128)S(1)}, /*...) while((s32[]{:T(128)}, f32[6,64,256]{2,1,0:T(8,128)S(1)}, ...), condition=%wide.region_12.11_spmd, body=%wide.region_3.10_spmd.sunk | while | flops 267278016 | bytes 6380193 | solution.py:49
  460.7 0.7 convolution_subtract_fusion.5
  463.1 0.8 bitcast_dynamic-update-slice_fusion.2
  466.2 0.7 convolution_subtract_fusion.5
  466.8 0.6 convolution_subtract_fusion.4
  468.6 0.8 bitcast_dynamic-update-slice_fusion.2
  471.7 0.7 convolution_subtract_fusion.5
  474.1 0.8 bitcast_dynamic-update-slice_fusion.2
  477.2 0.7 convolution_subtract_fusion.5
  477.8 0.6 convolution_subtract_fusion.4
  479.6 0.8 bitcast_dynamic-update-slice_fusion.2
  480.4 1.0 pad_maximum_fusion
  481.4 1.1 bitcast_reduce_fusion
  482.6 26.9 %psum.14 = f32[128]{0:T(128)S(1)} all-reduce(f32[128]{0:T(128)S(1)} %reduce_sum.135), channel_id=1, replica_groups=mesh['ctx'=64,'tp'=8] {'tp'}, use_global_device_ids=true, to_apply=%region_15.16 | all-reduce | flops 128 | bytes 1024 | tf_op jit(solution)/shard_map/psum | solution.py:128
  509.5 1.2 multiply_reduce_fusion.3
  510.8 12.4 %psum.15 = f32[128]{0:T(128)S(1)} all-reduce(f32[128]{0:T(128)S(1)} %reduce_sum.137), channel_id=1, replica_groups=mesh['ctx'=64,'tp'=8] {'tp'}, use_global_device_ids=true, to_apply=%region_17.18 | all-reduce | flops 128 | bytes 1024 | tf_op jit(solution)/shard_map/psum | solution.py:130
  523.2 1.2 copy.47
  524.6 0.7 multiply_convert_fusion
  (122 shorter events, 16.3 us)
Async XLA Ops:
  6.5 81.3 %copy-start = (bf16[128,3072]{1,0:T(8,128)(2,1)S(1)}, bf16[128,3072]{1,0:T(8,128)(2,1)}, u32[]{:S(2)}) copy-start(bf16[128,3072]{1,0:T(8,128)(2,1)} %param.17) | copy-start | bytes 2359300
  6.5 82.4 %copy-start.3 = (f32[6,64,256]{2,1,0:T(8,128)S(1)}, f32[6,64,256]{2,1,0:T(8,128)}, u32[]{:S(2)}) copy-start(f32[6,64,256]{2,1,0:T(8,128)} %param.21) | copy-start | bytes 1179652
  6.5 82.4 %copy-start.4 = (f32[6,64,256]{2,1,0:T(8,128)S(1)}, f32[6,64,256]{2,1,0:T(8,128)}, u32[]{:S(2)}) copy-start(f32[6,64,256]{2,1,0:T(8,128)} %param.20) | copy-start | bytes 1179652
  6.5 150.5 %all-gather.3.cloned.1.call-start = ((), (), s32[]{:S(2)}) async-start(), calls=%async_computation | async-start | bytes 7188480 | tf_op jit(solution)/shard_map/all_gather | solution.py:86
  173.2 1.0 copy-start.1
  173.2 1.0 copy-start.2
  174.2 15.3 %collective-permute-start = (f32[6,130,256]{2,1,0:T(8,128)}, f32[6,130,256]{2,1,0:T(8,128)}, u32[]{:S(2)}, u32[]{:S(2)}) collective-permute-start(f32[6,130,256]{2,1,0:T(8,128)} %get-tuple-element.807), channel_id=1, source_target_pairs={{0,8},{8,16},{16,24},{24,32},{32,40},{40,48},{48,56},{56,64},{64,7... | collective-permute-start | bytes 2396168 | tf_op jit(solution)/shard_map/while/body/eval_jaxpr/ppermute | solution.py:15
  189.5 42.4 %collective-permute-start = (f32[6,130,256]{2,1,0:T(8,128)}, f32[6,130,256]{2,1,0:T(8,128)}, u32[]{:S(2)}, u32[]{:S(2)}) collective-permute-start(f32[6,130,256]{2,1,0:T(8,128)} %get-tuple-element.807), channel_id=1, source_target_pairs={{0,8},{8,16},{16,24},{24,32},{32,40},{40,48},{48,56},{56,64},{64,7... | collective-permute-start | bytes 2396168 | tf_op jit(solution)/shard_map/while/body/eval_jaxpr/ppermute | solution.py:15
  231.9 18.4 %collective-permute-start = (f32[6,130,256]{2,1,0:T(8,128)}, f32[6,130,256]{2,1,0:T(8,128)}, u32[]{:S(2)}, u32[]{:S(2)}) collective-permute-start(f32[6,130,256]{2,1,0:T(8,128)} %get-tuple-element.807), channel_id=1, source_target_pairs={{0,8},{8,16},{16,24},{24,32},{32,40},{40,48},{48,56},{56,64},{64,7... | collective-permute-start | bytes 2396168 | tf_op jit(solution)/shard_map/while/body/eval_jaxpr/ppermute | solution.py:15
  250.4 31.6 %collective-permute-start = (f32[6,130,256]{2,1,0:T(8,128)}, f32[6,130,256]{2,1,0:T(8,128)}, u32[]{:S(2)}, u32[]{:S(2)}) collective-permute-start(f32[6,130,256]{2,1,0:T(8,128)} %get-tuple-element.807), channel_id=1, source_target_pairs={{0,8},{8,16},{16,24},{24,32},{32,40},{40,48},{48,56},{56,64},{64,7... | collective-permute-start | bytes 2396168 | tf_op jit(solution)/shard_map/while/body/eval_jaxpr/ppermute | solution.py:15
  282.0 25.8 %collective-permute-start = (f32[6,130,256]{2,1,0:T(8,128)}, f32[6,130,256]{2,1,0:T(8,128)}, u32[]{:S(2)}, u32[]{:S(2)}) collective-permute-start(f32[6,130,256]{2,1,0:T(8,128)} %get-tuple-element.807), channel_id=1, source_target_pairs={{0,8},{8,16},{16,24},{24,32},{32,40},{40,48},{48,56},{56,64},{64,7... | collective-permute-start | bytes 2396168 | tf_op jit(solution)/shard_map/while/body/eval_jaxpr/ppermute | solution.py:15
  307.9 24.5 %collective-permute-start = (f32[6,130,256]{2,1,0:T(8,128)}, f32[6,130,256]{2,1,0:T(8,128)}, u32[]{:S(2)}, u32[]{:S(2)}) collective-permute-start(f32[6,130,256]{2,1,0:T(8,128)} %get-tuple-element.807), channel_id=1, source_target_pairs={{0,8},{8,16},{16,24},{24,32},{32,40},{40,48},{48,56},{56,64},{64,7... | collective-permute-start | bytes 2396168 | tf_op jit(solution)/shard_map/while/body/eval_jaxpr/ppermute | solution.py:15
  332.4 35.5 %collective-permute-start = (f32[6,130,256]{2,1,0:T(8,128)}, f32[6,130,256]{2,1,0:T(8,128)}, u32[]{:S(2)}, u32[]{:S(2)}) collective-permute-start(f32[6,130,256]{2,1,0:T(8,128)} %get-tuple-element.807), channel_id=1, source_target_pairs={{0,8},{8,16},{16,24},{24,32},{32,40},{40,48},{48,56},{56,64},{64,7... | collective-permute-start | bytes 2396168 | tf_op jit(solution)/shard_map/while/body/eval_jaxpr/ppermute | solution.py:15
  367.9 88.6 %collective-permute-start = (f32[6,130,256]{2,1,0:T(8,128)}, f32[6,130,256]{2,1,0:T(8,128)}, u32[]{:S(2)}, u32[]{:S(2)}) collective-permute-start(f32[6,130,256]{2,1,0:T(8,128)} %get-tuple-element.807), channel_id=1, source_target_pairs={{0,8},{8,16},{16,24},{24,32},{32,40},{40,48},{48,56},{56,64},{64,7... | collective-permute-start | bytes 2396168 | tf_op jit(solution)/shard_map/while/body/eval_jaxpr/ppermute | solution.py:15
  482.5 42.1 %copy-start.5 = (f32[384]{0:T(512)S(1)}, f32[384]{0:T(512)}, u32[]{:S(2)}) copy-start(f32[384]{0:T(512)} %param.27) | copy-start | bytes 4612
Sparse Core Ops, SparseCore 0:
  10.4 146.6 all-gather.2
where the time goes:
time: 533 us; the launch traced here: 532 us
  waiting for transfers between devices  232 us (44%)
  blocking collectives  118 us (22%)
  starting transfers between devices  116 us (22%)
  matrix products  20.6 us (4%)
  local copies, waits for them, and re-layouts  17.7 us (3%)
  other arithmetic  13.7 us (3%)
  between operations  13.5 us (3%)
    ppermute x8, waiting for transfers between devices, passed_along(): return lax.ppermute(x, axis, pairs)  167 us
    ppermute x8, starting transfers between devices, passed_along(): return lax.ppermute(x, axis, pairs)  116 us
    all_gather x1, blocking collectives, local(): rate_piece = lax.all_gather(w_rate, 'ctx', axis=0, tiled=True)  79 us
    all_gather x1, waiting for transfers between devices, local(): weight_piece = lax.all_gather(w_qkv, 'ctx', axis=0, tiled=True)  64.7 us
    psum x1, blocking collectives, local(): feature_sum = lax.psum(jnp.sum(joined, -1), 'tp')  26.9 us
    psum x1, blocking collectives, local(): square_sum = lax.psum(jnp.sum(centre * centre, -1), 'tp')  12.4 us
  transfers between devices with their start and end apart: 9, of which 9 were waited for; matrix products, arithmetic and copies ran while one was open for 1% of the time, Pallas kernels for 0%

commit v1 on v0

v1 whole, which is shorter than its diff:
```python
import jax
import jax.numpy as jnp
from jax import lax
from jax.experimental import pallas as pl
from jax.experimental.pallas import tpu as pltpu
from jax.sharding import Mesh
from jax.sharding import PartitionSpec as P

D = 3072
HALF = 1536
HD = 64
HID = 256
TOK = 128
MB = 32
CLIP = 1024
STEPS = CLIP // MB
HEADS_DEV = 6
ROWS = 80
C1 = 0.7978845608028654
C2 = 0.044715 * C1
bf16 = jnp.bfloat16
f32 = jnp.float32
NN = (((1,), (0,)), ((), ()))
NT = (((1,), (1,)), ((), ()))
TN = (((0,), (0,)), ((), ()))


def mm(a, b, dims=NN):
    return lax.dot_general(a, b, dims, preferred_element_type=f32)


def gelu(h):
    hh = h * h
    return h * (0.5 + 0.5 * jnp.tanh(h * (C1 + C2 * hh)))


def gelu_and_slope(h):
    hh = h * h
    t = jnp.tanh(h * (C1 + C2 * hh))
    p = 0.5 + 0.5 * t
    return h * p, p + (0.5 * h) * (1.0 - t * t) * (C1 + (3 * C2) * hh)


def pack_kernel(w_ref, wr_ref, out_ref):
    for p in range(8):
        if p >= HEADS_DEV:
            out_ref[p % 4, p // 4] = jnp.zeros((ROWS, 128), bf16)
            continue
        cols = slice(p * HD, (p + 1) * HD)
        q = w_ref[0, :, cols].astype(f32)
        k = w_ref[1, :, cols].astype(f32)
        v = w_ref[2, :, cols].astype(f32)
        gate = wr_ref[p : p + 1, :].astype(f32)
        gate = jnp.concatenate([gate, jnp.zeros((1, 16), f32)], 1)
        gate = jnp.broadcast_to(gate, (16, HD))
        right = jnp.concatenate([q[32:48], gate], 0)
        block = jnp.concatenate(
            [jnp.concatenate([k, v], 1), jnp.concatenate([q[:32], right], 1)], 0
        )
        out_ref[p % 4, p // 4] = block.astype(bf16)


def pack(w, wr):
    return pl.pallas_call(
        pack_kernel,
        out_shape=jax.ShapeDtypeStruct((4, 2, ROWS, 128), bf16),
        name="pack_weights",
    )(w, wr)


def chain_kernel(
    idx,
    rate0,
    own,
    zm,
    zo,
    rm,
    ro,
    lm,
    lo,
    r2m,
    r2o,
    l2m,
    l2o,
    w_hbm,
    A0,
    B0,
    a0,
    b0,
    gain,
    bias,
    o_ref,
    T,
    W,
    WA,
    KV,
    Q,
    RT,
    A,
    B,
    Ab,
    Bb,
    a,
    b,
    hk,
    sem,
):
    head, zi, x, core = idx[0], idx[1], idx[2], idx[3]

    def place(src, z_of, x_of, half):
        row = pl.multiple_of((z_of * 4 + lax.rem(x_of + 8, 4)) * TOK, TOK)
        col = pl.multiple_of(half * HALF, HALF)
        return pltpu.make_async_copy(src, T.at[pl.ds(row, TOK), pl.ds(col, HALF)], sem.at[0])

    me, it = core, 1 - core
    row = pl.multiple_of((zi * 4 + x) * TOK, TOK)
    copies = [
        pltpu.make_async_copy(w_hbm, W, sem.at[1]),
        pltpu.make_async_copy(own, T.at[pl.ds(row, TOK), :], sem.at[0]),
    ]
    for half, z_, r_, l_, r2_, l2_ in ((me, zm, rm, lm, r2m, l2m), (it, zo, ro, lo, r2o, l2o)):
        copies += [
            place(z_, 1 - zi, x, half),
            place(r_.at[0:TOK], zi, x - 1, half),
            place(r_.at[TOK : 2 * TOK], 1 - zi, x - 1, half),
            place(l_.at[0:TOK], zi, x + 1, half),
            place(l_.at[TOK : 2 * TOK], 1 - zi, x + 1, half),
            place(r2_, zi, x + 2, half),
            place(l2_, 1 - zi, x + 2, half),
        ]
    for c in copies:
        c.start()

    gn = gain[pl.ds(head, 1), :]
    bs = bias[pl.ds(head, 1), :]
    A[...] = A0[head]
    Ab[...] = A0[head].astype(bf16)
    Bc = B0[head]
    Bc = Bc - jnp.mean(Bc, 0, keepdims=True)
    B[...] = Bc
    Bb[...] = Bc.astype(bf16)
    a[...] = a0[pl.ds(head, 1), :]
    bb = b0[pl.ds(head, 1), :]
    b[...] = bb - jnp.mean(bb, 1, keepdims=True)

    copies[0].wait()
    WA[:, 0:128] = W[:, 0:48, :].reshape(D, 128)
    X = W[:, 48:80, :]
    lane = lax.broadcasted_iota(jnp.int32, (1, 16, 128), 2)
    sub = lax.broadcasted_iota(jnp.int32, (1, 16, 128), 1)
    gate = X[:, 16:32, :].astype(f32)
    gates = jnp.concatenate(
        [jnp.where(lane == sub + (64 + 16 * j), gate, 0.0) for j in range(3)], 1
    )
    gates = mm(gates.astype(bf16).reshape(D, 128), jnp.ones((128, 128), bf16))
    qa = X[:, 0:16, :].astype(f32)
    qb = jnp.concatenate([qa[:, :, 64:], qa[:, :, :64]], 2)
    qs = jnp.concatenate([X.astype(f32), qb], 1).reshape(D, 128)
    wide = lax.broadcasted_iota(jnp.int32, (1, 128), 1)
    WA[:, 128:256] = jnp.where(wide < 64, qs, gates).astype(bf16)
    for c in copies[1:]:
        c.wait()

    base = rate0[head] * (1.0 / MB)

    def project(i, carry):
        rows = pl.ds(pl.multiple_of(i * 256, 256), 256)
        out = mm(T[rows, :], WA[...])
        KV[rows, :] = out[:, 0:128].astype(bf16)
        Q[rows, :] = out[:, 128:192].astype(bf16)
        RT[rows, :] = base * jax.nn.sigmoid(out[:, 192:256])
        return carry

    lax.fori_loop(0, CLIP // 256, project, 0)

    hk[...] = mm(KV[0:MB, 0:HD], Ab[...]) + a[...]
    g2 = gn * gn

    def answer(rows, q, act, Bv, bv):
        c = mm(act, Bv, NT) + bv
        scale = lax.rsqrt(jnp.mean(c * c, 1, keepdims=True) + 1e-6)
        o_ref[rows, :] = q.astype(f32) + (gn * c * scale + bs)

    def step(t, carry):
        now = pl.ds(pl.multiple_of(t * MB, MB), MB)
        nxt = pl.ds(pl.multiple_of(jnp.minimum(t + 1, STEPS - 1) * MB, MB), MB)
        old = pl.ds(pl.multiple_of(jnp.maximum(t - 1, 0) * MB, MB), MB)
        k = KV[now, 0:HD]
        v = KV[now, HD : 2 * HD]
        kn = KV[nxt, 0:HD]
        qp = Q[old, :]
        w = RT[now, :]
        Av, Bv, av, bv = Ab[...], Bb[...], a[...], b[...]
        act, slope = gelu_and_slope(hk[...])
        act = act.astype(bf16)
        c = mm(act, Bv, NT) + bv
        u = gn * (bs - (v.astype(f32) - k.astype(f32)))
        gc = g2 * c
        s1 = jnp.mean(c * c, 1, keepdims=True)
        s2 = jnp.mean(gc, 1, keepdims=True)
        s3 = jnp.mean(gc * c, 1, keepdims=True)
        s4 = jnp.mean(u * c, 1, keepdims=True)
        s5 = jnp.mean(u, 1, keepdims=True)
        rs = lax.rsqrt(s1 + 1e-6)
        dm = (w * rs) * (gc * rs + (u - (rs * s2 + s5)) - c * (rs * rs * (rs * s3 + s4)))
        dmb = dm.astype(bf16)
        dh = mm(dmb, Bv) * slope
        dhb = dh.astype(bf16)
        gram = (mm(kn, k, NT) + 1.0).astype(bf16)
        hk[...] = mm(kn, Av) + av - mm(gram, dhb)
        answer(old, qp, gelu(mm(qp, Av) + av).astype(bf16), Bv, bv)
        Bn = B[...] - mm(dmb, act, TN)
        B[...] = Bn
        Bb[...] = Bn.astype(bf16)
        b[...] = bv - jnp.sum(dm, 0, keepdims=True)
        An = A[...] - mm(k, dhb, TN)
        A[...] = An
        Ab[...] = An.astype(bf16)
        a[...] = av - jnp.sum(dh, 0, keepdims=True)
        return carry

    lax.fori_loop(0, STEPS, step, 0)
    last = pl.ds(CLIP - MB, MB)
    q = Q[last, :]
    answer(last, q, gelu(mm(q, Ab[...]) + a[...]).astype(bf16), Bb[...], b[...])


def chain(idx, rate0, pieces, w, params):
    hbm = pl.BlockSpec(memory_space=pl.ANY)
    smem = pl.BlockSpec(memory_space=pltpu.SMEM)
    vmem = pl.BlockSpec(memory_space=pltpu.VMEM)
    return pl.pallas_call(
        chain_kernel,
        out_shape=jax.ShapeDtypeStruct((CLIP, HD), f32),
        in_specs=[smem, smem] + [hbm] * (len(pieces) + 1) + [vmem] * len(params),
        out_specs=vmem,
        scratch_shapes=[
            pltpu.VMEM((CLIP, D), bf16),
            pltpu.VMEM((64, ROWS, 128), bf16),
            pltpu.VMEM((D, 256), bf16),
            pltpu.VMEM((CLIP, 2 * HD), bf16),
            pltpu.VMEM((CLIP, HD), bf16),
            pltpu.VMEM((CLIP, HD), f32),
            pltpu.VMEM((HD, HID), f32),
            pltpu.VMEM((HD, HID), f32),
            pltpu.VMEM((HD, HID), bf16),
            pltpu.VMEM((HD, HID), bf16),
            pltpu.VMEM((1, HID), f32),
            pltpu.VMEM((1, HD), f32),
            pltpu.VMEM((MB, HID), f32),
            pltpu.SemaphoreType.DMA((2,)),
        ],
        compiler_params=pltpu.CompilerParams(vmem_limit_bytes=40 * 1024 * 1024),
        name="clip_head",
    )(idx, rate0, *pieces, w, *params)


def ring(x, axis, by):
    size = lax.axis_size(axis)
    return lax.ppermute(x, axis, [(i, (i + by) % size) for i in range(size)])


def local(
    tokens,
    w_qkv,
    w_rate,
    layer_one,
    layer_two,
    bias_one,
    bias_two,
    inner_gain,
    inner_bias,
    inner_rate,
    out_gain,
):
    zi, x, core = (lax.axis_index(n).astype(jnp.int32) for n in ("zi", "x", "core"))
    blocks = pack(jnp.transpose(w_qkv, (1, 0, 2)), jnp.transpose(w_rate))
    blocks = lax.all_to_all(blocks, "x", 0, 0, tiled=True)
    blocks = jnp.transpose(blocks, (1, 0, 2, 3))[None]
    blocks = jnp.broadcast_to(blocks, (8, 2, 4, ROWS, 128)).reshape(16, 4, ROWS, 128)
    weights = lax.all_to_all(blocks, ("zc", "zi"), 0, 0, tiled=True)
    weights = weights.reshape(64, ROWS, 128)

    mine = lax.dynamic_slice(tokens, (0, core * HALF), (TOK, HALF))
    across = ring(mine, "zi", 1)
    pair = jnp.concatenate([mine, across], 0)
    right, left = ring(pair, "x", 1), ring(pair, "x", -1)
    far_own, far_across = ring(right[:TOK], "x", 1), ring(left[TOK:], "x", -1)
    pieces = [tokens]
    for piece in (across, right, left, far_own, far_across):
        pieces += [piece, ring(piece, "core", 1)]

    position = zi * 4 + x
    idx = jnp.stack([jnp.minimum(position, HEADS_DEV - 1), zi, x, core])
    params = (layer_one, layer_two, bias_one, bias_two, inner_gain, inner_bias)
    outs = chain(idx, inner_rate, pieces, weights, params)

    got = lax.all_to_all(outs.reshape(8, TOK, HD), ("zi", "x"), 0, 0, tiled=True)[:HEADS_DEV]
    total = jnp.sum(got, (0, 2))
    offset = got - (total / (HEADS_DEV * HD))[None, :, None]
    squares = jnp.sum(offset * offset, (0, 2))
    stats = jnp.broadcast_to(jnp.stack([total, squares])[None], (8, 2, TOK))
    stats = lax.all_to_all(stats, ("y", "core"), 0, 0, tiled=True)
    mean = jnp.sum(stats[:, 0], 0) / D
    shift = stats[:, 0] / (HEADS_DEV * HD) - mean
    variance = jnp.sum(stats[:, 1] + (HEADS_DEV * HD) * shift * shift, 0) / D
    normed = (got - mean[None, :, None]) * lax.rsqrt(variance + 1e-05)[None, :, None]
    joined = jnp.transpose(normed, (1, 0, 2)).reshape(TOK, HEADS_DEV * HD)
    return (joined * out_gain).astype(bf16)


def solution(mesh):
    fine = Mesh(mesh.devices.reshape(8, 2, 4, 4, 2), ("zc", "zi", "x", "y", "core"))
    ctx, tp = ("zc", "zi", "x"), ("y", "core")
    placed = (
        P(ctx, None),
        P(ctx, None, tp),
        P(ctx, tp),
        P(tp, None, None),
        P(tp, None, None),
        P(tp, None),
        P(tp, None),
        P(tp, None),
        P(tp, None),
        P(tp),
        P(tp),
    )
    return jax.shard_map(local, mesh=fine, in_specs=placed, out_specs=P(ctx, tp), check_vma=False)
```

time: 533 us -> 191 us (0.36)
  the two profiles are of different devices: /device:TPU:103 before, /device:TPU:1 now
where the time goes in v1:
time: 191 us; the launch traced here: 190 us
  waiting for transfers between devices  78.8 us (41%)
  starting transfers between devices  44.3 us (23%)
  Pallas kernels  30 us (16%)
  blocking collectives  29.5 us (15%)
  local copies, waits for them, and re-layouts  6.54 us (3%)
    ppermute x10, waiting for transfers between devices, ring(): return lax.ppermute(x, axis, [(i, (i + by) % size) for i in range(size)])  78.7 us
    ppermute x10, starting transfers between devices, ring(): return lax.ppermute(x, axis, [(i, (i + by) % size) for i in range(size)])  29.3 us
    pallas_call x1, Pallas kernels, chain(): pl.pallas_call(chain_kernel, out_shape=jax.ShapeDtypeStruct((CLIP, HD), f...  28.4 us
    all_to_all x1, starting transfers between devices, local(): weights = lax.all_to_all(blocks, ('zc', 'zi'), 0, 0, tiled=True)  15 us
    all_to_all x1, blocking collectives, local(): stats = lax.all_to_all(stats, ('y', 'core'), 0, 0, tiled=True)  10.8 us
    all_to_all x1, blocking collectives, local(): blocks = lax.all_to_all(blocks, 'x', 0, 0, tiled=True)  9.84 us
    all_to_all x1, blocking collectives, local(): lax.all_to_all(outs.reshape(8, TOK, HD), ('zi', 'x'), 0, 0, tiled=True)  8.8 us
    unnamed x24, local copies, waits for them, and re-layouts  4.16 us
  transfers between devices with their start and end apart: 11, of which 3 were waited for; matrix products, arithmetic and copies ran while one was open for 0% of the time, Pallas kernels for 0%

profile of v1, /device:TPU:1, one launch (start us, length us, event | category | flops | bytes accessed | tf_op | source)
XLA Modules:
  0.0 189.9 jit_solution(17204169172008508085)
XLA Ops:
  0.0 1.7 pack_weights.1
  1.7 9.8 %all_to_all.20 = bf16[4,2,80,128]{3,2,1,0:T(8,128)(2,1)S(1)} all-to-all(bf16[4,2,80,128]{3,2,1,0:T(8,128)(2,1)} %pack_weights.1), channel_id=1, replica_groups=mesh['zc'=8,'zi'=2,'x'=4,'y'=4,'core'=2] {'x'}, dimensions={0} | all-to-all | bytes 327680 | tf_op jit(solution)/shard_map/all_to_all | solution.py:278
  11.5 1.3 broadcast_in_dim.4
  12.9 15.0 %all-to-all-start.1 = ((bf16[16,4,80,128]{3,2,1,0:T(8,128)(2,1)}), bf16[16,4,80,128]{3,2,1,0:T(8,128)(2,1)S(1)}, u32[]{:S(2)}, u32[]{:S(2)}) async-start(bf16[16,4,80,128]{3,2,1,0:T(8,128)(2,1)} %bitcast.7), calls=%async_computation.1 | async-start | bytes 2621440 | tf_op jit(solution)/shard_map/all_to_all | solution.py:281
  27.9 0.0 copy-done
  28.0 0.0 copy-start.6
  28.0 0.0 copy-start.7
  28.0 0.0 copy-start.8
  28.0 0.0 copy-start.9
  28.0 0.0 copy-start.10
  28.0 3.4 %collective-permute-start = (bf16[128,1536]{1,0:T(8,128)(2,1)S(1)}, bf16[128,1536]{1,0:T(8,128)(2,1)S(1)}, u32[]{:S(2)}, u32[]{:S(2)}) collective-permute-start(bf16[128,1536]{1,0:T(8,128)(2,1)S(1)} %constant_dynamic-slice_fusion), channel_id=1, source_target_pairs={{0,32},{32,0},{1,33},{33,1},{2,34},{34,2},{3,35},{35,3},{4,36},{36... | collective-permute-start | bytes 1179656 | tf_op jit(solution)/shard_map/ppermute | solution.py:260
  31.4 63.0 %collective-permute-done.zm = bf16[128,1536]{1,0:T(8,128)(2,1)S(1)} collective-permute-done((bf16[128,1536]{1,0:T(8,128)(2,1)S(1)}, bf16[128,1536]{1,0:T(8,128)(2,1)S(1)}, u32[]{:S(2)}, u32[]{:S(2)}) %collective-permute-start) | collective-permute-done | bytes 393248 | tf_op jit(solution)/shard_map/ppermute | solution.py:260
  94.4 0.1 pad_maximum_fusion
  94.5 2.8 %collective-permute-start.4 = (bf16[256,1536]{1,0:T(8,128)(2,1)S(1)}, bf16[256,1536]{1,0:T(8,128)(2,1)S(1)}, u32[]{:S(2)}, u32[]{:S(2)}) collective-permute-start(bf16[256,1536]{1,0:T(8,128)(2,1)S(1)} %pad_maximum_fusion), channel_id=1, source_target_pairs={{0,24},{8,0},{16,8},{24,16},{1,25},{9,1},{17,9},{25,17},{2,26},{10... | collective-permute-start | bytes 2359304 | tf_op jit(solution)/shard_map/ppermute | solution.py:260
  97.3 2.5 %collective-permute-start.2 = (bf16[256,1536]{1,0:T(8,128)(2,1)S(1)}, bf16[256,1536]{1,0:T(8,128)(2,1)S(1)}, u32[]{:S(2)}, u32[]{:S(2)}) collective-permute-start(bf16[256,1536]{1,0:T(8,128)(2,1)S(1)} %pad_maximum_fusion), channel_id=1, source_target_pairs={{0,8},{8,16},{16,24},{24,0},{1,9},{9,17},{17,25},{25,1},{2,10},{10... | collective-permute-start | bytes 2359304 | tf_op jit(solution)/shard_map/ppermute | solution.py:260
  99.8 14.2 %collective-permute-done.4.lm = bf16[256,1536]{1,0:T(8,128)(2,1)S(1)} collective-permute-done((bf16[256,1536]{1,0:T(8,128)(2,1)S(1)}, bf16[256,1536]{1,0:T(8,128)(2,1)S(1)}, u32[]{:S(2)}, u32[]{:S(2)}) %collective-permute-start.4) | collective-permute-done | bytes 786464 | tf_op jit(solution)/shard_map/ppermute | solution.py:260
  114.0 4.0 %collective-permute-start.8 = (bf16[128,1536]{1,0:T(8,128)(2,1)S(1)}, bf16[128,1536]{1,0:T(8,128)(2,1)}, u32[]{:S(2)}, u32[]{:S(2)}) collective-permute-start(bf16[128,1536]{1,0:T(8,128)(2,1)S(1)} %slice.22), channel_id=1, source_target_pairs={{0,24},{8,0},{16,8},{24,16},{1,25},{9,1},{17,9},{25,17},{2,26},{10... | collective-permute-start | bytes 1179656 | tf_op jit(solution)/shard_map/ppermute | solution.py:260
  118.0 0.0 collective-permute-done.2.rm
  118.1 1.9 %collective-permute-start.6 = (bf16[128,1536]{1,0:T(8,128)(2,1)S(1)}, bf16[128,1536]{1,0:T(8,128)(2,1)}, u32[]{:S(2)}, u32[]{:S(2)}) collective-permute-start(bf16[128,1536]{1,0:T(8,128)(2,1)S(1)} %slice.21), channel_id=1, source_target_pairs={{0,8},{8,16},{16,24},{24,0},{1,9},{9,17},{17,25},{25,1},{2,10},{10... | collective-permute-start | bytes 1179656 | tf_op jit(solution)/shard_map/ppermute | solution.py:260
  120.0 4.6 %collective-permute-start.5 = (bf16[256,1536]{1,0:T(8,128)(2,1)S(1)}, bf16[256,1536]{1,0:T(8,128)(2,1)}, u32[]{:S(2)}, u32[]{:S(2)}) collective-permute-start(bf16[256,1536]{1,0:T(8,128)(2,1)S(1)} %collective-permute-done.4.lm), channel_id=1, source_target_pairs={{0,1},{1,0},{2,3},{3,2},{4,5},{5,4},{6,7},{7,6},{8,9},{9,8},{10,11... | collective-permute-start | bytes 2359304 | tf_op jit(solution)/shard_map/ppermute | solution.py:260
  124.6 1.9 %collective-permute-start.3 = (bf16[256,1536]{1,0:T(8,128)(2,1)S(1)}, bf16[256,1536]{1,0:T(8,128)(2,1)}, u32[]{:S(2)}, u32[]{:S(2)}) collective-permute-start(bf16[256,1536]{1,0:T(8,128)(2,1)S(1)} %collective-permute-done.2.rm), channel_id=1, source_target_pairs={{0,1},{1,0},{2,3},{3,2},{4,5},{5,4},{6,7},{7,6},{8,9},{9,8},{10,11... | collective-permute-start | bytes 2359304 | tf_op jit(solution)/shard_map/ppermute | solution.py:260
  126.5 0.0 copy-done.2
  126.5 2.4 %collective-permute-start.1 = (bf16[128,1536]{1,0:T(8,128)(2,1)S(1)}, bf16[128,1536]{1,0:T(8,128)(2,1)}, u32[]{:S(2)}, u32[]{:S(2)}) collective-permute-start(bf16[128,1536]{1,0:T(8,128)(2,1)S(1)} %collective-permute-done.zm), channel_id=1, source_target_pairs={{0,1},{1,0},{2,3},{3,2},{4,5},{5,4},{6,7},{7,6},{8,9},{9,8},{10,11... | collective-permute-start | bytes 1179656 | tf_op jit(solution)/shard_map/ppermute | solution.py:260
  128.9 0.0 collective-permute-done.8.l2m
  128.9 1.9 %collective-permute-start.9 = (bf16[128,1536]{1,0:T(8,128)(2,1)}, bf16[128,1536]{1,0:T(8,128)(2,1)}, u32[]{:S(2)}, u32[]{:S(2)}) collective-permute-start(bf16[128,1536]{1,0:T(8,128)(2,1)} %collective-permute-done.8.l2m), channel_id=1, source_target_pairs={{0,1},{1,0},{2,3},{3,2},{4,5},{5,4},{6,7},{7,6},{8,9},{9,8},{10,11... | collective-permute-start | bytes 1179656 | tf_op jit(solution)/shard_map/ppermute | solution.py:260
  130.9 0.0 collective-permute-done.6.r2m
  130.9 3.8 %collective-permute-start.7 = (bf16[128,1536]{1,0:T(8,128)(2,1)}, bf16[128,1536]{1,0:T(8,128)(2,1)}, u32[]{:S(2)}, u32[]{:S(2)}) collective-permute-start(bf16[128,1536]{1,0:T(8,128)(2,1)} %collective-permute-done.6.r2m), channel_id=1, source_target_pairs={{0,1},{1,0},{2,3},{3,2},{4,5},{5,4},{6,7},{7,6},{8,9},{9,8},{10,11... | collective-permute-start | bytes 1179656 | tf_op jit(solution)/shard_map/ppermute | solution.py:260
  134.7 0.1 pad_add_fusion.idx
  134.8 0.0 collective-permute-done.1.zo
  134.8 0.0 collective-permute-done.9.l2o
  134.8 0.0 collective-permute-done.5.lo
  134.8 1.6 collective-permute-done.7.r2o
  136.4 0.0 collective-permute-done.3.ro
  136.4 0.0 all-to-all-done.1
  136.4 0.0 copy-start.1
  136.4 1.1 copy-done.1
  137.6 1.0 copy-done.3
  138.6 1.0 copy-done.4
  139.6 1.0 copy-done.5
  140.5 28.4 %clip_head.1 = f32[1024,64]{1,0:T(8,128)S(1)} custom-call(s32[4]{0:T(128)S(1)} %pad_add_fusion.idx, f32[6]{0:T(128)S(1)} %copy-done.10, bf16[128,3072]{1,0:T(8,128)(2,1)S(1)} %copy-done.1, bf16[128,1536]{1,0:T(8,128)(2,1)S(1)} %copy-done.3, bf16[128,1536]{1,0:T(8,128)(2,1)} %collective-permute-done.1.zo, bf16[256,1536]{1,0:T(8,128)(2,1)S(1)} %collective-permute-done.2.rm, ...), custom_call_target="tpu_custom_call" | custom-call | tf_op jit(solution)/shard_map/clip_head/pallas_call | solution.py:232
  168.9 0.0 copy-start.11
  168.9 0.2 copy.23
  169.1 8.8 %all_to_all.21 = f32[8,128,64]{1,2,0:T(8,128)S(1)} all-to-all(f32[8,128,64]{1,2,0:T(8,128)S(1)} %copy.23), channel_id=1, replica_groups=mesh['zc'=8,'zi'=2,'x'=4,'y'=4,'core'=2] {'zi','x'}, dimensions={0} | all-to-all | bytes 524288 | tf_op jit(solution)/shard_map/all_to_all | solution.py:298
  177.9 0.1 slice_reduce_fusion
  178.0 0.1 multiply_reduce_fusion
  178.1 10.8 %all_to_all.22 = f32[8,2,128]{2,1,0:T(2,128)S(1)} all-to-all(f32[8,2,128]{2,1,0:T(2,128)S(1)} %broadcast_in_dim.5), channel_id=1, replica_groups=mesh['zc'=8,'zi'=2,'x'=4,'y'=4,'core'=2] {'y','core'}, dimensions={0} | all-to-all | bytes 16384 | tf_op jit(solution)/shard_map/all_to_all | solution.py:303
  189.1 0.1 fusion
  189.2 0.8 copy.25
  (24 shorter events, 0.2 us)
Async XLA Ops:
  12.9 15.1 %copy-start = (bf16[128,3072]{1,0:T(8,128)(2,1)S(1)}, bf16[128,3072]{1,0:T(8,128)(2,1)}, u32[]{:S(2)}) copy-start(bf16[128,3072]{1,0:T(8,128)(2,1)} %own.1) | copy-start | bytes 2359300
  12.9 123.5 %all-to-all-start.1 = ((bf16[16,4,80,128]{3,2,1,0:T(8,128)(2,1)}), bf16[16,4,80,128]{3,2,1,0:T(8,128)(2,1)S(1)}, u32[]{:S(2)}, u32[]{:S(2)}) async-start(bf16[16,4,80,128]{3,2,1,0:T(8,128)(2,1)} %bitcast.7), calls=%async_computation.1 | async-start | bytes 2621440 | tf_op jit(solution)/shard_map/all_to_all | solution.py:281
  28.0 108.4 %copy-start.6 = (f32[6,256]{1,0:T(8,128)S(1)}, f32[6,256]{1,0:T(8,128)}, u32[]{:S(2)}) copy-start(f32[6,256]{1,0:T(8,128)} %a0.1) | copy-start | bytes 18436
  28.0 108.4 %copy-start.7 = (f32[6,64]{1,0:T(8,128)S(1)}, f32[6,64]{1,0:T(8,128)}, u32[]{:S(2)}) copy-start(f32[6,64]{1,0:T(8,128)} %b0.1) | copy-start | bytes 4612
  28.0 108.4 %copy-start.8 = (f32[6,64]{1,0:T(8,128)S(1)}, f32[6,64]{1,0:T(8,128)}, u32[]{:S(2)}) copy-start(f32[6,64]{1,0:T(8,128)} %gain.1) | copy-start | bytes 4612
  28.0 108.4 %copy-start.9 = (f32[6,64]{1,0:T(8,128)S(1)}, f32[6,64]{1,0:T(8,128)}, u32[]{:S(2)}) copy-start(f32[6,64]{1,0:T(8,128)} %bias.1) | copy-start | bytes 4612
  28.0 108.4 %copy-start.10 = (f32[6]{0:T(128)S(1)}, f32[6]{0:T(128)}, u32[]{:S(2)}) copy-start(f32[6]{0:T(128)} %rate0.1) | copy-start | bytes 76
  28.0 66.4 %collective-permute-start = (bf16[128,1536]{1,0:T(8,128)(2,1)S(1)}, bf16[128,1536]{1,0:T(8,128)(2,1)S(1)}, u32[]{:S(2)}, u32[]{:S(2)}) collective-permute-start(bf16[128,1536]{1,0:T(8,128)(2,1)S(1)} %constant_dynamic-slice_fusion), channel_id=1, source_target_pairs={{0,32},{32,0},{1,33},{33,1},{2,34},{34,2},{3,35},{35,3},{4,36},{36... | collective-permute-start | bytes 1179656 | tf_op jit(solution)/shard_map/ppermute | solution.py:260
  94.4 32.1 %copy-start.2 = (bf16[128,1536]{1,0:T(8,128)(2,1)}, bf16[128,1536]{1,0:T(8,128)(2,1)S(1)}, u32[]{:S(2)}) copy-start(bf16[128,1536]{1,0:T(8,128)(2,1)S(1)} %collective-permute-done.zm) | copy-start | bytes 1179652
  94.5 19.5 %collective-permute-start.4 = (bf16[256,1536]{1,0:T(8,128)(2,1)S(1)}, bf16[256,1536]{1,0:T(8,128)(2,1)S(1)}, u32[]{:S(2)}, u32[]{:S(2)}) collective-permute-start(bf16[256,1536]{1,0:T(8,128)(2,1)S(1)} %pad_maximum_fusion), channel_id=1, source_target_pairs={{0,24},{8,0},{16,8},{24,16},{1,25},{9,1},{17,9},{25,17},{2,26},{10... | collective-permute-start | bytes 2359304 | tf_op jit(solution)/shard_map/ppermute | solution.py:260
  97.3 20.7 %collective-permute-start.2 = (bf16[256,1536]{1,0:T(8,128)(2,1)S(1)}, bf16[256,1536]{1,0:T(8,128)(2,1)S(1)}, u32[]{:S(2)}, u32[]{:S(2)}) collective-permute-start(bf16[256,1536]{1,0:T(8,128)(2,1)S(1)} %pad_maximum_fusion), channel_id=1, source_target_pairs={{0,8},{8,16},{16,24},{24,0},{1,9},{9,17},{17,25},{25,1},{2,10},{10... | collective-permute-start | bytes 2359304 | tf_op jit(solution)/shard_map/ppermute | solution.py:260
  114.0 14.9 %collective-permute-start.8 = (bf16[128,1536]{1,0:T(8,128)(2,1)S(1)}, bf16[128,1536]{1,0:T(8,128)(2,1)}, u32[]{:S(2)}, u32[]{:S(2)}) collective-permute-start(bf16[128,1536]{1,0:T(8,128)(2,1)S(1)} %slice.22), channel_id=1, source_target_pairs={{0,24},{8,0},{16,8},{24,16},{1,25},{9,1},{17,9},{25,17},{2,26},{10... | collective-permute-start | bytes 1179656 | tf_op jit(solution)/shard_map/ppermute | solution.py:260
  118.1 12.8 %collective-permute-start.6 = (bf16[128,1536]{1,0:T(8,128)(2,1)S(1)}, bf16[128,1536]{1,0:T(8,128)(2,1)}, u32[]{:S(2)}, u32[]{:S(2)}) collective-permute-start(bf16[128,1536]{1,0:T(8,128)(2,1)S(1)} %slice.21), channel_id=1, source_target_pairs={{0,8},{8,16},{16,24},{24,0},{1,9},{9,17},{17,25},{25,1},{2,10},{10... | collective-permute-start | bytes 1179656 | tf_op jit(solution)/shard_map/ppermute | solution.py:260
  120.0 14.8 %collective-permute-start.5 = (bf16[256,1536]{1,0:T(8,128)(2,1)S(1)}, bf16[256,1536]{1,0:T(8,128)(2,1)}, u32[]{:S(2)}, u32[]{:S(2)}) collective-permute-start(bf16[256,1536]{1,0:T(8,128)(2,1)S(1)} %collective-permute-done.4.lm), channel_id=1, source_target_pairs={{0,1},{1,0},{2,3},{3,2},{4,5},{5,4},{6,7},{7,6},{8,9},{9,8},{10,11... | collective-permute-start | bytes 2359304 | tf_op jit(solution)/shard_map/ppermute | solution.py:260
  124.6 11.8 %collective-permute-start.3 = (bf16[256,1536]{1,0:T(8,128)(2,1)S(1)}, bf16[256,1536]{1,0:T(8,128)(2,1)}, u32[]{:S(2)}, u32[]{:S(2)}) collective-permute-start(bf16[256,1536]{1,0:T(8,128)(2,1)S(1)} %collective-permute-done.2.rm), channel_id=1, source_target_pairs={{0,1},{1,0},{2,3},{3,2},{4,5},{5,4},{6,7},{7,6},{8,9},{9,8},{10,11... | collective-permute-start | bytes 2359304 | tf_op jit(solution)/shard_map/ppermute | solution.py:260
  126.5 8.3 %collective-permute-start.1 = (bf16[128,1536]{1,0:T(8,128)(2,1)S(1)}, bf16[128,1536]{1,0:T(8,128)(2,1)}, u32[]{:S(2)}, u32[]{:S(2)}) collective-permute-start(bf16[128,1536]{1,0:T(8,128)(2,1)S(1)} %collective-permute-done.zm), channel_id=1, source_target_pairs={{0,1},{1,0},{2,3},{3,2},{4,5},{5,4},{6,7},{7,6},{8,9},{9,8},{10,11... | collective-permute-start | bytes 1179656 | tf_op jit(solution)/shard_map/ppermute | solution.py:260
  128.9 5.9 %collective-permute-start.9 = (bf16[128,1536]{1,0:T(8,128)(2,1)}, bf16[128,1536]{1,0:T(8,128)(2,1)}, u32[]{:S(2)}, u32[]{:S(2)}) collective-permute-start(bf16[128,1536]{1,0:T(8,128)(2,1)} %collective-permute-done.8.l2m), channel_id=1, source_target_pairs={{0,1},{1,0},{2,3},{3,2},{4,5},{5,4},{6,7},{7,6},{8,9},{9,8},{10,11... | collective-permute-start | bytes 1179656 | tf_op jit(solution)/shard_map/ppermute | solution.py:260
  130.9 5.5 %collective-permute-start.7 = (bf16[128,1536]{1,0:T(8,128)(2,1)}, bf16[128,1536]{1,0:T(8,128)(2,1)}, u32[]{:S(2)}, u32[]{:S(2)}) collective-permute-start(bf16[128,1536]{1,0:T(8,128)(2,1)} %collective-permute-done.6.r2m), channel_id=1, source_target_pairs={{0,1},{1,0},{2,3},{3,2},{4,5},{5,4},{6,7},{7,6},{8,9},{9,8},{10,11... | collective-permute-start | bytes 1179656 | tf_op jit(solution)/shard_map/ppermute | solution.py:260
  136.4 1.1 copy-start.1
  137.6 1.0 copy-start.3
  138.6 1.0 copy-start.4
  139.5 1.0 copy-start.5
  168.9 20.1 %copy-start.11 = (f32[384]{0:T(512)S(1)}, f32[384]{0:T(512)}, u32[]{:S(2)}) copy-start(f32[384]{0:T(512)} %param.21) | copy-start | bytes 4612

commit v2 on v1

--- a/solution.py
+++ b/solution.py
@@ -15,6 +15,7 @@
 CLIP = 1024
 STEPS = CLIP // MB
 HEADS_DEV = 6
+SHIFTS = (1, -1, 2)
 ROWS = 80
 C1 = 0.7978845608028654
 C2 = 0.044715 * C1
@@ -43,14 +44,15 @@
 
 def pack_kernel(w_ref, wr_ref, out_ref):
     for p in range(8):
-        if p >= HEADS_DEV:
+        head = 2 * (p % 4) + p // 4
+        if head >= HEADS_DEV:
             out_ref[p % 4, p // 4] = jnp.zeros((ROWS, 128), bf16)
             continue
-        cols = slice(p * HD, (p + 1) * HD)
+        cols = slice(head * HD, (head + 1) * HD)
         q = w_ref[0, :, cols].astype(f32)
         k = w_ref[1, :, cols].astype(f32)
         v = w_ref[2, :, cols].astype(f32)
-        gate = wr_ref[p : p + 1, :].astype(f32)
+        gate = wr_ref[head : head + 1, :].astype(f32)
         gate = jnp.concatenate([gate, jnp.zeros((1, 16), f32)], 1)
         gate = jnp.broadcast_to(gate, (16, HD))
         right = jnp.concatenate([q[32:48], gate], 0)
@@ -72,26 +74,32 @@
     idx,
     rate0,
     own,
-    zm,
-    zo,
-    rm,
-    ro,
-    lm,
-    lo,
-    r2m,
-    r2o,
-    l2m,
-    l2o,
-    w_hbm,
+    z_half,
+    r_half,
+    l_half,
+    f_half,
+    z_sibling,
+    r_sibling,
+    l_sibling,
+    f_sibling,
+    near,
+    other,
+    A0_hbm,
+    B0_hbm,
+    a0_hbm,
+    b0_hbm,
+    gain_hbm,
+    bias_hbm,
+    o_ref,
     A0,
     B0,
     a0,
     b0,
     gain,
     bias,
-    o_ref,
     T,
     W,
+    O,
     WA,
     KV,
     Q,
@@ -107,35 +115,42 @@
 ):
     head, zi, x, core = idx[0], idx[1], idx[2], idx[3]
 
-    def place(src, z_of, x_of, half):
+    def place(src, z_of, x_of, part):
         row = pl.multiple_of((z_of * 4 + lax.rem(x_of + 8, 4)) * TOK, TOK)
-        col = pl.multiple_of(half * HALF, HALF)
+        col = pl.multiple_of(part * HALF, HALF)
         return pltpu.make_async_copy(src, T.at[pl.ds(row, TOK), pl.ds(col, HALF)], sem.at[0])
 
-    me, it = core, 1 - core
     row = pl.multiple_of((zi * 4 + x) * TOK, TOK)
     copies = [
-        pltpu.make_async_copy(w_hbm, W, sem.at[1]),
+        pltpu.make_async_copy(near, W.at[:, zi], sem.at[1]),
+        pltpu.make_async_copy(other, W.at[:, 1 - zi], sem.at[1]),
         pltpu.make_async_copy(own, T.at[pl.ds(row, TOK), :], sem.at[0]),
     ]
-    for half, z_, r_, l_, r2_, l2_ in ((me, zm, rm, lm, r2m, l2m), (it, zo, ro, lo, r2o, l2o)):
-        copies += [
-            place(z_, 1 - zi, x, half),
-            place(r_.at[0:TOK], zi, x - 1, half),
-            place(r_.at[TOK : 2 * TOK], 1 - zi, x - 1, half),
-            place(l_.at[0:TOK], zi, x + 1, half),
-            place(l_.at[TOK : 2 * TOK], 1 - zi, x + 1, half),
-            place(r2_, zi, x + 2, half),
-            place(l2_, 1 - zi, x + 2, half),
-        ]
-    for c in copies:
+    halves = (z_half, r_half, l_half, f_half)
+    siblings = (z_sibling, r_sibling, l_sibling, f_sibling)
+    for (across, *pairs), part in ((halves, core), (siblings, 1 - core)):
+        copies.append(place(across, 1 - zi, x, part))
+        for by, pair in zip(SHIFTS, pairs):
+            copies.append(place(pair.at[0:TOK], zi, x - by, part))
+            copies.append(place(pair.at[TOK : 2 * TOK], 1 - zi, x - by, part))
+    small = [
+        pltpu.make_async_copy(A0_hbm.at[head], A0, sem.at[2]),
+        pltpu.make_async_copy(B0_hbm.at[head], B0, sem.at[2]),
+        pltpu.make_async_copy(a0_hbm, a0, sem.at[2]),
+        pltpu.make_async_copy(b0_hbm, b0, sem.at[2]),
+        pltpu.make_async_copy(gain_hbm, gain, sem.at[2]),
+        pltpu.make_async_copy(bias_hbm, bias, sem.at[2]),
+    ]
+    for c in small + copies:
         c.start()
+    for c in small:
+        c.wait()
 
     gn = gain[pl.ds(head, 1), :]
     bs = bias[pl.ds(head, 1), :]
-    A[...] = A0[head]
-    Ab[...] = A0[head].astype(bf16)
-    Bc = B0[head]
+    A[...] = A0[...]
+    Ab[...] = A0[...].astype(bf16)
+    Bc = B0[...]
     Bc = Bc - jnp.mean(Bc, 0, keepdims=True)
     B[...] = Bc
     Bb[...] = Bc.astype(bf16)
@@ -144,8 +159,9 @@
     b[...] = bb - jnp.mean(bb, 1, keepdims=True)
 
     copies[0].wait()
-    WA[:, 0:128] = W[:, 0:48, :].reshape(D, 128)
-    X = W[:, 48:80, :]
+    copies[1].wait()
+    WA[:, 0:128] = W[:, :, :, 0:48, :].reshape(D, 128)
+    X = W[:, :, :, 48:80, :].reshape(64, 32, 128)
     lane = lax.broadcasted_iota(jnp.int32, (1, 16, 128), 2)
     sub = lax.broadcasted_iota(jnp.int32, (1, 16, 128), 1)
     gate = X[:, 16:32, :].astype(f32)
@@ -158,7 +174,7 @@
     qs = jnp.concatenate([X.astype(f32), qb], 1).reshape(D, 128)
     wide = lax.broadcasted_iota(jnp.int32, (1, 128), 1)
     WA[:, 128:256] = jnp.where(wide < 64, qs, gates).astype(bf16)
-    for c in copies[1:]:
+    for c in copies[2:]:
         c.wait()
 
     base = rate0[head] * (1.0 / MB)
@@ -179,7 +195,7 @@
     def answer(rows, q, act, Bv, bv):
         c = mm(act, Bv, NT) + bv
         scale = lax.rsqrt(jnp.mean(c * c, 1, keepdims=True) + 1e-6)
-        o_ref[rows, :] = q.astype(f32) + (gn * c * scale + bs)
+        O[rows, :] = q.astype(f32) + (gn * c * scale + bs)
 
     def step(t, carry):
         now = pl.ds(pl.multiple_of(t * MB, MB), MB)
@@ -219,24 +235,33 @@
         a[...] = av - jnp.sum(dh, 0, keepdims=True)
         return carry
 
-    lax.fori_loop(0, STEPS, step, 0)
+    lax.fori_loop(0, STEPS, step, 0, unroll=4)
     last = pl.ds(CLIP - MB, MB)
     q = Q[last, :]
     answer(last, q, gelu(mm(q, Ab[...]) + a[...]).astype(bf16), Bb[...], b[...])
-
-
-def chain(idx, rate0, pieces, w, params):
+    for i in range(8):
+        o_ref[i] = jnp.transpose(O[i * TOK : (i + 1) * TOK, :])
+
+
+def chain(idx, rate0, pieces, weights, params):
     hbm = pl.BlockSpec(memory_space=pl.ANY)
     smem = pl.BlockSpec(memory_space=pltpu.SMEM)
     vmem = pl.BlockSpec(memory_space=pltpu.VMEM)
     return pl.pallas_call(
         chain_kernel,
-        out_shape=jax.ShapeDtypeStruct((CLIP, HD), f32),
-        in_specs=[smem, smem] + [hbm] * (len(pieces) + 1) + [vmem] * len(params),
+        out_shape=jax.ShapeDtypeStruct((8, HD, TOK), f32),
+        in_specs=[smem, smem] + [hbm] * (len(pieces) + len(weights) + len(params)),
         out_specs=vmem,
         scratch_shapes=[
+            pltpu.VMEM((HD, HID), f32),
+            pltpu.VMEM((HD, HID), f32),
+            pltpu.VMEM((HEADS_DEV, HID), f32),
+            pltpu.VMEM((HEADS_DEV, HD), f32),
+            pltpu.VMEM((HEADS_DEV, HD), f32),
+            pltpu.VMEM((HEADS_DEV, HD), f32),
             pltpu.VMEM((CLIP, D), bf16),
-            pltpu.VMEM((64, ROWS, 128), bf16),
+            pltpu.VMEM((8, 2, 4, ROWS, 128), bf16),
+            pltpu.VMEM((CLIP, HD), f32),
             pltpu.VMEM((D, 256), bf16),
             pltpu.VMEM((CLIP, 2 * HD), bf16),
             pltpu.VMEM((CLIP, HD), bf16),
@@ -248,16 +273,20 @@
             pltpu.VMEM((1, HID), f32),
             pltpu.VMEM((1, HD), f32),
             pltpu.VMEM((MB, HID), f32),
-            pltpu.SemaphoreType.DMA((2,)),
+            pltpu.SemaphoreType.DMA((3,)),
         ],
-        compiler_params=pltpu.CompilerParams(vmem_limit_bytes=40 * 1024 * 1024),
+        compiler_params=pltpu.CompilerParams(vmem_limit_bytes=56 * 1024 * 1024),
         name="clip_head",
-    )(idx, rate0, *pieces, w, *params)
+    )(idx, rate0, *pieces, *weights, *params)
 
 
 def ring(x, axis, by):
     size = lax.axis_size(axis)
     return lax.ppermute(x, axis, [(i, (i + by) % size) for i in range(size)])
+
+
+def to_workers(x, by):
+    return lax.ppermute(x, "x", [(i, (i + by) % 4) for i in range(4) if (i + by) % 4 < 3])
 
 
 def local(
@@ -273,39 +302,45 @@
     inner_rate,
     out_gain,
 ):
-    zi, x, core = (lax.axis_index(n).astype(jnp.int32) for n in ("zi", "x", "core"))
+    zc, zi, x, core = (lax.axis_index(n).astype(jnp.int32) for n in ("zc", "zi", "x", "core"))
+    odd = zc % 2
     blocks = pack(jnp.transpose(w_qkv, (1, 0, 2)), jnp.transpose(w_rate))
     blocks = lax.all_to_all(blocks, "x", 0, 0, tiled=True)
-    blocks = jnp.transpose(blocks, (1, 0, 2, 3))[None]
-    blocks = jnp.broadcast_to(blocks, (8, 2, 4, ROWS, 128)).reshape(16, 4, ROWS, 128)
-    weights = lax.all_to_all(blocks, ("zc", "zi"), 0, 0, tiled=True)
-    weights = weights.reshape(64, ROWS, 128)
-
     mine = lax.dynamic_slice(tokens, (0, core * HALF), (TOK, HALF))
     across = ring(mine, "zi", 1)
+    blocks, across = lax.optimization_barrier((blocks, across))
+    keep = lax.dynamic_index_in_dim(blocks, zi, 1, keepdims=False)
+    flip = lax.dynamic_index_in_dim(blocks, 1 - zi, 1, keepdims=False)
+    blocks = jnp.broadcast_to(jnp.stack([keep, flip])[None], (4, 2, 4, ROWS, 128))
+    near = lax.all_to_all(blocks.reshape(8, 4, ROWS, 128), "zc", 0, 0, tiled=True)
+    swap = [(i, (i + 1) % 16 if i % 2 else (i - 1) % 16) for i in range(16)]
+
     pair = jnp.concatenate([mine, across], 0)
-    right, left = ring(pair, "x", 1), ring(pair, "x", -1)
-    far_own, far_across = ring(right[:TOK], "x", 1), ring(left[TOK:], "x", -1)
-    pieces = [tokens]
-    for piece in (across, right, left, far_own, far_across):
-        pieces += [piece, ring(piece, "core", 1)]
-
-    position = zi * 4 + x
-    idx = jnp.stack([jnp.minimum(position, HEADS_DEV - 1), zi, x, core])
+    parts = [to_workers(pair, by) for by in SHIFTS]
+    other = lax.ppermute(near, ("zc", "zi"), swap)
+    parts = [across] + parts
+    pieces = [tokens] + parts + [ring(part, "core", 1) for part in parts]
+
+    head = 2 * x + (zi + odd) % 2
+    idx = jnp.stack([jnp.minimum(head, HEADS_DEV - 1), zi, x, core])
     params = (layer_one, layer_two, bias_one, bias_two, inner_gain, inner_bias)
-    outs = chain(idx, inner_rate, pieces, weights, params)
-
-    got = lax.all_to_all(outs.reshape(8, TOK, HD), ("zi", "x"), 0, 0, tiled=True)[:HEADS_DEV]
-    total = jnp.sum(got, (0, 2))
-    offset = got - (total / (HEADS_DEV * HD))[None, :, None]
-    squares = jnp.sum(offset * offset, (0, 2))
+    outs = chain(idx, inner_rate, pieces, (near, other), params)
+
+    got = lax.all_to_all(outs, ("zi", "x"), 0, 0, tiled=True)
+    even_heads, odd_heads = got[:3], got[4:7]
+    got = jnp.stack(
+        [jnp.where(odd == 0, even_heads, odd_heads), jnp.where(odd == 0, odd_heads, even_heads)], 1
+    ).reshape(HEADS_DEV, HD, TOK)
+    total = jnp.sum(got, (0, 1))
+    offset = got - (total / (HEADS_DEV * HD))
+    squares = jnp.sum(offset * offset, (0, 1))
     stats = jnp.broadcast_to(jnp.stack([total, squares])[None], (8, 2, TOK))
     stats = lax.all_to_all(stats, ("y", "core"), 0, 0, tiled=True)
     mean = jnp.sum(stats[:, 0], 0) / D
     shift = stats[:, 0] / (HEADS_DEV * HD) - mean
     variance = jnp.sum(stats[:, 1] + (HEADS_DEV * HD) * shift * shift, 0) / D
-    normed = (got - mean[None, :, None]) * lax.rsqrt(variance + 1e-05)[None, :, None]
-    joined = jnp.transpose(normed, (1, 0, 2)).reshape(TOK, HEADS_DEV * HD)
+    normed = (got - mean) * lax.rsqrt(variance + 1e-05)
+    joined = jnp.transpose(normed.reshape(HEADS_DEV * HD, TOK))
     return (joined * out_gain).astype(bf16)
 
 

time: 191 us -> 143 us (0.75)
  blocking collectives: 29.5 us -> 0 us
  waiting for transfers between devices: 78.8 us -> 51.8 us
  starting transfers between devices: 44.3 us -> 58.5 us
  local copies, waits for them, and re-layouts: 6.54 us -> 3.36 us
  Pallas kernels: 30 us -> 27.4 us
    ppermute x10 -> x5, waiting for transfers between devices: 78.7 us -> 0.91 us  [ring(): return lax.ppermute(x, axis, [(i, (i + by) % size) for i in range(size)])]
    ppermute x0 -> x4, waiting for transfers between devices: none -> 35.1 us  [the longest x3 23.7 us: to_workers(): lax.ppermute(x, 'x', [(i, (i + by) % 4) for i in range(4) if (i + by) % 4...]
    all_to_all x3 -> x0, blocking collectives: 29.5 us -> none  [the longest x1 10.8 us: local(): stats = lax.all_to_all(stats, ('y', 'core'), 0, 0, tiled=True)]
    all_to_all x1 -> x4, waiting for transfers between devices: 0.01 us -> 15.7 us  [the longest x1 6.12 us: local(): got = lax.all_to_all(outs, ('zi', 'x'), 0, 0, tiled=True)]
    all_to_all x1 -> x4, starting transfers between devices: 15 us -> 28.5 us  [the longest x1 13.9 us: local(): lax.all_to_all(blocks.reshape(8, 4, ROWS, 128), 'zc', 0, 0, tiled=True)]
    ppermute x0 -> x4, starting transfers between devices: none -> 13.5 us  [the longest x3 8.46 us: to_workers(): lax.ppermute(x, 'x', [(i, (i + by) % 4) for i in range(4) if (i + by) % 4...]
    ppermute x10 -> x5, starting transfers between devices: 29.3 us -> 16.4 us  [ring(): return lax.ppermute(x, axis, [(i, (i + by) % size) for i in range(size)])]
    unnamed x24 -> x12, local copies, waits for them, and re-layouts: 4.16 us -> 0.03 us
  transfers between devices with their start and end apart: 11 -> 13, of which waited for: 3 -> 7; matrix products, arithmetic and copies ran while one was open for 0% -> 0% of each run, Pallas kernels for 0% -> 1%
where the time goes in v2:
time: 143 us; the launch traced here: 142 us
  starting transfers between devices  58.5 us (41%)
  waiting for transfers between devices  51.8 us (36%)
  Pallas kernels  27.4 us (19%)
  local copies, waits for them, and re-layouts  3.36 us (2%)
    pallas_call x1, Pallas kernels, chain(): pl.pallas_call(chain_kernel, out_shape=jax.ShapeDtypeStruct((8, HD, TOK),...  25.7 us
    ppermute x3, waiting for transfers between devices, to_workers(): lax.ppermute(x, 'x', [(i, (i + by) % 4) for i in range(4) if (i + by) % 4...  23.7 us
    ppermute x5, starting transfers between devices, ring(): return lax.ppermute(x, axis, [(i, (i + by) % size) for i in range(size)])  16.4 us
    all_to_all x1, starting transfers between devices, local(): lax.all_to_all(blocks.reshape(8, 4, ROWS, 128), 'zc', 0, 0, tiled=True)  13.9 us
    ppermute x1, waiting for transfers between devices, local(): other = lax.ppermute(near, ('zc', 'zi'), swap)  11.4 us
    ppermute x3, starting transfers between devices, to_workers(): lax.ppermute(x, 'x', [(i, (i + by) % 4) for i in range(4) if (i + by) % 4...  8.46 us
    all_to_all x1, starting transfers between devices, local(): stats = lax.all_to_all(stats, ('y', 'core'), 0, 0, tiled=True)  6.88 us
    all_to_all x1, waiting for transfers between devices, local(): got = lax.all_to_all(outs, ('zi', 'x'), 0, 0, tiled=True)  6.12 us
  transfers between devices with their start and end apart: 13, of which 7 were waited for; matrix products, arithmetic and copies ran while one was open for 0% of the time, Pallas kernels for 1%

profile of v2, /device:TPU:1, one launch (start us, length us, event | category | flops | bytes accessed | tf_op | source)
XLA Modules:
  0.0 142.2 jit_solution(3166954153248588419)
XLA Ops:
  0.0 1.0 constant_dynamic-slice_fusion
  1.0 4.4 %collective-permute-start = (bf16[128,1536]{1,0:T(8,128)(2,1)S(1)}, bf16[128,1536]{1,0:T(8,128)(2,1)S(1)}, u32[]{:S(2)}, u32[]{:S(2)}) collective-permute-start(bf16[128,1536]{1,0:T(8,128)(2,1)S(1)} %constant_dynamic-slice_fusion), channel_id=1, source_target_pairs={{0,32},{32,0},{1,33},{33,1},{2,34},{34,2},{3,35},{35,3},{4,36},{36... | collective-permute-start | bytes 1179656 | tf_op jit(solution)/shard_map/ppermute | solution.py:285
  5.4 1.7 %pack_weights.1 = bf16[4,2,80,128]{3,2,1,0:T(8,128)(2,1)} custom-call(bf16[3,48,384]{2,1,0:T(8,128)(2,1)} %bitcast.34, bf16[6,48]{1,0:T(8,128)(2,1)} %bitcast.38), custom_call_target="tpu_custom_call" | custom-call | tf_op jit(solution)/shard_map/pack_weights/pallas_call | solution.py:66
  7.1 4.0 %all-to-all-start = ((bf16[4,2,80,128]{3,2,1,0:T(8,128)(2,1)}), bf16[4,2,80,128]{3,2,1,0:T(8,128)(2,1)S(1)}, u32[]{:S(2)}, u32[]{:S(2)}) async-start(bf16[4,2,80,128]{3,2,1,0:T(8,128)(2,1)} %pack_weights.1), calls=%async_computation | async-start | bytes 327680 | tf_op jit(solution)/shard_map/all_to_all | solution.py:308
  11.1 5.0 %all-to-all-done = bf16[4,2,80,128]{3,2,1,0:T(8,128)(2,1)S(1)} async-done(((bf16[4,2,80,128]{3,2,1,0:T(8,128)(2,1)}), bf16[4,2,80,128]{3,2,1,0:T(8,128)(2,1)S(1)}, u32[]{:S(2)}, u32[]{:S(2)}) %all-to-all-start) | async-done | bytes 163872 | tf_op jit(solution)/shard_map/all_to_all | solution.py:308
  16.1 0.0 collective-permute-done.z_half
  16.1 0.0 copy-start.1
  16.1 0.9 broadcast_in_dim.4
  17.1 13.9 %all-to-all-start.1 = ((bf16[8,4,80,128]{3,2,1,0:T(8,128)(2,1)}), bf16[8,4,80,128]{3,2,1,0:T(8,128)(2,1)S(1)}, u32[]{:S(2)}, u32[]{:S(2)}) async-start(bf16[8,4,80,128]{3,2,1,0:T(8,128)(2,1)} %bitcast.8), calls=%async_computation.1 | async-start | bytes 1310720 | tf_op jit(solution)/shard_map/all_to_all | solution.py:315
  31.0 0.1 pad_maximum_fusion
  31.0 3.2 %collective-permute-start.3 = (bf16[256,1536]{1,0:T(8,128)(2,1)S(1)}, bf16[256,1536]{1,0:T(8,128)(2,1)S(1)}, u32[]{:S(2)}, u32[]{:S(2)}) collective-permute-start(bf16[256,1536]{1,0:T(8,128)(2,1)S(1)} %pad_maximum_fusion), channel_id=1, source_target_pairs={{0,16},{16,0},{24,8},{1,17},{17,1},{25,9},{2,18},{18,2},{26,10},{3... | collective-permute-start | bytes 2359304 | tf_op jit(solution)/shard_map/ppermute | solution.py:289
  34.2 1.3 collective-permute-start.2
  35.5 4.0 %collective-permute-start.1 = (bf16[256,1536]{1,0:T(8,128)(2,1)S(1)}, bf16[256,1536]{1,0:T(8,128)(2,1)S(1)}, u32[]{:S(2)}, u32[]{:S(2)}) collective-permute-start(bf16[256,1536]{1,0:T(8,128)(2,1)S(1)} %pad_maximum_fusion), channel_id=1, source_target_pairs={{0,8},{8,16},{24,0},{1,9},{9,17},{25,1},{2,10},{10,18},{26,2},{3,1... | collective-permute-start | bytes 2359304 | tf_op jit(solution)/shard_map/ppermute | solution.py:289
  39.5 11.3 %collective-permute-done.3.f_half = bf16[256,1536]{1,0:T(8,128)(2,1)S(1)} collective-permute-done((bf16[256,1536]{1,0:T(8,128)(2,1)S(1)}, bf16[256,1536]{1,0:T(8,128)(2,1)S(1)}, u32[]{:S(2)}, u32[]{:S(2)}) %collective-permute-start.3) | collective-permute-done | bytes 786464 | tf_op jit(solution)/shard_map/ppermute | solution.py:289
  50.8 0.0 copy-start.2
  50.9 5.5 %collective-permute-start.7 = (bf16[256,1536]{1,0:T(8,128)(2,1)S(1)}, bf16[256,1536]{1,0:T(8,128)(2,1)}, u32[]{:S(2)}, u32[]{:S(2)}) collective-permute-start(bf16[256,1536]{1,0:T(8,128)(2,1)S(1)} %collective-permute-done.3.f_half), channel_id=1, source_target_pairs={{0,1},{1,0},{2,3},{3,2},{4,5},{5,4},{6,7},{7,6},{8,9},{9,8},{10,11... | collective-permute-start | bytes 2359304 | tf_op jit(solution)/shard_map/ppermute | solution.py:285
  56.4 0.0 collective-permute-done.2.l_half
  56.4 0.0 copy-start.3
  56.4 1.9 %collective-permute-start.6 = (bf16[256,1536]{1,0:T(8,128)(2,1)S(1)}, bf16[256,1536]{1,0:T(8,128)(2,1)}, u32[]{:S(2)}, u32[]{:S(2)}) collective-permute-start(bf16[256,1536]{1,0:T(8,128)(2,1)S(1)} %collective-permute-done.2.l_half), channel_id=1, source_target_pairs={{0,1},{1,0},{2,3},{3,2},{4,5},{5,4},{6,7},{7,6},{8,9},{9,8},{10,11... | collective-permute-start | bytes 2359304 | tf_op jit(solution)/shard_map/ppermute | solution.py:285
  58.4 12.4 %collective-permute-done.1.r_half = bf16[256,1536]{1,0:T(8,128)(2,1)S(1)} collective-permute-done((bf16[256,1536]{1,0:T(8,128)(2,1)S(1)}, bf16[256,1536]{1,0:T(8,128)(2,1)S(1)}, u32[]{:S(2)}, u32[]{:S(2)}) %collective-permute-start.1) | collective-permute-done | bytes 786464 | tf_op jit(solution)/shard_map/ppermute | solution.py:289
  70.8 0.0 copy-start.4
  70.8 2.4 %collective-permute-start.5 = (bf16[256,1536]{1,0:T(8,128)(2,1)S(1)}, bf16[256,1536]{1,0:T(8,128)(2,1)}, u32[]{:S(2)}, u32[]{:S(2)}) collective-permute-start(bf16[256,1536]{1,0:T(8,128)(2,1)S(1)} %collective-permute-done.1.r_half), channel_id=1, source_target_pairs={{0,1},{1,0},{2,3},{3,2},{4,5},{5,4},{6,7},{7,6},{8,9},{9,8},{10,11... | collective-permute-start | bytes 2359304 | tf_op jit(solution)/shard_map/ppermute | solution.py:285
  73.2 0.0 all-to-all-done.1.near
  73.2 0.0 copy-start
  73.2 5.0 %collective-permute-start.8 = (bf16[8,4,80,128]{3,2,1,0:T(8,128)(2,1)S(1)}, bf16[8,4,80,128]{3,2,1,0:T(8,128)(2,1)}, u32[]{:S(2)}, u32[]{:S(2)}) collective-permute-start(bf16[8,4,80,128]{3,2,1,0:T(8,128)(2,1)S(1)} %all-to-all-done.1.near), channel_id=1, source_target_pairs={{0,480},{32,64},{64,32},{96,128},{128,96},{160,192},{192,160},{224... | collective-permute-start | bytes 1966088 | tf_op jit(solution)/shard_map/ppermute | solution.py:320
  78.2 0.0 copy-done.1
  78.2 2.2 %collective-permute-start.4 = (bf16[128,1536]{1,0:T(8,128)(2,1)S(1)}, bf16[128,1536]{1,0:T(8,128)(2,1)}, u32[]{:S(2)}, u32[]{:S(2)}) collective-permute-start(bf16[128,1536]{1,0:T(8,128)(2,1)S(1)} %collective-permute-done.z_half), channel_id=1, source_target_pairs={{0,1},{1,0},{2,3},{3,2},{4,5},{5,4},{6,7},{7,6},{8,9},{9,8},{10,11... | collective-permute-start | bytes 1179656 | tf_op jit(solution)/shard_map/ppermute | solution.py:285
  80.5 0.6 pad_add_fusion.idx
  81.1 0.9 collective-permute-done.4.z_sibling
  82.0 0.0 collective-permute-done.7.f_sibling
  82.0 0.0 collective-permute-done.6.l_sibling
  82.0 0.0 collective-permute-done.5.r_sibling
  82.0 11.4 %collective-permute-done.8.other = bf16[8,4,80,128]{3,2,1,0:T(8,128)(2,1)} collective-permute-done((bf16[8,4,80,128]{3,2,1,0:T(8,128)(2,1)S(1)}, bf16[8,4,80,128]{3,2,1,0:T(8,128)(2,1)}, u32[]{:S(2)}, u32[]{:S(2)}) %collective-permute-start.8) | collective-permute-done | bytes 655392 | tf_op jit(solution)/shard_map/ppermute | solution.py:320
  93.4 0.0 copy-done.2
  93.4 0.0 copy-done.3
  93.4 0.0 copy-done.4
  93.4 0.0 copy-done
  93.4 25.7 %clip_head.1 = f32[8,64,128]{2,1,0:T(8,128)} custom-call(s32[4]{0:T(128)} %pad_add_fusion.idx, f32[6]{0:T(128)} %rate0.1, bf16[128,3072]{1,0:T(8,128)(2,1)} %own.1, bf16[128,1536]{1,0:T(8,128)(2,1)} %copy-done.1, bf16[256,1536]{1,0:T(8,128)(2,1)} %copy-done.4, bf16[256,1536]{1,0:T(8,128)(2,1)} %copy-done.3, bf16[256,1536]{1,0:T(8,128)(2,1)} %copy-done.2, ...), custom_call_target="tpu_custom_call" | custom-call | tf_op jit(solution)/shard_map/clip_head/pallas_call | solution.py:250
  119.1 0.0 copy-start.5
  119.2 3.7 %all-to-all-start.2 = ((f32[8,64,128]{2,1,0:T(8,128)}), f32[8,64,128]{2,1,0:T(8,128)S(1)}, u32[]{:S(2)}, u32[]{:S(2)}) async-start(f32[8,64,128]{2,1,0:T(8,128)} %clip_head.1), calls=%async_computation.2 | async-start | bytes 524288 | tf_op jit(solution)/shard_map/all_to_all | solution.py:329
  122.9 6.1 %all-to-all-done.2 = f32[8,64,128]{2,1,0:T(8,128)S(1)} async-done(((f32[8,64,128]{2,1,0:T(8,128)}), f32[8,64,128]{2,1,0:T(8,128)S(1)}, u32[]{:S(2)}, u32[]{:S(2)}) %all-to-all-start.2) | async-done | bytes 262176 | tf_op jit(solution)/shard_map/all_to_all | solution.py:329
  129.1 0.1 multiply_reduce_fusion
  129.1 0.6 broadcast_in_dim.5
  129.8 6.9 %all-to-all-start.3 = ((f32[8,2,128]{2,1,0:T(2,128)}), f32[8,2,128]{2,1,0:T(2,128)S(1)}, u32[]{:S(2)}, u32[]{:S(2)}) async-start(f32[8,2,128]{2,1,0:T(2,128)} %broadcast_in_dim.5), calls=%async_computation.3 | async-start | bytes 16384 | tf_op jit(solution)/shard_map/all_to_all | solution.py:338
  136.6 4.6 %all-to-all-done.3 = f32[8,2,128]{2,1,0:T(2,128)S(1)} async-done(((f32[8,2,128]{2,1,0:T(2,128)}), f32[8,2,128]{2,1,0:T(2,128)S(1)}, u32[]{:S(2)}, u32[]{:S(2)}) %all-to-all-start.3) | async-done | bytes 8224 | tf_op jit(solution)/shard_map/all_to_all | solution.py:338
  141.3 0.0 copy-done.5
  141.3 0.1 fusion.2
  141.4 0.8 copy.20
  (11 shorter events, 0.2 us)
Async XLA Ops:
  1.0 15.1 %collective-permute-start = (bf16[128,1536]{1,0:T(8,128)(2,1)S(1)}, bf16[128,1536]{1,0:T(8,128)(2,1)S(1)}, u32[]{:S(2)}, u32[]{:S(2)}) collective-permute-start(bf16[128,1536]{1,0:T(8,128)(2,1)S(1)} %constant_dynamic-slice_fusion), channel_id=1, source_target_pairs={{0,32},{32,0},{1,33},{33,1},{2,34},{34,2},{3,35},{35,3},{4,36},{36... | collective-permute-start | bytes 1179656 | tf_op jit(solution)/shard_map/ppermute | solution.py:285
  7.1 9.0 %all-to-all-start = ((bf16[4,2,80,128]{3,2,1,0:T(8,128)(2,1)}), bf16[4,2,80,128]{3,2,1,0:T(8,128)(2,1)S(1)}, u32[]{:S(2)}, u32[]{:S(2)}) async-start(bf16[4,2,80,128]{3,2,1,0:T(8,128)(2,1)} %pack_weights.1), calls=%async_computation | async-start | bytes 327680 | tf_op jit(solution)/shard_map/all_to_all | solution.py:308
  16.1 62.1 %copy-start.1 = (bf16[128,1536]{1,0:T(8,128)(2,1)}, bf16[128,1536]{1,0:T(8,128)(2,1)S(1)}, u32[]{:S(2)}) copy-start(bf16[128,1536]{1,0:T(8,128)(2,1)S(1)} %collective-permute-done.z_half) | copy-start | bytes 1179652
  17.1 56.1 %all-to-all-start.1 = ((bf16[8,4,80,128]{3,2,1,0:T(8,128)(2,1)}), bf16[8,4,80,128]{3,2,1,0:T(8,128)(2,1)S(1)}, u32[]{:S(2)}, u32[]{:S(2)}) async-start(bf16[8,4,80,128]{3,2,1,0:T(8,128)(2,1)} %bitcast.8), calls=%async_computation.1 | async-start | bytes 1310720 | tf_op jit(solution)/shard_map/all_to_all | solution.py:315
  31.0 19.8 %collective-permute-start.3 = (bf16[256,1536]{1,0:T(8,128)(2,1)S(1)}, bf16[256,1536]{1,0:T(8,128)(2,1)S(1)}, u32[]{:S(2)}, u32[]{:S(2)}) collective-permute-start(bf16[256,1536]{1,0:T(8,128)(2,1)S(1)} %pad_maximum_fusion), channel_id=1, source_target_pairs={{0,16},{16,0},{24,8},{1,17},{17,1},{25,9},{2,18},{18,2},{26,10},{3... | collective-permute-start | bytes 2359304 | tf_op jit(solution)/shard_map/ppermute | solution.py:289
  34.2 22.2 %collective-permute-start.2 = (bf16[256,1536]{1,0:T(8,128)(2,1)S(1)}, bf16[256,1536]{1,0:T(8,128)(2,1)S(1)}, u32[]{:S(2)}, u32[]{:S(2)}) collective-permute-start(bf16[256,1536]{1,0:T(8,128)(2,1)S(1)} %pad_maximum_fusion), channel_id=1, source_target_pairs={{8,0},{16,8},{24,16},{9,1},{17,9},{25,17},{10,2},{18,10},{26,18},{... | collective-permute-start | bytes 2359304 | tf_op jit(solution)/shard_map/ppermute | solution.py:289
  35.5 35.2 %collective-permute-start.1 = (bf16[256,1536]{1,0:T(8,128)(2,1)S(1)}, bf16[256,1536]{1,0:T(8,128)(2,1)S(1)}, u32[]{:S(2)}, u32[]{:S(2)}) collective-permute-start(bf16[256,1536]{1,0:T(8,128)(2,1)S(1)} %pad_maximum_fusion), channel_id=1, source_target_pairs={{0,8},{8,16},{24,0},{1,9},{9,17},{25,1},{2,10},{10,18},{26,2},{3,1... | collective-permute-start | bytes 2359304 | tf_op jit(solution)/shard_map/ppermute | solution.py:289
  50.8 42.5 %copy-start.2 = (bf16[256,1536]{1,0:T(8,128)(2,1)}, bf16[256,1536]{1,0:T(8,128)(2,1)S(1)}, u32[]{:S(2)}) copy-start(bf16[256,1536]{1,0:T(8,128)(2,1)S(1)} %collective-permute-done.3.f_half) | copy-start | bytes 2359300
  50.9 31.1 %collective-permute-start.7 = (bf16[256,1536]{1,0:T(8,128)(2,1)S(1)}, bf16[256,1536]{1,0:T(8,128)(2,1)}, u32[]{:S(2)}, u32[]{:S(2)}) collective-permute-start(bf16[256,1536]{1,0:T(8,128)(2,1)S(1)} %collective-permute-done.3.f_half), channel_id=1, source_target_pairs={{0,1},{1,0},{2,3},{3,2},{4,5},{5,4},{6,7},{7,6},{8,9},{9,8},{10,11... | collective-permute-start | bytes 2359304 | tf_op jit(solution)/shard_map/ppermute | solution.py:285
  56.4 37.0 %copy-start.3 = (bf16[256,1536]{1,0:T(8,128)(2,1)}, bf16[256,1536]{1,0:T(8,128)(2,1)S(1)}, u32[]{:S(2)}) copy-start(bf16[256,1536]{1,0:T(8,128)(2,1)S(1)} %collective-permute-done.2.l_half) | copy-start | bytes 2359300
  56.4 25.6 %collective-permute-start.6 = (bf16[256,1536]{1,0:T(8,128)(2,1)S(1)}, bf16[256,1536]{1,0:T(8,128)(2,1)}, u32[]{:S(2)}, u32[]{:S(2)}) collective-permute-start(bf16[256,1536]{1,0:T(8,128)(2,1)S(1)} %collective-permute-done.2.l_half), channel_id=1, source_target_pairs={{0,1},{1,0},{2,3},{3,2},{4,5},{5,4},{6,7},{7,6},{8,9},{9,8},{10,11... | collective-permute-start | bytes 2359304 | tf_op jit(solution)/shard_map/ppermute | solution.py:285
  70.8 22.6 %copy-start.4 = (bf16[256,1536]{1,0:T(8,128)(2,1)}, bf16[256,1536]{1,0:T(8,128)(2,1)S(1)}, u32[]{:S(2)}) copy-start(bf16[256,1536]{1,0:T(8,128)(2,1)S(1)} %collective-permute-done.1.r_half) | copy-start | bytes 2359300
  70.8 11.2 %collective-permute-start.5 = (bf16[256,1536]{1,0:T(8,128)(2,1)S(1)}, bf16[256,1536]{1,0:T(8,128)(2,1)}, u32[]{:S(2)}, u32[]{:S(2)}) collective-permute-start(bf16[256,1536]{1,0:T(8,128)(2,1)S(1)} %collective-permute-done.1.r_half), channel_id=1, source_target_pairs={{0,1},{1,0},{2,3},{3,2},{4,5},{5,4},{6,7},{7,6},{8,9},{9,8},{10,11... | collective-permute-start | bytes 2359304 | tf_op jit(solution)/shard_map/ppermute | solution.py:285
  73.2 20.2 %copy-start = (bf16[8,4,80,128]{3,2,1,0:T(8,128)(2,1)}, bf16[8,4,80,128]{3,2,1,0:T(8,128)(2,1)S(1)}, u32[]{:S(2)}) copy-start(bf16[8,4,80,128]{3,2,1,0:T(8,128)(2,1)S(1)} %all-to-all-done.1.near) | copy-start | bytes 1966084
  73.2 20.2 %collective-permute-start.8 = (bf16[8,4,80,128]{3,2,1,0:T(8,128)(2,1)S(1)}, bf16[8,4,80,128]{3,2,1,0:T(8,128)(2,1)}, u32[]{:S(2)}, u32[]{:S(2)}) collective-permute-start(bf16[8,4,80,128]{3,2,1,0:T(8,128)(2,1)S(1)} %all-to-all-done.1.near), channel_id=1, source_target_pairs={{0,480},{32,64},{64,32},{96,128},{128,96},{160,192},{192,160},{224... | collective-permute-start | bytes 1966088 | tf_op jit(solution)/shard_map/ppermute | solution.py:320
  78.2 3.7 %collective-permute-start.4 = (bf16[128,1536]{1,0:T(8,128)(2,1)S(1)}, bf16[128,1536]{1,0:T(8,128)(2,1)}, u32[]{:S(2)}, u32[]{:S(2)}) collective-permute-start(bf16[128,1536]{1,0:T(8,128)(2,1)S(1)} %collective-permute-done.z_half), channel_id=1, source_target_pairs={{0,1},{1,0},{2,3},{3,2},{4,5},{5,4},{6,7},{7,6},{8,9},{9,8},{10,11... | collective-permute-start | bytes 1179656 | tf_op jit(solution)/shard_map/ppermute | solution.py:285
  119.1 22.2 %copy-start.5 = (f32[384]{0:T(512)S(1)}, f32[384]{0:T(512)}, u32[]{:S(2)}) copy-start(f32[384]{0:T(512)} %param.21) | copy-start | bytes 4612
  119.2 9.9 %all-to-all-start.2 = ((f32[8,64,128]{2,1,0:T(8,128)}), f32[8,64,128]{2,1,0:T(8,128)S(1)}, u32[]{:S(2)}, u32[]{:S(2)}) async-start(f32[8,64,128]{2,1,0:T(8,128)} %clip_head.1), calls=%async_computation.2 | async-start | bytes 524288 | tf_op jit(solution)/shard_map/all_to_all | solution.py:329
  129.8 11.5 %all-to-all-start.3 = ((f32[8,2,128]{2,1,0:T(2,128)}), f32[8,2,128]{2,1,0:T(2,128)S(1)}, u32[]{:S(2)}, u32[]{:S(2)}) async-start(f32[8,2,128]{2,1,0:T(2,128)} %broadcast_in_dim.5), calls=%async_computation.3 | async-start | bytes 16384 | tf_op jit(solution)/shard_map/all_to_all | solution.py:338

commit v3 on v2

--- a/solution.py
+++ b/solution.py
@@ -109,22 +109,30 @@
     Ab,
     Bb,
     a,
-    b,
     hk,
     sem,
+    row_sem,
 ):
     head, zi, x, core = idx[0], idx[1], idx[2], idx[3]
 
     def place(src, z_of, x_of, part):
-        row = pl.multiple_of((z_of * 4 + lax.rem(x_of + 8, 4)) * TOK, TOK)
+        spot = z_of * 4 + lax.rem(x_of + 8, 4)
+        row = pl.multiple_of(spot * TOK, TOK)
         col = pl.multiple_of(part * HALF, HALF)
-        return pltpu.make_async_copy(src, T.at[pl.ds(row, TOK), pl.ds(col, HALF)], sem.at[0])
-
+        there = T.at[pl.ds(row, TOK), pl.ds(col, HALF)]
+        return pltpu.make_async_copy(src, there, row_sem.at[spot])
+
+    def wait_rows(spot):
+        rows = T.at[pl.ds(pl.multiple_of(spot * TOK, TOK), TOK), :]
+        pltpu.make_async_copy(rows, rows, row_sem.at[spot]).wait()
+
+    heavy = [
+        pltpu.make_async_copy(near, W.at[:, zi], sem.at[1]),
+        pltpu.make_async_copy(other, W.at[:, 1 - zi], sem.at[1]),
+    ]
     row = pl.multiple_of((zi * 4 + x) * TOK, TOK)
     copies = [
-        pltpu.make_async_copy(near, W.at[:, zi], sem.at[1]),
-        pltpu.make_async_copy(other, W.at[:, 1 - zi], sem.at[1]),
-        pltpu.make_async_copy(own, T.at[pl.ds(row, TOK), :], sem.at[0]),
+        pltpu.make_async_copy(own, T.at[pl.ds(row, TOK), :], row_sem.at[zi * 4 + x]),
     ]
     halves = (z_half, r_half, l_half, f_half)
     siblings = (z_sibling, r_sibling, l_sibling, f_sibling)
@@ -134,32 +142,17 @@
             copies.append(place(pair.at[0:TOK], zi, x - by, part))
             copies.append(place(pair.at[TOK : 2 * TOK], 1 - zi, x - by, part))
     small = [
-        pltpu.make_async_copy(A0_hbm.at[head], A0, sem.at[2]),
-        pltpu.make_async_copy(B0_hbm.at[head], B0, sem.at[2]),
-        pltpu.make_async_copy(a0_hbm, a0, sem.at[2]),
-        pltpu.make_async_copy(b0_hbm, b0, sem.at[2]),
-        pltpu.make_async_copy(gain_hbm, gain, sem.at[2]),
-        pltpu.make_async_copy(bias_hbm, bias, sem.at[2]),
+        pltpu.make_async_copy(A0_hbm.at[head], A0, sem.at[0]),
+        pltpu.make_async_copy(B0_hbm.at[head], B0, sem.at[0]),
+        pltpu.make_async_copy(a0_hbm, a0, sem.at[0]),
+        pltpu.make_async_copy(b0_hbm, b0, sem.at[0]),
+        pltpu.make_async_copy(gain_hbm, gain, sem.at[0]),
+        pltpu.make_async_copy(bias_hbm, bias, sem.at[0]),
     ]
-    for c in small + copies:
+    for c in heavy + small + copies:
         c.start()
-    for c in small:
+    for c in heavy:
         c.wait()
-
-    gn = gain[pl.ds(head, 1), :]
-    bs = bias[pl.ds(head, 1), :]
-    A[...] = A0[...]
-    Ab[...] = A0[...].astype(bf16)
-    Bc = B0[...]
-    Bc = Bc - jnp.mean(Bc, 0, keepdims=True)
-    B[...] = Bc
-    Bb[...] = Bc.astype(bf16)
-    a[...] = a0[pl.ds(head, 1), :]
-    bb = b0[pl.ds(head, 1), :]
-    b[...] = bb - jnp.mean(bb, 1, keepdims=True)
-
-    copies[0].wait()
-    copies[1].wait()
     WA[:, 0:128] = W[:, :, :, 0:48, :].reshape(D, 128)
     X = W[:, :, :, 48:80, :].reshape(64, 32, 128)
     lane = lax.broadcasted_iota(jnp.int32, (1, 16, 128), 2)
@@ -174,30 +167,48 @@
     qs = jnp.concatenate([X.astype(f32), qb], 1).reshape(D, 128)
     wide = lax.broadcasted_iota(jnp.int32, (1, 128), 1)
     WA[:, 128:256] = jnp.where(wide < 64, qs, gates).astype(bf16)
-    for c in copies[2:]:
+    for c in small:
         c.wait()
 
+    gn = gain[pl.ds(head, 1), :]
+    bs = bias[pl.ds(head, 1), :]
+    A[...] = A0[...]
+    Ab[...] = A0[...].astype(bf16)
+    Bc = B0[...]
+    Bc = Bc - jnp.mean(Bc, 0, keepdims=True)
+    B[...] = Bc
+    Bb[...] = Bc.astype(bf16)
+    a[...] = a0[pl.ds(head, 1), :]
+    bb = b0[pl.ds(head, 1), :]
+    bb = bb - jnp.mean(bb, 1, keepdims=True)
+    gain_col = jnp.transpose(gn)
+    square_col = gain_col * gain_col
     base = rate0[head] * (1.0 / MB)
 
     def project(i, carry):
-        rows = pl.ds(pl.multiple_of(i * 256, 256), 256)
+        for j in range(4):
+            wait_rows(4 * i + j)
+        rows = pl.ds(pl.multiple_of(i * 512, 512), 512)
         out = mm(T[rows, :], WA[...])
         KV[rows, :] = out[:, 0:128].astype(bf16)
         Q[rows, :] = out[:, 128:192].astype(bf16)
         RT[rows, :] = base * jax.nn.sigmoid(out[:, 192:256])
         return carry
 
-    lax.fori_loop(0, CLIP // 256, project, 0)
+    lax.fori_loop(0, CLIP // 512, project, 0)
 
     hk[...] = mm(KV[0:MB, 0:HD], Ab[...]) + a[...]
-    g2 = gn * gn
 
     def answer(rows, q, act, Bv, bv):
         c = mm(act, Bv, NT) + bv
         scale = lax.rsqrt(jnp.mean(c * c, 1, keepdims=True) + 1e-6)
         O[rows, :] = q.astype(f32) + (gn * c * scale + bs)
 
+    def mean(z):
+        return jnp.sum(z, 0, keepdims=True) * (1.0 / HD)
+
     def step(t, carry):
+        b_col, b_row = carry
         now = pl.ds(pl.multiple_of(t * MB, MB), MB)
         nxt = pl.ds(pl.multiple_of(jnp.minimum(t + 1, STEPS - 1) * MB, MB), MB)
         old = pl.ds(pl.multiple_of(jnp.maximum(t - 1, 0) * MB, MB), MB)
@@ -205,40 +216,38 @@
         v = KV[now, HD : 2 * HD]
         kn = KV[nxt, 0:HD]
         qp = Q[old, :]
-        w = RT[now, :]
-        Av, Bv, av, bv = Ab[...], Bb[...], a[...], b[...]
+        Av, Bv, av = Ab[...], Bb[...], a[...]
+        u = jnp.transpose(gn * (bs - (v.astype(f32) - k.astype(f32))))
+        w = jnp.transpose(RT[now, :])[0:1, :]
+        s5 = mean(u)
         act, slope = gelu_and_slope(hk[...])
         act = act.astype(bf16)
-        c = mm(act, Bv, NT) + bv
-        u = gn * (bs - (v.astype(f32) - k.astype(f32)))
-        gc = g2 * c
-        s1 = jnp.mean(c * c, 1, keepdims=True)
-        s2 = jnp.mean(gc, 1, keepdims=True)
-        s3 = jnp.mean(gc * c, 1, keepdims=True)
-        s4 = jnp.mean(u * c, 1, keepdims=True)
-        s5 = jnp.mean(u, 1, keepdims=True)
+        c = mm(Bv, act, NT) + b_col
+        gc = square_col * c
+        s1, s2, s3, s4 = mean(c * c), mean(gc), mean(gc * c), mean(u * c)
         rs = lax.rsqrt(s1 + 1e-6)
-        dm = (w * rs) * (gc * rs + (u - (rs * s2 + s5)) - c * (rs * rs * (rs * s3 + s4)))
+        wr = w * rs
+        dm = gc * (wr * rs) + (u - s5) * wr - wr * (rs * s2) - c * (wr * (rs * rs) * (rs * s3 + s4))
         dmb = dm.astype(bf16)
-        dh = mm(dmb, Bv) * slope
+        dh = mm(dmb, Bv, TN) * slope
         dhb = dh.astype(bf16)
         gram = (mm(kn, k, NT) + 1.0).astype(bf16)
         hk[...] = mm(kn, Av) + av - mm(gram, dhb)
-        answer(old, qp, gelu(mm(qp, Av) + av).astype(bf16), Bv, bv)
-        Bn = B[...] - mm(dmb, act, TN)
+        answer(old, qp, gelu(mm(qp, Av) + av).astype(bf16), Bv, b_row)
+        Bn = B[...] - mm(dmb, act)
         B[...] = Bn
         Bb[...] = Bn.astype(bf16)
-        b[...] = bv - jnp.sum(dm, 0, keepdims=True)
         An = A[...] - mm(k, dhb, TN)
         A[...] = An
         Ab[...] = An.astype(bf16)
         a[...] = av - jnp.sum(dh, 0, keepdims=True)
-        return carry
-
-    lax.fori_loop(0, STEPS, step, 0, unroll=4)
+        b_col = b_col - jnp.sum(dm, 1, keepdims=True)
+        return b_col, jnp.transpose(b_col)
+
+    _, b_row = lax.fori_loop(0, STEPS, step, (jnp.transpose(bb), bb), unroll=8)
     last = pl.ds(CLIP - MB, MB)
     q = Q[last, :]
-    answer(last, q, gelu(mm(q, Ab[...]) + a[...]).astype(bf16), Bb[...], b[...])
+    answer(last, q, gelu(mm(q, Ab[...]) + a[...]).astype(bf16), Bb[...], b_row)
     for i in range(8):
         o_ref[i] = jnp.transpose(O[i * TOK : (i + 1) * TOK, :])
 
@@ -271,9 +280,9 @@
             pltpu.VMEM((HD, HID), bf16),
             pltpu.VMEM((HD, HID), bf16),
             pltpu.VMEM((1, HID), f32),
-            pltpu.VMEM((1, HD), f32),
             pltpu.VMEM((MB, HID), f32),
-            pltpu.SemaphoreType.DMA((3,)),
+            pltpu.SemaphoreType.DMA((2,)),
+            pltpu.SemaphoreType.DMA((8,)),
         ],
         compiler_params=pltpu.CompilerParams(vmem_limit_bytes=56 * 1024 * 1024),
         name="clip_head",

time: 143 us -> 141 us (0.986)
  Pallas kernels: 27.4 us -> 25.3 us
    pallas_call x1, Pallas kernels: 25.7 us -> 23.6 us  [chain(): pl.pallas_call(chain_kernel, out_shape=jax.ShapeDtypeStruct((8, HD, TOK),...]
where the time goes in v3:
time: 141 us; the launch traced here: 140 us
  starting transfers between devices  58.5 us (41%)
  waiting for transfers between devices  51.8 us (37%)
  Pallas kernels  25.3 us (18%)
  local copies, waits for them, and re-layouts  3.36 us (2%)
    ppermute x3, waiting for transfers between devices, to_workers(): lax.ppermute(x, 'x', [(i, (i + by) % 4) for i in range(4) if (i + by) % 4...  23.7 us
    pallas_call x1, Pallas kernels, chain(): pl.pallas_call(chain_kernel, out_shape=jax.ShapeDtypeStruct((8, HD, TOK),...  23.6 us
    ppermute x5, starting transfers between devices, ring(): return lax.ppermute(x, axis, [(i, (i + by) % size) for i in range(size)])  16.4 us
    all_to_all x1, starting transfers between devices, local(): lax.all_to_all(blocks.reshape(8, 4, ROWS, 128), 'zc', 0, 0, tiled=True)  13.9 us
    ppermute x1, waiting for transfers between devices, local(): other = lax.ppermute(near, ('zc', 'zi'), swap)  11.4 us
    ppermute x3, starting transfers between devices, to_workers(): lax.ppermute(x, 'x', [(i, (i + by) % 4) for i in range(4) if (i + by) % 4...  8.46 us
    all_to_all x1, starting transfers between devices, local(): stats = lax.all_to_all(stats, ('y', 'core'), 0, 0, tiled=True)  6.88 us
    all_to_all x1, waiting for transfers between devices, local(): got = lax.all_to_all(outs, ('zi', 'x'), 0, 0, tiled=True)  6.12 us
  transfers between devices with their start and end apart: 13, of which 7 were waited for; matrix products, arithmetic and copies ran while one was open for 0% of the time, Pallas kernels for 1%

profile of v3, /device:TPU:1, one launch (start us, length us, event | category | flops | bytes accessed | tf_op | source)
XLA Modules:
  0.0 140.1 jit_solution(12624939983803682421)
XLA Ops:
  0.0 1.0 constant_dynamic-slice_fusion
  1.0 4.4 %collective-permute-start = (bf16[128,1536]{1,0:T(8,128)(2,1)S(1)}, bf16[128,1536]{1,0:T(8,128)(2,1)S(1)}, u32[]{:S(2)}, u32[]{:S(2)}) collective-permute-start(bf16[128,1536]{1,0:T(8,128)(2,1)S(1)} %constant_dynamic-slice_fusion), channel_id=1, source_target_pairs={{0,32},{32,0},{1,33},{33,1},{2,34},{34,2},{3,35},{35,3},{4,36},{36... | collective-permute-start | bytes 1179656 | tf_op jit(solution)/shard_map/ppermute | solution.py:294
  5.4 1.7 %pack_weights.1 = bf16[4,2,80,128]{3,2,1,0:T(8,128)(2,1)} custom-call(bf16[3,48,384]{2,1,0:T(8,128)(2,1)} %bitcast.34, bf16[6,48]{1,0:T(8,128)(2,1)} %bitcast.38), custom_call_target="tpu_custom_call" | custom-call | tf_op jit(solution)/shard_map/pack_weights/pallas_call | solution.py:66
  7.1 4.0 %all-to-all-start = ((bf16[4,2,80,128]{3,2,1,0:T(8,128)(2,1)}), bf16[4,2,80,128]{3,2,1,0:T(8,128)(2,1)S(1)}, u32[]{:S(2)}, u32[]{:S(2)}) async-start(bf16[4,2,80,128]{3,2,1,0:T(8,128)(2,1)} %pack_weights.1), calls=%async_computation | async-start | bytes 327680 | tf_op jit(solution)/shard_map/all_to_all | solution.py:317
  11.1 5.0 %all-to-all-done = bf16[4,2,80,128]{3,2,1,0:T(8,128)(2,1)S(1)} async-done(((bf16[4,2,80,128]{3,2,1,0:T(8,128)(2,1)}), bf16[4,2,80,128]{3,2,1,0:T(8,128)(2,1)S(1)}, u32[]{:S(2)}, u32[]{:S(2)}) %all-to-all-start) | async-done | bytes 163872 | tf_op jit(solution)/shard_map/all_to_all | solution.py:317
  16.1 0.0 collective-permute-done.z_half
  16.1 0.0 copy-start.1
  16.1 0.9 broadcast_in_dim.4
  17.1 13.9 %all-to-all-start.1 = ((bf16[8,4,80,128]{3,2,1,0:T(8,128)(2,1)}), bf16[8,4,80,128]{3,2,1,0:T(8,128)(2,1)S(1)}, u32[]{:S(2)}, u32[]{:S(2)}) async-start(bf16[8,4,80,128]{3,2,1,0:T(8,128)(2,1)} %bitcast.8), calls=%async_computation.1 | async-start | bytes 1310720 | tf_op jit(solution)/shard_map/all_to_all | solution.py:324
  31.0 0.1 pad_maximum_fusion
  31.0 3.2 %collective-permute-start.3 = (bf16[256,1536]{1,0:T(8,128)(2,1)S(1)}, bf16[256,1536]{1,0:T(8,128)(2,1)S(1)}, u32[]{:S(2)}, u32[]{:S(2)}) collective-permute-start(bf16[256,1536]{1,0:T(8,128)(2,1)S(1)} %pad_maximum_fusion), channel_id=1, source_target_pairs={{0,16},{16,0},{24,8},{1,17},{17,1},{25,9},{2,18},{18,2},{26,10},{3... | collective-permute-start | bytes 2359304 | tf_op jit(solution)/shard_map/ppermute | solution.py:298
  34.2 1.3 collective-permute-start.2
  35.5 4.0 %collective-permute-start.1 = (bf16[256,1536]{1,0:T(8,128)(2,1)S(1)}, bf16[256,1536]{1,0:T(8,128)(2,1)S(1)}, u32[]{:S(2)}, u32[]{:S(2)}) collective-permute-start(bf16[256,1536]{1,0:T(8,128)(2,1)S(1)} %pad_maximum_fusion), channel_id=1, source_target_pairs={{0,8},{8,16},{24,0},{1,9},{9,17},{25,1},{2,10},{10,18},{26,2},{3,1... | collective-permute-start | bytes 2359304 | tf_op jit(solution)/shard_map/ppermute | solution.py:298
  39.5 11.3 %collective-permute-done.3.f_half = bf16[256,1536]{1,0:T(8,128)(2,1)S(1)} collective-permute-done((bf16[256,1536]{1,0:T(8,128)(2,1)S(1)}, bf16[256,1536]{1,0:T(8,128)(2,1)S(1)}, u32[]{:S(2)}, u32[]{:S(2)}) %collective-permute-start.3) | collective-permute-done | bytes 786464 | tf_op jit(solution)/shard_map/ppermute | solution.py:298
  50.8 0.0 copy-start.2
  50.9 5.5 %collective-permute-start.7 = (bf16[256,1536]{1,0:T(8,128)(2,1)S(1)}, bf16[256,1536]{1,0:T(8,128)(2,1)}, u32[]{:S(2)}, u32[]{:S(2)}) collective-permute-start(bf16[256,1536]{1,0:T(8,128)(2,1)S(1)} %collective-permute-done.3.f_half), channel_id=1, source_target_pairs={{0,1},{1,0},{2,3},{3,2},{4,5},{5,4},{6,7},{7,6},{8,9},{9,8},{10,11... | collective-permute-start | bytes 2359304 | tf_op jit(solution)/shard_map/ppermute | solution.py:294
  56.4 0.0 collective-permute-done.2.l_half
  56.4 0.0 copy-start.3
  56.4 1.9 %collective-permute-start.6 = (bf16[256,1536]{1,0:T(8,128)(2,1)S(1)}, bf16[256,1536]{1,0:T(8,128)(2,1)}, u32[]{:S(2)}, u32[]{:S(2)}) collective-permute-start(bf16[256,1536]{1,0:T(8,128)(2,1)S(1)} %collective-permute-done.2.l_half), channel_id=1, source_target_pairs={{0,1},{1,0},{2,3},{3,2},{4,5},{5,4},{6,7},{7,6},{8,9},{9,8},{10,11... | collective-permute-start | bytes 2359304 | tf_op jit(solution)/shard_map/ppermute | solution.py:294
  58.4 12.4 %collective-permute-done.1.r_half = bf16[256,1536]{1,0:T(8,128)(2,1)S(1)} collective-permute-done((bf16[256,1536]{1,0:T(8,128)(2,1)S(1)}, bf16[256,1536]{1,0:T(8,128)(2,1)S(1)}, u32[]{:S(2)}, u32[]{:S(2)}) %collective-permute-start.1) | collective-permute-done | bytes 786464 | tf_op jit(solution)/shard_map/ppermute | solution.py:298
  70.8 0.0 copy-start.4
  70.8 2.4 %collective-permute-start.5 = (bf16[256,1536]{1,0:T(8,128)(2,1)S(1)}, bf16[256,1536]{1,0:T(8,128)(2,1)}, u32[]{:S(2)}, u32[]{:S(2)}) collective-permute-start(bf16[256,1536]{1,0:T(8,128)(2,1)S(1)} %collective-permute-done.1.r_half), channel_id=1, source_target_pairs={{0,1},{1,0},{2,3},{3,2},{4,5},{5,4},{6,7},{7,6},{8,9},{9,8},{10,11... | collective-permute-start | bytes 2359304 | tf_op jit(solution)/shard_map/ppermute | solution.py:294
  73.2 0.0 all-to-all-done.1.near
  73.2 0.0 copy-start
  73.2 5.0 %collective-permute-start.8 = (bf16[8,4,80,128]{3,2,1,0:T(8,128)(2,1)S(1)}, bf16[8,4,80,128]{3,2,1,0:T(8,128)(2,1)}, u32[]{:S(2)}, u32[]{:S(2)}) collective-permute-start(bf16[8,4,80,128]{3,2,1,0:T(8,128)(2,1)S(1)} %all-to-all-done.1.near), channel_id=1, source_target_pairs={{0,480},{32,64},{64,32},{96,128},{128,96},{160,192},{192,160},{224... | collective-permute-start | bytes 1966088 | tf_op jit(solution)/shard_map/ppermute | solution.py:329
  78.2 0.0 copy-done.1
  78.2 2.2 %collective-permute-start.4 = (bf16[128,1536]{1,0:T(8,128)(2,1)S(1)}, bf16[128,1536]{1,0:T(8,128)(2,1)}, u32[]{:S(2)}, u32[]{:S(2)}) collective-permute-start(bf16[128,1536]{1,0:T(8,128)(2,1)S(1)} %collective-permute-done.z_half), channel_id=1, source_target_pairs={{0,1},{1,0},{2,3},{3,2},{4,5},{5,4},{6,7},{7,6},{8,9},{9,8},{10,11... | collective-permute-start | bytes 1179656 | tf_op jit(solution)/shard_map/ppermute | solution.py:294
  80.5 0.6 pad_add_fusion.idx
  81.1 0.9 collective-permute-done.4.z_sibling
  82.0 0.0 collective-permute-done.7.f_sibling
  82.0 0.0 collective-permute-done.6.l_sibling
  82.0 0.0 collective-permute-done.5.r_sibling
  82.0 11.4 %collective-permute-done.8.other = bf16[8,4,80,128]{3,2,1,0:T(8,128)(2,1)} collective-permute-done((bf16[8,4,80,128]{3,2,1,0:T(8,128)(2,1)S(1)}, bf16[8,4,80,128]{3,2,1,0:T(8,128)(2,1)}, u32[]{:S(2)}, u32[]{:S(2)}) %collective-permute-start.8) | collective-permute-done | bytes 655392 | tf_op jit(solution)/shard_map/ppermute | solution.py:329
  93.4 0.0 copy-done.2
  93.4 0.0 copy-done.3
  93.4 0.0 copy-done.4
  93.4 0.0 copy-done
  93.4 23.6 %clip_head.1 = f32[8,64,128]{2,1,0:T(8,128)} custom-call(s32[4]{0:T(128)} %pad_add_fusion.idx, f32[6]{0:T(128)} %rate0.1, bf16[128,3072]{1,0:T(8,128)(2,1)} %own.1, bf16[128,1536]{1,0:T(8,128)(2,1)} %copy-done.1, bf16[256,1536]{1,0:T(8,128)(2,1)} %copy-done.4, bf16[256,1536]{1,0:T(8,128)(2,1)} %copy-done.3, bf16[256,1536]{1,0:T(8,128)(2,1)} %copy-done.2, ...), custom_call_target="tpu_custom_call" | custom-call | tf_op jit(solution)/shard_map/clip_head/pallas_call | solution.py:259
  117.0 0.0 copy-start.5
  117.0 3.7 %all-to-all-start.2 = ((f32[8,64,128]{2,1,0:T(8,128)}), f32[8,64,128]{2,1,0:T(8,128)S(1)}, u32[]{:S(2)}, u32[]{:S(2)}) async-start(f32[8,64,128]{2,1,0:T(8,128)} %clip_head.1), calls=%async_computation.2 | async-start | bytes 524288 | tf_op jit(solution)/shard_map/all_to_all | solution.py:338
  120.8 6.1 %all-to-all-done.2 = f32[8,64,128]{2,1,0:T(8,128)S(1)} async-done(((f32[8,64,128]{2,1,0:T(8,128)}), f32[8,64,128]{2,1,0:T(8,128)S(1)}, u32[]{:S(2)}, u32[]{:S(2)}) %all-to-all-start.2) | async-done | bytes 262176 | tf_op jit(solution)/shard_map/all_to_all | solution.py:338
  127.0 0.1 multiply_reduce_fusion
  127.0 0.6 broadcast_in_dim.5
  127.7 6.9 %all-to-all-start.3 = ((f32[8,2,128]{2,1,0:T(2,128)}), f32[8,2,128]{2,1,0:T(2,128)S(1)}, u32[]{:S(2)}, u32[]{:S(2)}) async-start(f32[8,2,128]{2,1,0:T(2,128)} %broadcast_in_dim.5), calls=%async_computation.3 | async-start | bytes 16384 | tf_op jit(solution)/shard_map/all_to_all | solution.py:347
  134.6 4.6 %all-to-all-done.3 = f32[8,2,128]{2,1,0:T(2,128)S(1)} async-done(((f32[8,2,128]{2,1,0:T(2,128)}), f32[8,2,128]{2,1,0:T(2,128)S(1)}, u32[]{:S(2)}, u32[]{:S(2)}) %all-to-all-start.3) | async-done | bytes 8224 | tf_op jit(solution)/shard_map/all_to_all | solution.py:347
  139.2 0.0 copy-done.5
  139.2 0.1 fusion.2
  139.4 0.8 copy.20
  (11 shorter events, 0.2 us)
Async XLA Ops:
  1.0 15.1 %collective-permute-start = (bf16[128,1536]{1,0:T(8,128)(2,1)S(1)}, bf16[128,1536]{1,0:T(8,128)(2,1)S(1)}, u32[]{:S(2)}, u32[]{:S(2)}) collective-permute-start(bf16[128,1536]{1,0:T(8,128)(2,1)S(1)} %constant_dynamic-slice_fusion), channel_id=1, source_target_pairs={{0,32},{32,0},{1,33},{33,1},{2,34},{34,2},{3,35},{35,3},{4,36},{36... | collective-permute-start | bytes 1179656 | tf_op jit(solution)/shard_map/ppermute | solution.py:294
  7.1 9.0 %all-to-all-start = ((bf16[4,2,80,128]{3,2,1,0:T(8,128)(2,1)}), bf16[4,2,80,128]{3,2,1,0:T(8,128)(2,1)S(1)}, u32[]{:S(2)}, u32[]{:S(2)}) async-start(bf16[4,2,80,128]{3,2,1,0:T(8,128)(2,1)} %pack_weights.1), calls=%async_computation | async-start | bytes 327680 | tf_op jit(solution)/shard_map/all_to_all | solution.py:317
  16.1 62.1 %copy-start.1 = (bf16[128,1536]{1,0:T(8,128)(2,1)}, bf16[128,1536]{1,0:T(8,128)(2,1)S(1)}, u32[]{:S(2)}) copy-start(bf16[128,1536]{1,0:T(8,128)(2,1)S(1)} %collective-permute-done.z_half) | copy-start | bytes 1179652
  17.1 56.1 %all-to-all-start.1 = ((bf16[8,4,80,128]{3,2,1,0:T(8,128)(2,1)}), bf16[8,4,80,128]{3,2,1,0:T(8,128)(2,1)S(1)}, u32[]{:S(2)}, u32[]{:S(2)}) async-start(bf16[8,4,80,128]{3,2,1,0:T(8,128)(2,1)} %bitcast.8), calls=%async_computation.1 | async-start | bytes 1310720 | tf_op jit(solution)/shard_map/all_to_all | solution.py:324
  31.0 19.8 %collective-permute-start.3 = (bf16[256,1536]{1,0:T(8,128)(2,1)S(1)}, bf16[256,1536]{1,0:T(8,128)(2,1)S(1)}, u32[]{:S(2)}, u32[]{:S(2)}) collective-permute-start(bf16[256,1536]{1,0:T(8,128)(2,1)S(1)} %pad_maximum_fusion), channel_id=1, source_target_pairs={{0,16},{16,0},{24,8},{1,17},{17,1},{25,9},{2,18},{18,2},{26,10},{3... | collective-permute-start | bytes 2359304 | tf_op jit(solution)/shard_map/ppermute | solution.py:298
  34.2 22.2 %collective-permute-start.2 = (bf16[256,1536]{1,0:T(8,128)(2,1)S(1)}, bf16[256,1536]{1,0:T(8,128)(2,1)S(1)}, u32[]{:S(2)}, u32[]{:S(2)}) collective-permute-start(bf16[256,1536]{1,0:T(8,128)(2,1)S(1)} %pad_maximum_fusion), channel_id=1, source_target_pairs={{8,0},{16,8},{24,16},{9,1},{17,9},{25,17},{10,2},{18,10},{26,18},{... | collective-permute-start | bytes 2359304 | tf_op jit(solution)/shard_map/ppermute | solution.py:298
  35.5 35.2 %collective-permute-start.1 = (bf16[256,1536]{1,0:T(8,128)(2,1)S(1)}, bf16[256,1536]{1,0:T(8,128)(2,1)S(1)}, u32[]{:S(2)}, u32[]{:S(2)}) collective-permute-start(bf16[256,1536]{1,0:T(8,128)(2,1)S(1)} %pad_maximum_fusion), channel_id=1, source_target_pairs={{0,8},{8,16},{24,0},{1,9},{9,17},{25,1},{2,10},{10,18},{26,2},{3,1... | collective-permute-start | bytes 2359304 | tf_op jit(solution)/shard_map/ppermute | solution.py:298
  50.8 42.5 %copy-start.2 = (bf16[256,1536]{1,0:T(8,128)(2,1)}, bf16[256,1536]{1,0:T(8,128)(2,1)S(1)}, u32[]{:S(2)}) copy-start(bf16[256,1536]{1,0:T(8,128)(2,1)S(1)} %collective-permute-done.3.f_half) | copy-start | bytes 2359300
  50.9 31.1 %collective-permute-start.7 = (bf16[256,1536]{1,0:T(8,128)(2,1)S(1)}, bf16[256,1536]{1,0:T(8,128)(2,1)}, u32[]{:S(2)}, u32[]{:S(2)}) collective-permute-start(bf16[256,1536]{1,0:T(8,128)(2,1)S(1)} %collective-permute-done.3.f_half), channel_id=1, source_target_pairs={{0,1},{1,0},{2,3},{3,2},{4,5},{5,4},{6,7},{7,6},{8,9},{9,8},{10,11... | collective-permute-start | bytes 2359304 | tf_op jit(solution)/shard_map/ppermute | solution.py:294
  56.4 37.0 %copy-start.3 = (bf16[256,1536]{1,0:T(8,128)(2,1)}, bf16[256,1536]{1,0:T(8,128)(2,1)S(1)}, u32[]{:S(2)}) copy-start(bf16[256,1536]{1,0:T(8,128)(2,1)S(1)} %collective-permute-done.2.l_half) | copy-start | bytes 2359300
  56.4 25.6 %collective-permute-start.6 = (bf16[256,1536]{1,0:T(8,128)(2,1)S(1)}, bf16[256,1536]{1,0:T(8,128)(2,1)}, u32[]{:S(2)}, u32[]{:S(2)}) collective-permute-start(bf16[256,1536]{1,0:T(8,128)(2,1)S(1)} %collective-permute-done.2.l_half), channel_id=1, source_target_pairs={{0,1},{1,0},{2,3},{3,2},{4,5},{5,4},{6,7},{7,6},{8,9},{9,8},{10,11... | collective-permute-start | bytes 2359304 | tf_op jit(solution)/shard_map/ppermute | solution.py:294
  70.8 22.6 %copy-start.4 = (bf16[256,1536]{1,0:T(8,128)(2,1)}, bf16[256,1536]{1,0:T(8,128)(2,1)S(1)}, u32[]{:S(2)}) copy-start(bf16[256,1536]{1,0:T(8,128)(2,1)S(1)} %collective-permute-done.1.r_half) | copy-start | bytes 2359300
  70.8 11.2 %collective-permute-start.5 = (bf16[256,1536]{1,0:T(8,128)(2,1)S(1)}, bf16[256,1536]{1,0:T(8,128)(2,1)}, u32[]{:S(2)}, u32[]{:S(2)}) collective-permute-start(bf16[256,1536]{1,0:T(8,128)(2,1)S(1)} %collective-permute-done.1.r_half), channel_id=1, source_target_pairs={{0,1},{1,0},{2,3},{3,2},{4,5},{5,4},{6,7},{7,6},{8,9},{9,8},{10,11... | collective-permute-start | bytes 2359304 | tf_op jit(solution)/shard_map/ppermute | solution.py:294
  73.2 20.2 %copy-start = (bf16[8,4,80,128]{3,2,1,0:T(8,128)(2,1)}, bf16[8,4,80,128]{3,2,1,0:T(8,128)(2,1)S(1)}, u32[]{:S(2)}) copy-start(bf16[8,4,80,128]{3,2,1,0:T(8,128)(2,1)S(1)} %all-to-all-done.1.near) | copy-start | bytes 1966084
  73.2 20.2 %collective-permute-start.8 = (bf16[8,4,80,128]{3,2,1,0:T(8,128)(2,1)S(1)}, bf16[8,4,80,128]{3,2,1,0:T(8,128)(2,1)}, u32[]{:S(2)}, u32[]{:S(2)}) collective-permute-start(bf16[8,4,80,128]{3,2,1,0:T(8,128)(2,1)S(1)} %all-to-all-done.1.near), channel_id=1, source_target_pairs={{0,480},{32,64},{64,32},{96,128},{128,96},{160,192},{192,160},{224... | collective-permute-start | bytes 1966088 | tf_op jit(solution)/shard_map/ppermute | solution.py:329
  78.2 3.7 %collective-permute-start.4 = (bf16[128,1536]{1,0:T(8,128)(2,1)S(1)}, bf16[128,1536]{1,0:T(8,128)(2,1)}, u32[]{:S(2)}, u32[]{:S(2)}) collective-permute-start(bf16[128,1536]{1,0:T(8,128)(2,1)S(1)} %collective-permute-done.z_half), channel_id=1, source_target_pairs={{0,1},{1,0},{2,3},{3,2},{4,5},{5,4},{6,7},{7,6},{8,9},{9,8},{10,11... | collective-permute-start | bytes 1179656 | tf_op jit(solution)/shard_map/ppermute | solution.py:294
  117.0 22.2 %copy-start.5 = (f32[384]{0:T(512)S(1)}, f32[384]{0:T(512)}, u32[]{:S(2)}) copy-start(f32[384]{0:T(512)} %param.21) | copy-start | bytes 4612
  117.0 9.9 %all-to-all-start.2 = ((f32[8,64,128]{2,1,0:T(8,128)}), f32[8,64,128]{2,1,0:T(8,128)S(1)}, u32[]{:S(2)}, u32[]{:S(2)}) async-start(f32[8,64,128]{2,1,0:T(8,128)} %clip_head.1), calls=%async_computation.2 | async-start | bytes 524288 | tf_op jit(solution)/shard_map/all_to_all | solution.py:338
  127.7 11.5 %all-to-all-start.3 = ((f32[8,2,128]{2,1,0:T(2,128)}), f32[8,2,128]{2,1,0:T(2,128)S(1)}, u32[]{:S(2)}, u32[]{:S(2)}) async-start(f32[8,2,128]{2,1,0:T(2,128)} %broadcast_in_dim.5), calls=%async_computation.3 | async-start | bytes 16384 | tf_op jit(solution)/shard_map/all_to_all | solution.py:347

commit v4 on v3

--- a/solution.py
+++ b/solution.py
@@ -15,7 +15,6 @@
 CLIP = 1024
 STEPS = CLIP // MB
 HEADS_DEV = 6
-SHIFTS = (1, -1, 2)
 ROWS = 80
 C1 = 0.7978845608028654
 C2 = 0.044715 * C1
@@ -78,10 +77,12 @@
     r_half,
     l_half,
     f_half,
+    g_half,
     z_sibling,
     r_sibling,
     l_sibling,
     f_sibling,
+    g_sibling,
     near,
     other,
     A0_hbm,
@@ -134,13 +135,15 @@
     copies = [
         pltpu.make_async_copy(own, T.at[pl.ds(row, TOK), :], row_sem.at[zi * 4 + x]),
     ]
-    halves = (z_half, r_half, l_half, f_half)
-    siblings = (z_sibling, r_sibling, l_sibling, f_sibling)
-    for (across, *pairs), part in ((halves, core), (siblings, 1 - core)):
+    halves = (z_half, r_half, l_half, f_half, g_half)
+    siblings = (z_sibling, r_sibling, l_sibling, f_sibling, g_sibling)
+    for (across, right, left, far_own, far_across), part in ((halves, core), (siblings, 1 - core)):
         copies.append(place(across, 1 - zi, x, part))
-        for by, pair in zip(SHIFTS, pairs):
+        for by, pair in ((1, right), (-1, left)):
             copies.append(place(pair.at[0:TOK], zi, x - by, part))
             copies.append(place(pair.at[TOK : 2 * TOK], 1 - zi, x - by, part))
+        copies.append(place(far_own, zi, x + 2, part))
+        copies.append(place(far_across, 1 - zi, x + 2, part))
     small = [
         pltpu.make_async_copy(A0_hbm.at[head], A0, sem.at[0]),
         pltpu.make_async_copy(B0_hbm.at[head], B0, sem.at[0]),
@@ -294,10 +297,6 @@
     return lax.ppermute(x, axis, [(i, (i + by) % size) for i in range(size)])
 
 
-def to_workers(x, by):
-    return lax.ppermute(x, "x", [(i, (i + by) % 4) for i in range(4) if (i + by) % 4 < 3])
-
-
 def local(
     tokens,
     w_qkv,
@@ -325,9 +324,10 @@
     swap = [(i, (i + 1) % 16 if i % 2 else (i - 1) % 16) for i in range(16)]
 
     pair = jnp.concatenate([mine, across], 0)
-    parts = [to_workers(pair, by) for by in SHIFTS]
+    right, left = ring(pair, "x", 1), ring(pair, "x", -1)
+    far_own, far_across = ring(right[:TOK], "x", 1), ring(left[TOK:], "x", -1)
     other = lax.ppermute(near, ("zc", "zi"), swap)
-    parts = [across] + parts
+    parts = [across, right, left, far_own, far_across]
     pieces = [tokens] + parts + [ring(part, "core", 1) for part in parts]
 
     head = 2 * x + (zi + odd) % 2

time: 141 us -> 133 us (0.943)
  waiting for transfers between devices: 51.8 us -> 33 us
  starting transfers between devices: 58.5 us -> 68.1 us
  local copies, waits for them, and re-layouts: 3.36 us -> 5.06 us
    ppermute x3 -> x0, waiting for transfers between devices: 23.7 us -> none  [to_workers(): lax.ppermute(x, 'x', [(i, (i + by) % 4) for i in range(4) if (i + by) % 4...]
    ppermute x5 -> x10, starting transfers between devices: 16.4 us -> 33.1 us  [ring(): return lax.ppermute(x, axis, [(i, (i + by) % size) for i in range(size)])]
    ppermute x3 -> x0, starting transfers between devices: 8.46 us -> none  [to_workers(): lax.ppermute(x, 'x', [(i, (i + by) % 4) for i in range(4) if (i + by) % 4...]
    ppermute x5 -> x10, waiting for transfers between devices: 0.91 us -> 9.21 us  [ring(): return lax.ppermute(x, axis, [(i, (i + by) % size) for i in range(size)])]
    ppermute x1, waiting for transfers between devices: 11.4 us -> 8.07 us  [local(): other = lax.ppermute(near, ('zc', 'zi'), swap)]
    slice x0 -> x2, local copies, waits for them, and re-layouts: none -> 1.67 us  [local(): far_own, far_across = (ring(right[:TOK], 'x', 1), ring(left[TOK:], 'x', -1))]
  transfers between devices with their start and end apart: 13 -> 15, of which waited for: 7 -> 6; matrix products, arithmetic and copies ran while one was open for 0% -> 2% of each run, Pallas kernels for 1% -> 1%
where the time goes in v4:
time: 133 us
  starting transfers between devices  68.1 us (51%)
  waiting for transfers between devices  33 us (25%)
  Pallas kernels  25.3 us (19%)
  local copies, waits for them, and re-layouts  5.06 us (4%)
    ppermute x10, starting transfers between devices, ring(): return lax.ppermute(x, axis, [(i, (i + by) % size) for i in range(size)])  33.1 us
    pallas_call x1, Pallas kernels, chain(): pl.pallas_call(chain_kernel, out_shape=jax.ShapeDtypeStruct((8, HD, TOK),...  23.6 us
    all_to_all x1, starting transfers between devices, local(): lax.all_to_all(blocks.reshape(8, 4, ROWS, 128), 'zc', 0, 0, tiled=True)  13.9 us
    ppermute x10, waiting for transfers between devices, ring(): return lax.ppermute(x, axis, [(i, (i + by) % size) for i in range(size)])  9.21 us
    ppermute x1, waiting for transfers between devices, local(): other = lax.ppermute(near, ('zc', 'zi'), swap)  8.07 us
    all_to_all x1, starting transfers between devices, local(): stats = lax.all_to_all(stats, ('y', 'core'), 0, 0, tiled=True)  7.54 us
    all_to_all x1, waiting for transfers between devices, local(): got = lax.all_to_all(outs, ('zi', 'x'), 0, 0, tiled=True)  6.08 us
    ppermute x1, starting transfers between devices, local(): other = lax.ppermute(near, ('zc', 'zi'), swap)  5.04 us
  transfers between devices with their start and end apart: 15, of which 6 were waited for; matrix products, arithmetic and copies ran while one was open for 2% of the time, Pallas kernels for 1%

profile of v4, /device:TPU:1, one launch (start us, length us, event | category | flops | bytes accessed | tf_op | source)
XLA Modules:
  0.0 132.7 jit_solution(12722382353105421614)
XLA Ops:
  0.0 1.0 constant_dynamic-slice_fusion
  1.0 4.4 %collective-permute-start = (bf16[128,1536]{1,0:T(8,128)(2,1)S(1)}, bf16[128,1536]{1,0:T(8,128)(2,1)S(1)}, u32[]{:S(2)}, u32[]{:S(2)}) collective-permute-start(bf16[128,1536]{1,0:T(8,128)(2,1)S(1)} %constant_dynamic-slice_fusion), channel_id=1, source_target_pairs={{0,32},{32,0},{1,33},{33,1},{2,34},{34,2},{3,35},{35,3},{4,36},{36... | collective-permute-start | bytes 1179656 | tf_op jit(solution)/shard_map/ppermute | solution.py:297
  5.4 1.7 %pack_weights.1 = bf16[4,2,80,128]{3,2,1,0:T(8,128)(2,1)} custom-call(bf16[3,48,384]{2,1,0:T(8,128)(2,1)} %bitcast.34, bf16[6,48]{1,0:T(8,128)(2,1)} %bitcast.38), custom_call_target="tpu_custom_call" | custom-call | tf_op jit(solution)/shard_map/pack_weights/pallas_call | solution.py:65
  7.1 4.0 %all-to-all-start = ((bf16[4,2,80,128]{3,2,1,0:T(8,128)(2,1)}), bf16[4,2,80,128]{3,2,1,0:T(8,128)(2,1)S(1)}, u32[]{:S(2)}, u32[]{:S(2)}) async-start(bf16[4,2,80,128]{3,2,1,0:T(8,128)(2,1)} %pack_weights.1), calls=%async_computation | async-start | bytes 327680 | tf_op jit(solution)/shard_map/all_to_all | solution.py:316
  11.1 5.0 %all-to-all-done = bf16[4,2,80,128]{3,2,1,0:T(8,128)(2,1)S(1)} async-done(((bf16[4,2,80,128]{3,2,1,0:T(8,128)(2,1)}), bf16[4,2,80,128]{3,2,1,0:T(8,128)(2,1)S(1)}, u32[]{:S(2)}, u32[]{:S(2)}) %all-to-all-start) | async-done | bytes 163872 | tf_op jit(solution)/shard_map/all_to_all | solution.py:316
  16.1 0.0 collective-permute-done.z_half
  16.2 1.0 broadcast_in_dim.4
  17.1 13.9 %all-to-all-start.1 = ((bf16[8,4,80,128]{3,2,1,0:T(8,128)(2,1)}), bf16[8,4,80,128]{3,2,1,0:T(8,128)(2,1)S(1)}, u32[]{:S(2)}, u32[]{:S(2)}) async-start(bf16[8,4,80,128]{3,2,1,0:T(8,128)(2,1)} %bitcast.8), calls=%async_computation.1 | async-start | bytes 1310720 | tf_op jit(solution)/shard_map/all_to_all | solution.py:323
  31.0 0.1 pad_maximum_fusion
  31.1 2.9 %collective-permute-start.2 = (bf16[256,1536]{1,0:T(8,128)(2,1)S(1)}, bf16[256,1536]{1,0:T(8,128)(2,1)S(1)}, u32[]{:S(2)}, u32[]{:S(2)}) collective-permute-start(bf16[256,1536]{1,0:T(8,128)(2,1)S(1)} %pad_maximum_fusion), channel_id=1, source_target_pairs={{0,24},{8,0},{16,8},{24,16},{1,25},{9,1},{17,9},{25,17},{2,26},{10... | collective-permute-start | bytes 2359304 | tf_op jit(solution)/shard_map/ppermute | solution.py:297
  34.0 2.4 %collective-permute-start.1 = (bf16[256,1536]{1,0:T(8,128)(2,1)S(1)}, bf16[256,1536]{1,0:T(8,128)(2,1)S(1)}, u32[]{:S(2)}, u32[]{:S(2)}) collective-permute-start(bf16[256,1536]{1,0:T(8,128)(2,1)S(1)} %pad_maximum_fusion), channel_id=1, source_target_pairs={{0,8},{8,16},{16,24},{24,0},{1,9},{9,17},{17,25},{25,1},{2,10},{10... | collective-permute-start | bytes 2359304 | tf_op jit(solution)/shard_map/ppermute | solution.py:297
  36.4 0.0 copy-done.3
  36.4 5.1 %collective-permute-start.5 = (bf16[128,1536]{1,0:T(8,128)(2,1)S(1)}, bf16[128,1536]{1,0:T(8,128)(2,1)}, u32[]{:S(2)}, u32[]{:S(2)}) collective-permute-start(bf16[128,1536]{1,0:T(8,128)(2,1)S(1)} %collective-permute-done.z_half), channel_id=1, source_target_pairs={{0,1},{1,0},{2,3},{3,2},{4,5},{5,4},{6,7},{7,6},{8,9},{9,8},{10,11... | collective-permute-start | bytes 1179656 | tf_op jit(solution)/shard_map/ppermute | solution.py:297
  41.5 7.8 %collective-permute-done.2.l_half = bf16[256,1536]{1,0:T(8,128)(2,1)S(1)} collective-permute-done((bf16[256,1536]{1,0:T(8,128)(2,1)S(1)}, bf16[256,1536]{1,0:T(8,128)(2,1)S(1)}, u32[]{:S(2)}, u32[]{:S(2)}) %collective-permute-start.2) | collective-permute-done | bytes 786464 | tf_op jit(solution)/shard_map/ppermute | solution.py:297
  49.3 0.8 slice.26
  50.2 4.2 %collective-permute-start.4 = (bf16[128,1536]{1,0:T(8,128)(2,1)}, bf16[128,1536]{1,0:T(8,128)(2,1)}, u32[]{:S(2)}, u32[]{:S(2)}) collective-permute-start(bf16[128,1536]{1,0:T(8,128)(2,1)} %slice.26), channel_id=1, source_target_pairs={{0,24},{8,0},{16,8},{24,16},{1,25},{9,1},{17,9},{25,17},{2,26},{10... | collective-permute-start | bytes 1179656 | tf_op jit(solution)/shard_map/ppermute | solution.py:297
  54.4 0.0 collective-permute-done.1.r_half
  54.4 0.0 copy-start.2
  54.4 0.8 slice.25
  55.3 1.9 %collective-permute-start.3 = (bf16[128,1536]{1,0:T(8,128)(2,1)}, bf16[128,1536]{1,0:T(8,128)(2,1)}, u32[]{:S(2)}, u32[]{:S(2)}) collective-permute-start(bf16[128,1536]{1,0:T(8,128)(2,1)} %slice.25), channel_id=1, source_target_pairs={{0,8},{8,16},{16,24},{24,0},{1,9},{9,17},{17,25},{25,1},{2,10},{10... | collective-permute-start | bytes 1179656 | tf_op jit(solution)/shard_map/ppermute | solution.py:297
  57.2 0.0 copy-done.1
  57.2 5.7 %collective-permute-start.7 = (bf16[256,1536]{1,0:T(8,128)(2,1)S(1)}, bf16[256,1536]{1,0:T(8,128)(2,1)S(1)}, u32[]{:S(2)}, u32[]{:S(2)}) collective-permute-start(bf16[256,1536]{1,0:T(8,128)(2,1)S(1)} %collective-permute-done.2.l_half), channel_id=1, source_target_pairs={{0,1},{1,0},{2,3},{3,2},{4,5},{5,4},{6,7},{7,6},{8,9},{9,8},{10,11... | collective-permute-start | bytes 2359304 | tf_op jit(solution)/shard_map/ppermute | solution.py:297
  62.9 1.9 %collective-permute-start.6 = (bf16[256,1536]{1,0:T(8,128)(2,1)S(1)}, bf16[256,1536]{1,0:T(8,128)(2,1)}, u32[]{:S(2)}, u32[]{:S(2)}) collective-permute-start(bf16[256,1536]{1,0:T(8,128)(2,1)S(1)} %collective-permute-done.1.r_half), channel_id=1, source_target_pairs={{0,1},{1,0},{2,3},{3,2},{4,5},{5,4},{6,7},{7,6},{8,9},{9,8},{10,11... | collective-permute-start | bytes 2359304 | tf_op jit(solution)/shard_map/ppermute | solution.py:297
  64.8 0.0 collective-permute-done.5.z_sibling
  64.8 0.0 all-to-all-done.1.near
  64.8 5.0 %collective-permute-start.10 = (bf16[8,4,80,128]{3,2,1,0:T(8,128)(2,1)S(1)}, bf16[8,4,80,128]{3,2,1,0:T(8,128)(2,1)}, u32[]{:S(2)}, u32[]{:S(2)}) collective-permute-start(bf16[8,4,80,128]{3,2,1,0:T(8,128)(2,1)S(1)} %all-to-all-done.1.near), channel_id=1, source_target_pairs={{0,480},{32,64},{64,32},{96,128},{128,96},{160,192},{192,160},{224... | collective-permute-start | bytes 1966088 | tf_op jit(solution)/shard_map/ppermute | solution.py:329
  69.9 0.0 collective-permute-done.4.g_half
  69.9 2.7 %collective-permute-start.9 = (bf16[128,1536]{1,0:T(8,128)(2,1)}, bf16[128,1536]{1,0:T(8,128)(2,1)S(1)}, u32[]{:S(2)}, u32[]{:S(2)}) collective-permute-start(bf16[128,1536]{1,0:T(8,128)(2,1)} %collective-permute-done.4.g_half), channel_id=1, source_target_pairs={{0,1},{1,0},{2,3},{3,2},{4,5},{5,4},{6,7},{7,6},{8,9},{9,8},{10,11... | collective-permute-start | bytes 1179656 | tf_op jit(solution)/shard_map/ppermute | solution.py:297
  72.6 0.0 collective-permute-done.3.f_half
  72.6 1.9 %collective-permute-start.8 = (bf16[128,1536]{1,0:T(8,128)(2,1)}, bf16[128,1536]{1,0:T(8,128)(2,1)}, u32[]{:S(2)}, u32[]{:S(2)}) collective-permute-start(bf16[128,1536]{1,0:T(8,128)(2,1)} %collective-permute-done.3.f_half), channel_id=1, source_target_pairs={{0,1},{1,0},{2,3},{3,2},{4,5},{5,4},{6,7},{7,6},{8,9},{9,8},{10,11... | collective-permute-start | bytes 1179656 | tf_op jit(solution)/shard_map/ppermute | solution.py:297
  74.5 0.6 pad_add_fusion.idx
  75.1 0.0 collective-permute-done.9.g_sibling
  75.1 0.0 collective-permute-done.7.l_sibling
  75.2 1.4 %collective-permute-done.8.f_sibling = bf16[128,1536]{1,0:T(8,128)(2,1)} collective-permute-done((bf16[128,1536]{1,0:T(8,128)(2,1)}, bf16[128,1536]{1,0:T(8,128)(2,1)}, u32[]{:S(2)}, u32[]{:S(2)}) %collective-permute-start.8) | collective-permute-done | bytes 393248 | tf_op jit(solution)/shard_map/ppermute | solution.py:297
  76.5 0.0 collective-permute-done.6.r_sibling
  76.5 8.1 %collective-permute-done.10.other = bf16[8,4,80,128]{3,2,1,0:T(8,128)(2,1)} collective-permute-done((bf16[8,4,80,128]{3,2,1,0:T(8,128)(2,1)S(1)}, bf16[8,4,80,128]{3,2,1,0:T(8,128)(2,1)}, u32[]{:S(2)}, u32[]{:S(2)}) %collective-permute-start.10) | collective-permute-done | bytes 655392 | tf_op jit(solution)/shard_map/ppermute | solution.py:329
  84.6 0.0 copy-done
  84.6 23.6 %clip_head.1 = f32[8,64,128]{2,1,0:T(8,128)} custom-call(s32[4]{0:T(128)} %pad_add_fusion.idx, f32[6]{0:T(128)} %rate0.1, bf16[128,3072]{1,0:T(8,128)(2,1)} %own.1, bf16[128,1536]{1,0:T(8,128)(2,1)} %copy-done.3, bf16[256,1536]{1,0:T(8,128)(2,1)} %copy-done.2, bf16[256,1536]{1,0:T(8,128)(2,1)} %copy-done.1, bf16[128,1536]{1,0:T(8,128)(2,1)} %collective-permute-done.3.f_half, ...), custom_call_target="tpu_custom_call" | custom-call | tf_op jit(solution)/shard_map/clip_head/pallas_call | solution.py:262
  108.3 0.0 copy-start.6
  108.3 4.5 %all-to-all-start.2 = ((f32[8,64,128]{2,1,0:T(8,128)}), f32[8,64,128]{2,1,0:T(8,128)S(1)}, u32[]{:S(2)}, u32[]{:S(2)}) async-start(f32[8,64,128]{2,1,0:T(8,128)} %clip_head.1), calls=%async_computation.2 | async-start | bytes 524288 | tf_op jit(solution)/shard_map/all_to_all | solution.py:338
  112.7 6.1 %all-to-all-done.2 = f32[8,64,128]{2,1,0:T(8,128)S(1)} async-done(((f32[8,64,128]{2,1,0:T(8,128)}), f32[8,64,128]{2,1,0:T(8,128)S(1)}, u32[]{:S(2)}, u32[]{:S(2)}) %all-to-all-start.2) | async-done | bytes 262176 | tf_op jit(solution)/shard_map/all_to_all | solution.py:338
  118.9 0.1 multiply_reduce_fusion
  119.0 0.6 broadcast_in_dim.5
  119.6 7.5 %all-to-all-start.3 = ((f32[8,2,128]{2,1,0:T(2,128)}), f32[8,2,128]{2,1,0:T(2,128)S(1)}, u32[]{:S(2)}, u32[]{:S(2)}) async-start(f32[8,2,128]{2,1,0:T(2,128)} %broadcast_in_dim.5), calls=%async_computation.3 | async-start | bytes 16384 | tf_op jit(solution)/shard_map/all_to_all | solution.py:347
  127.1 4.6 %all-to-all-done.3 = f32[8,2,128]{2,1,0:T(2,128)S(1)} async-done(((f32[8,2,128]{2,1,0:T(2,128)}), f32[8,2,128]{2,1,0:T(2,128)S(1)}, u32[]{:S(2)}, u32[]{:S(2)}) %all-to-all-start.3) | async-done | bytes 8224 | tf_op jit(solution)/shard_map/all_to_all | solution.py:347
  131.8 0.0 copy-done.6
  131.8 0.1 fusion.2
  131.9 0.8 copy.20
  (19 shorter events, 0.2 us)
Async XLA Ops:
  1.0 15.1 %collective-permute-start = (bf16[128,1536]{1,0:T(8,128)(2,1)S(1)}, bf16[128,1536]{1,0:T(8,128)(2,1)S(1)}, u32[]{:S(2)}, u32[]{:S(2)}) collective-permute-start(bf16[128,1536]{1,0:T(8,128)(2,1)S(1)} %constant_dynamic-slice_fusion), channel_id=1, source_target_pairs={{0,32},{32,0},{1,33},{33,1},{2,34},{34,2},{3,35},{35,3},{4,36},{36... | collective-permute-start | bytes 1179656 | tf_op jit(solution)/shard_map/ppermute | solution.py:297
  7.1 9.0 %all-to-all-start = ((bf16[4,2,80,128]{3,2,1,0:T(8,128)(2,1)}), bf16[4,2,80,128]{3,2,1,0:T(8,128)(2,1)S(1)}, u32[]{:S(2)}, u32[]{:S(2)}) async-start(bf16[4,2,80,128]{3,2,1,0:T(8,128)(2,1)} %pack_weights.1), calls=%async_computation | async-start | bytes 327680 | tf_op jit(solution)/shard_map/all_to_all | solution.py:316
  16.1 20.3 %copy-start.3 = (bf16[128,1536]{1,0:T(8,128)(2,1)}, bf16[128,1536]{1,0:T(8,128)(2,1)S(1)}, u32[]{:S(2)}) copy-start(bf16[128,1536]{1,0:T(8,128)(2,1)S(1)} %collective-permute-done.z_half) | copy-start | bytes 1179652
  17.1 47.7 %all-to-all-start.1 = ((bf16[8,4,80,128]{3,2,1,0:T(8,128)(2,1)}), bf16[8,4,80,128]{3,2,1,0:T(8,128)(2,1)S(1)}, u32[]{:S(2)}, u32[]{:S(2)}) async-start(bf16[8,4,80,128]{3,2,1,0:T(8,128)(2,1)} %bitcast.8), calls=%async_computation.1 | async-start | bytes 1310720 | tf_op jit(solution)/shard_map/all_to_all | solution.py:323
  31.1 18.3 %collective-permute-start.2 = (bf16[256,1536]{1,0:T(8,128)(2,1)S(1)}, bf16[256,1536]{1,0:T(8,128)(2,1)S(1)}, u32[]{:S(2)}, u32[]{:S(2)}) collective-permute-start(bf16[256,1536]{1,0:T(8,128)(2,1)S(1)} %pad_maximum_fusion), channel_id=1, source_target_pairs={{0,24},{8,0},{16,8},{24,16},{1,25},{9,1},{17,9},{25,17},{2,26},{10... | collective-permute-start | bytes 2359304 | tf_op jit(solution)/shard_map/ppermute | solution.py:297
  34.0 20.4 %collective-permute-start.1 = (bf16[256,1536]{1,0:T(8,128)(2,1)S(1)}, bf16[256,1536]{1,0:T(8,128)(2,1)S(1)}, u32[]{:S(2)}, u32[]{:S(2)}) collective-permute-start(bf16[256,1536]{1,0:T(8,128)(2,1)S(1)} %pad_maximum_fusion), channel_id=1, source_target_pairs={{0,8},{8,16},{16,24},{24,0},{1,9},{9,17},{17,25},{25,1},{2,10},{10... | collective-permute-start | bytes 2359304 | tf_op jit(solution)/shard_map/ppermute | solution.py:297
  36.4 28.4 %collective-permute-start.5 = (bf16[128,1536]{1,0:T(8,128)(2,1)S(1)}, bf16[128,1536]{1,0:T(8,128)(2,1)}, u32[]{:S(2)}, u32[]{:S(2)}) collective-permute-start(bf16[128,1536]{1,0:T(8,128)(2,1)S(1)} %collective-permute-done.z_half), channel_id=1, source_target_pairs={{0,1},{1,0},{2,3},{3,2},{4,5},{5,4},{6,7},{7,6},{8,9},{9,8},{10,11... | collective-permute-start | bytes 1179656 | tf_op jit(solution)/shard_map/ppermute | solution.py:297
  49.3 7.8 %copy-start.1 = (bf16[256,1536]{1,0:T(8,128)(2,1)}, bf16[256,1536]{1,0:T(8,128)(2,1)S(1)}, u32[]{:S(2)}) copy-start(bf16[256,1536]{1,0:T(8,128)(2,1)S(1)} %collective-permute-done.2.l_half) | copy-start | bytes 2359300
  50.2 19.7 %collective-permute-start.4 = (bf16[128,1536]{1,0:T(8,128)(2,1)}, bf16[128,1536]{1,0:T(8,128)(2,1)}, u32[]{:S(2)}, u32[]{:S(2)}) collective-permute-start(bf16[128,1536]{1,0:T(8,128)(2,1)} %slice.26), channel_id=1, source_target_pairs={{0,24},{8,0},{16,8},{24,16},{1,25},{9,1},{17,9},{25,17},{2,26},{10... | collective-permute-start | bytes 1179656 | tf_op jit(solution)/shard_map/ppermute | solution.py:297
  54.4 30.2 %copy-start.2 = (bf16[256,1536]{1,0:T(8,128)(2,1)}, bf16[256,1536]{1,0:T(8,128)(2,1)S(1)}, u32[]{:S(2)}) copy-start(bf16[256,1536]{1,0:T(8,128)(2,1)S(1)} %collective-permute-done.1.r_half) | copy-start | bytes 2359300
  55.3 17.3 %collective-permute-start.3 = (bf16[128,1536]{1,0:T(8,128)(2,1)}, bf16[128,1536]{1,0:T(8,128)(2,1)}, u32[]{:S(2)}, u32[]{:S(2)}) collective-permute-start(bf16[128,1536]{1,0:T(8,128)(2,1)} %slice.25), channel_id=1, source_target_pairs={{0,8},{8,16},{16,24},{24,0},{1,9},{9,17},{17,25},{25,1},{2,10},{10... | collective-permute-start | bytes 1179656 | tf_op jit(solution)/shard_map/ppermute | solution.py:297
  57.2 18.0 %collective-permute-start.7 = (bf16[256,1536]{1,0:T(8,128)(2,1)S(1)}, bf16[256,1536]{1,0:T(8,128)(2,1)S(1)}, u32[]{:S(2)}, u32[]{:S(2)}) collective-permute-start(bf16[256,1536]{1,0:T(8,128)(2,1)S(1)} %collective-permute-done.2.l_half), channel_id=1, source_target_pairs={{0,1},{1,0},{2,3},{3,2},{4,5},{5,4},{6,7},{7,6},{8,9},{9,8},{10,11... | collective-permute-start | bytes 2359304 | tf_op jit(solution)/shard_map/ppermute | solution.py:297
  62.9 13.7 %collective-permute-start.6 = (bf16[256,1536]{1,0:T(8,128)(2,1)S(1)}, bf16[256,1536]{1,0:T(8,128)(2,1)}, u32[]{:S(2)}, u32[]{:S(2)}) collective-permute-start(bf16[256,1536]{1,0:T(8,128)(2,1)S(1)} %collective-permute-done.1.r_half), channel_id=1, source_target_pairs={{0,1},{1,0},{2,3},{3,2},{4,5},{5,4},{6,7},{7,6},{8,9},{9,8},{10,11... | collective-permute-start | bytes 2359304 | tf_op jit(solution)/shard_map/ppermute | solution.py:297
  64.8 19.8 %copy-start = (bf16[8,4,80,128]{3,2,1,0:T(8,128)(2,1)}, bf16[8,4,80,128]{3,2,1,0:T(8,128)(2,1)S(1)}, u32[]{:S(2)}) copy-start(bf16[8,4,80,128]{3,2,1,0:T(8,128)(2,1)S(1)} %all-to-all-done.1.near) | copy-start | bytes 1966084
  64.8 19.8 %collective-permute-start.10 = (bf16[8,4,80,128]{3,2,1,0:T(8,128)(2,1)S(1)}, bf16[8,4,80,128]{3,2,1,0:T(8,128)(2,1)}, u32[]{:S(2)}, u32[]{:S(2)}) collective-permute-start(bf16[8,4,80,128]{3,2,1,0:T(8,128)(2,1)S(1)} %all-to-all-done.1.near), channel_id=1, source_target_pairs={{0,480},{32,64},{64,32},{96,128},{128,96},{160,192},{192,160},{224... | collective-permute-start | bytes 1966088 | tf_op jit(solution)/shard_map/ppermute | solution.py:329
  69.9 5.3 %collective-permute-start.9 = (bf16[128,1536]{1,0:T(8,128)(2,1)}, bf16[128,1536]{1,0:T(8,128)(2,1)S(1)}, u32[]{:S(2)}, u32[]{:S(2)}) collective-permute-start(bf16[128,1536]{1,0:T(8,128)(2,1)} %collective-permute-done.4.g_half), channel_id=1, source_target_pairs={{0,1},{1,0},{2,3},{3,2},{4,5},{5,4},{6,7},{7,6},{8,9},{9,8},{10,11... | collective-permute-start | bytes 1179656 | tf_op jit(solution)/shard_map/ppermute | solution.py:297
  72.6 4.0 %collective-permute-start.8 = (bf16[128,1536]{1,0:T(8,128)(2,1)}, bf16[128,1536]{1,0:T(8,128)(2,1)}, u32[]{:S(2)}, u32[]{:S(2)}) collective-permute-start(bf16[128,1536]{1,0:T(8,128)(2,1)} %collective-permute-done.3.f_half), channel_id=1, source_target_pairs={{0,1},{1,0},{2,3},{3,2},{4,5},{5,4},{6,7},{7,6},{8,9},{9,8},{10,11... | collective-permute-start | bytes 1179656 | tf_op jit(solution)/shard_map/ppermute | solution.py:297
  75.1 9.5 %copy-start.5 = (bf16[128,1536]{1,0:T(8,128)(2,1)}, bf16[128,1536]{1,0:T(8,128)(2,1)S(1)}, u32[]{:S(2)}) copy-start(bf16[128,1536]{1,0:T(8,128)(2,1)S(1)} %collective-permute-done.9.g_sibling) | copy-start | bytes 1179652
  75.1 9.5 %copy-start.4 = (bf16[256,1536]{1,0:T(8,128)(2,1)}, bf16[256,1536]{1,0:T(8,128)(2,1)S(1)}, u32[]{:S(2)}) copy-start(bf16[256,1536]{1,0:T(8,128)(2,1)S(1)} %collective-permute-done.7.l_sibling) | copy-start | bytes 2359300
  108.3 23.5 %copy-start.6 = (f32[384]{0:T(512)S(1)}, f32[384]{0:T(512)}, u32[]{:S(2)}) copy-start(f32[384]{0:T(512)} %param.21) | copy-start | bytes 4612
  108.3 10.5 %all-to-all-start.2 = ((f32[8,64,128]{2,1,0:T(8,128)}), f32[8,64,128]{2,1,0:T(8,128)S(1)}, u32[]{:S(2)}, u32[]{:S(2)}) async-start(f32[8,64,128]{2,1,0:T(8,128)} %clip_head.1), calls=%async_computation.2 | async-start | bytes 524288 | tf_op jit(solution)/shard_map/all_to_all | solution.py:338
  119.6 12.2 %all-to-all-start.3 = ((f32[8,2,128]{2,1,0:T(2,128)}), f32[8,2,128]{2,1,0:T(2,128)S(1)}, u32[]{:S(2)}, u32[]{:S(2)}) async-start(f32[8,2,128]{2,1,0:T(2,128)} %broadcast_in_dim.5), calls=%async_computation.3 | async-start | bytes 16384 | tf_op jit(solution)/shard_map/all_to_all | solution.py:347

commit v5 on v4

--- a/solution.py
+++ b/solution.py
@@ -16,6 +16,7 @@
 STEPS = CLIP // MB
 HEADS_DEV = 6
 ROWS = 80
+SLAB = 304
 C1 = 0.7978845608028654
 C2 = 0.044715 * C1
 bf16 = jnp.bfloat16
@@ -52,11 +53,10 @@
         k = w_ref[1, :, cols].astype(f32)
         v = w_ref[2, :, cols].astype(f32)
         gate = wr_ref[head : head + 1, :].astype(f32)
-        gate = jnp.concatenate([gate, jnp.zeros((1, 16), f32)], 1)
-        gate = jnp.broadcast_to(gate, (16, HD))
-        right = jnp.concatenate([q[32:48], gate], 0)
+        gate = jnp.concatenate([gate, jnp.zeros((1, 80), f32)], 1)
+        queries = jnp.concatenate([q[:24], q[24:]], 1)
         block = jnp.concatenate(
-            [jnp.concatenate([k, v], 1), jnp.concatenate([q[:32], right], 1)], 0
+            [jnp.concatenate([k, v], 1), queries, jnp.broadcast_to(gate, (8, 128))], 0
         )
         out_ref[p % 4, p // 4] = block.astype(bf16)
 
@@ -156,18 +156,20 @@
         c.start()
     for c in heavy:
         c.wait()
-    WA[:, 0:128] = W[:, :, :, 0:48, :].reshape(D, 128)
-    X = W[:, :, :, 48:80, :].reshape(64, 32, 128)
-    lane = lax.broadcasted_iota(jnp.int32, (1, 16, 128), 2)
-    sub = lax.broadcasted_iota(jnp.int32, (1, 16, 128), 1)
-    gate = X[:, 16:32, :].astype(f32)
-    gates = jnp.concatenate(
-        [jnp.where(lane == sub + (64 + 16 * j), gate, 0.0) for j in range(3)], 1
-    )
-    gates = mm(gates.astype(bf16).reshape(D, 128), jnp.ones((128, 128), bf16))
-    qa = X[:, 0:16, :].astype(f32)
-    qb = jnp.concatenate([qa[:, :, 64:], qa[:, :, :64]], 2)
-    qs = jnp.concatenate([X.astype(f32), qb], 1).reshape(D, 128)
+    blocks = W[...].reshape(16, SLAB, 128)
+    WA[:, 0:128] = blocks[:, 0:192, :].reshape(D, 128)
+    X = blocks[:, 192:288, :].astype(f32)
+    G = blocks[:, 288:304, :].astype(f32)
+    lane = lax.broadcasted_iota(jnp.int32, (1, 48, 128), 2)
+    sub = lax.broadcasted_iota(jnp.int32, (1, 48, 128), 1)
+    gates, qs = [], []
+    for i in range(4):
+        gates.append(jnp.where(lane == sub, G[:, 4 * i : 4 * i + 1, :], 0.0))
+        q = X[:, 24 * i : 24 * i + 24, :]
+        qs += [q, jnp.concatenate([q[:, :, 64:], q[:, :, :64]], 2)]
+    gates = jnp.concatenate(gates, 1).astype(bf16).reshape(D, 128)
+    gates = mm(gates, jnp.ones((128, 128), bf16))
+    qs = jnp.concatenate(qs, 1).reshape(D, 128)
     wide = lax.broadcasted_iota(jnp.int32, (1, 128), 1)
     WA[:, 128:256] = jnp.where(wide < 64, qs, gates).astype(bf16)
     for c in small:
@@ -212,9 +214,9 @@
 
     def step(t, carry):
         b_col, b_row = carry
-        now = pl.ds(pl.multiple_of(t * MB, MB), MB)
-        nxt = pl.ds(pl.multiple_of(jnp.minimum(t + 1, STEPS - 1) * MB, MB), MB)
-        old = pl.ds(pl.multiple_of(jnp.maximum(t - 1, 0) * MB, MB), MB)
+        now = pl.ds(t * MB, MB)
+        nxt = pl.ds(min(t + 1, STEPS - 1) * MB, MB)
+        old = pl.ds(max(t - 1, 0) * MB, MB)
         k = KV[now, 0:HD]
         v = KV[now, HD : 2 * HD]
         kn = KV[nxt, 0:HD]
@@ -234,9 +236,11 @@
         dmb = dm.astype(bf16)
         dh = mm(dmb, Bv, TN) * slope
         dhb = dh.astype(bf16)
-        gram = (mm(kn, k, NT) + 1.0).astype(bf16)
-        hk[...] = mm(kn, Av) + av - mm(gram, dhb)
-        answer(old, qp, gelu(mm(qp, Av) + av).astype(bf16), Bv, b_row)
+        if t < STEPS - 1:
+            gram = (mm(kn, k, NT) + 1.0).astype(bf16)
+            hk[...] = mm(kn, Av) + av - mm(gram, dhb)
+        if t > 0:
+            answer(old, qp, gelu(mm(qp, Av) + av).astype(bf16), Bv, b_row)
         Bn = B[...] - mm(dmb, act)
         B[...] = Bn
         Bb[...] = Bn.astype(bf16)
@@ -247,7 +251,10 @@
         b_col = b_col - jnp.sum(dm, 1, keepdims=True)
         return b_col, jnp.transpose(b_col)
 
-    _, b_row = lax.fori_loop(0, STEPS, step, (jnp.transpose(bb), bb), unroll=8)
+    state = (jnp.transpose(bb), bb)
+    for t in range(STEPS):
+        state = step(t, state)
+    _, b_row = state
     last = pl.ds(CLIP - MB, MB)
     q = Q[last, :]
     answer(last, q, gelu(mm(q, Ab[...]) + a[...]).astype(bf16), Bb[...], b_row)
@@ -272,7 +279,7 @@
             pltpu.VMEM((HEADS_DEV, HD), f32),
             pltpu.VMEM((HEADS_DEV, HD), f32),
             pltpu.VMEM((CLIP, D), bf16),
-            pltpu.VMEM((8, 2, 4, ROWS, 128), bf16),
+            pltpu.VMEM((8, 2, SLAB, 128), bf16),
             pltpu.VMEM((CLIP, HD), f32),
             pltpu.VMEM((D, 256), bf16),
             pltpu.VMEM((CLIP, 2 * HD), bf16),
@@ -292,6 +299,18 @@
     )(idx, rate0, *pieces, *weights, *params)
 
 
+def turn_kernel(x_ref, o_ref):
+    o_ref[...] = jnp.transpose(x_ref[...].reshape(HEADS_DEV * HD, TOK))
+
+
+def by_token(x):
+    return pl.pallas_call(
+        turn_kernel,
+        out_shape=jax.ShapeDtypeStruct((TOK, HEADS_DEV * HD), f32),
+        name="by_token",
+    )(x)
+
+
 def ring(x, axis, by):
     size = lax.axis_size(axis)
     return lax.ppermute(x, axis, [(i, (i + by) % size) for i in range(size)])
@@ -313,14 +332,19 @@
     zc, zi, x, core = (lax.axis_index(n).astype(jnp.int32) for n in ("zc", "zi", "x", "core"))
     odd = zc % 2
     blocks = pack(jnp.transpose(w_qkv, (1, 0, 2)), jnp.transpose(w_rate))
-    blocks = lax.all_to_all(blocks, "x", 0, 0, tiled=True)
+    blocks = lax.all_to_all(blocks.reshape(4, 2 * ROWS, 128), "x", 0, 0, tiled=True)
+    blocks = blocks.reshape(4, 2, ROWS, 128)
     mine = lax.dynamic_slice(tokens, (0, core * HALF), (TOK, HALF))
     across = ring(mine, "zi", 1)
     blocks, across = lax.optimization_barrier((blocks, across))
-    keep = lax.dynamic_index_in_dim(blocks, zi, 1, keepdims=False)
-    flip = lax.dynamic_index_in_dim(blocks, 1 - zi, 1, keepdims=False)
-    blocks = jnp.broadcast_to(jnp.stack([keep, flip])[None], (4, 2, 4, ROWS, 128))
-    near = lax.all_to_all(blocks.reshape(8, 4, ROWS, 128), "zc", 0, 0, tiled=True)
+    def gathered(which):
+        block = lax.dynamic_index_in_dim(blocks, which, 1, keepdims=False)
+        parts = block[:, :48], block[:, 48:72], block[:, 72:76]
+        return jnp.concatenate([part.reshape(-1, 128) for part in parts], 0)
+
+    both = jnp.stack([gathered(zi), gathered(1 - zi)])[None]
+    both = jnp.broadcast_to(both, (4, 2, SLAB, 128)).reshape(8, SLAB, 128)
+    near = lax.all_to_all(both, "zc", 0, 0, tiled=True)
     swap = [(i, (i + 1) % 16 if i % 2 else (i - 1) % 16) for i in range(16)]
 
     pair = jnp.concatenate([mine, across], 0)
@@ -344,13 +368,13 @@
     offset = got - (total / (HEADS_DEV * HD))
     squares = jnp.sum(offset * offset, (0, 1))
     stats = jnp.broadcast_to(jnp.stack([total, squares])[None], (8, 2, TOK))
+    joined = by_token(got)
     stats = lax.all_to_all(stats, ("y", "core"), 0, 0, tiled=True)
     mean = jnp.sum(stats[:, 0], 0) / D
     shift = stats[:, 0] / (HEADS_DEV * HD) - mean
     variance = jnp.sum(stats[:, 1] + (HEADS_DEV * HD) * shift * shift, 0) / D
-    normed = (got - mean) * lax.rsqrt(variance + 1e-05)
-    joined = jnp.transpose(normed.reshape(HEADS_DEV * HD, TOK))
-    return (joined * out_gain).astype(bf16)
+    scale = lax.rsqrt(variance + 1e-05)
+    return ((joined - mean[:, None]) * scale[:, None] * out_gain).astype(bf16)
 
 
 def solution(mesh):

time: 133 us -> 132 us (level)
  waiting for transfers between devices: 33 us -> 29.9 us
  other arithmetic: 0.97 us -> 2.54 us
    all_to_all x1, waiting for transfers between devices: 4.6 us -> 2.19 us  [local(): stats = lax.all_to_all(stats, ('y', 'core'), 0, 0, tiled=True)]
    pallas_call x0 -> x1, Pallas kernels: none -> 1.74 us  [by_token(): pl.pallas_call(turn_kernel, out_shape=jax.ShapeDtypeStruct((TOK, HEADS_DE...]
    convert_element_type x1, other arithmetic: 0.12 us -> 1.68 us  [local(): return ((joined - mean[:, None]) * scale[:, None] * out_gain).astype(bf16)]
  transfers between devices with their start and end apart: 15 -> 15, of which waited for: 6 -> 6; matrix products, arithmetic and copies ran while one was open for 2% -> 2% of each run, Pallas kernels for 1% -> 3%
where the time goes in v5:
time: 132 us; the launch traced here: 131 us
  starting transfers between devices  67.2 us (51%)
  waiting for transfers between devices  29.9 us (23%)
  Pallas kernels  25.8 us (20%)
  local copies, waits for them, and re-layouts  4.97 us (4%)
  other arithmetic  2.54 us (2%)
    ppermute x10, starting transfers between devices, ring(): return lax.ppermute(x, axis, [(i, (i + by) % size) for i in range(size)])  33.1 us
    pallas_call x1, Pallas kernels, chain(): pl.pallas_call(chain_kernel, out_shape=jax.ShapeDtypeStruct((8, HD, TOK),...  22.3 us
    all_to_all x1, starting transfers between devices, local(): near = lax.all_to_all(both, 'zc', 0, 0, tiled=True)  13.9 us
    ppermute x10, waiting for transfers between devices, ring(): return lax.ppermute(x, axis, [(i, (i + by) % size) for i in range(size)])  9.21 us
    ppermute x1, waiting for transfers between devices, local(): other = lax.ppermute(near, ('zc', 'zi'), swap)  7.37 us
    all_to_all x1, starting transfers between devices, local(): stats = lax.all_to_all(stats, ('y', 'core'), 0, 0, tiled=True)  6.88 us
    all_to_all x1, waiting for transfers between devices, local(): got = lax.all_to_all(outs, ('zi', 'x'), 0, 0, tiled=True)  6.11 us
    ppermute x1, starting transfers between devices, local(): other = lax.ppermute(near, ('zc', 'zi'), swap)  5.04 us
  transfers between devices with their start and end apart: 15, of which 6 were waited for; matrix products, arithmetic and copies ran while one was open for 2% of the time, Pallas kernels for 3%

profile of v5, /device:TPU:1, one launch (start us, length us, event | category | flops | bytes accessed | tf_op | source)
XLA Modules:
  0.0 130.7 jit_solution(17905318388304535356)
XLA Ops:
  0.0 1.0 constant_dynamic-slice_fusion
  1.0 4.4 %collective-permute-start = (bf16[128,1536]{1,0:T(8,128)(2,1)S(1)}, bf16[128,1536]{1,0:T(8,128)(2,1)S(1)}, u32[]{:S(2)}, u32[]{:S(2)}) collective-permute-start(bf16[128,1536]{1,0:T(8,128)(2,1)S(1)} %constant_dynamic-slice_fusion), channel_id=1, source_target_pairs={{0,32},{32,0},{1,33},{33,1},{2,34},{34,2},{3,35},{35,3},{4,36},{36... | collective-permute-start | bytes 1179656 | tf_op jit(solution)/shard_map/ppermute | solution.py:316
  5.4 1.7 %pack_weights.1 = bf16[4,2,80,128]{3,2,1,0:T(8,128)(2,1)} custom-call(bf16[3,48,384]{2,1,0:T(8,128)(2,1)} %bitcast.42, bf16[6,48]{1,0:T(8,128)(2,1)} %bitcast.50), custom_call_target="tpu_custom_call" | custom-call | tf_op jit(solution)/shard_map/pack_weights/pallas_call | solution.py:65
  7.1 4.0 %all-to-all-start = ((bf16[4,160,128]{2,1,0:T(8,128)(2,1)}), bf16[4,160,128]{2,1,0:T(8,128)(2,1)S(1)}, u32[]{:S(2)}, u32[]{:S(2)}) async-start(bf16[4,160,128]{2,1,0:T(8,128)(2,1)} %bitcast.39), calls=%async_computation | async-start | bytes 327680 | tf_op jit(solution)/shard_map/all_to_all | solution.py:335
  11.1 5.0 %all-to-all-done = bf16[4,160,128]{2,1,0:T(8,128)(2,1)S(1)} async-done(((bf16[4,160,128]{2,1,0:T(8,128)(2,1)}), bf16[4,160,128]{2,1,0:T(8,128)(2,1)S(1)}, u32[]{:S(2)}, u32[]{:S(2)}) %all-to-all-start) | async-done | bytes 163872 | tf_op jit(solution)/shard_map/all_to_all | solution.py:335
  16.1 0.0 collective-permute-done.z_half
  16.2 0.9 broadcast_in_dim.4
  17.2 13.9 %all-to-all-start.1 = ((bf16[8,304,128]{2,1,0:T(8,128)(2,1)}), bf16[8,304,128]{2,1,0:T(8,128)(2,1)S(1)}, u32[]{:S(2)}, u32[]{:S(2)}) async-start(bf16[8,304,128]{2,1,0:T(8,128)(2,1)} %bitcast.18), calls=%async_computation.1 | async-start | bytes 1245184 | tf_op jit(solution)/shard_map/all_to_all | solution.py:347
  31.1 0.1 pad_maximum_fusion
  31.1 2.9 %collective-permute-start.2 = (bf16[256,1536]{1,0:T(8,128)(2,1)S(1)}, bf16[256,1536]{1,0:T(8,128)(2,1)S(1)}, u32[]{:S(2)}, u32[]{:S(2)}) collective-permute-start(bf16[256,1536]{1,0:T(8,128)(2,1)S(1)} %pad_maximum_fusion), channel_id=1, source_target_pairs={{0,24},{8,0},{16,8},{24,16},{1,25},{9,1},{17,9},{25,17},{2,26},{10... | collective-permute-start | bytes 2359304 | tf_op jit(solution)/shard_map/ppermute | solution.py:316
  34.0 2.4 %collective-permute-start.1 = (bf16[256,1536]{1,0:T(8,128)(2,1)S(1)}, bf16[256,1536]{1,0:T(8,128)(2,1)S(1)}, u32[]{:S(2)}, u32[]{:S(2)}) collective-permute-start(bf16[256,1536]{1,0:T(8,128)(2,1)S(1)} %pad_maximum_fusion), channel_id=1, source_target_pairs={{0,8},{8,16},{16,24},{24,0},{1,9},{9,17},{17,25},{25,1},{2,10},{10... | collective-permute-start | bytes 2359304 | tf_op jit(solution)/shard_map/ppermute | solution.py:316
  36.4 5.1 %collective-permute-start.5 = (bf16[128,1536]{1,0:T(8,128)(2,1)S(1)}, bf16[128,1536]{1,0:T(8,128)(2,1)}, u32[]{:S(2)}, u32[]{:S(2)}) collective-permute-start(bf16[128,1536]{1,0:T(8,128)(2,1)S(1)} %collective-permute-done.z_half), channel_id=1, source_target_pairs={{0,1},{1,0},{2,3},{3,2},{4,5},{5,4},{6,7},{7,6},{8,9},{9,8},{10,11... | collective-permute-start | bytes 1179656 | tf_op jit(solution)/shard_map/ppermute | solution.py:316
  41.6 7.8 %collective-permute-done.2.l_half = bf16[256,1536]{1,0:T(8,128)(2,1)S(1)} collective-permute-done((bf16[256,1536]{1,0:T(8,128)(2,1)S(1)}, bf16[256,1536]{1,0:T(8,128)(2,1)S(1)}, u32[]{:S(2)}, u32[]{:S(2)}) %collective-permute-start.2) | collective-permute-done | bytes 786464 | tf_op jit(solution)/shard_map/ppermute | solution.py:316
  49.4 0.8 slice.50
  50.2 4.2 %collective-permute-start.4 = (bf16[128,1536]{1,0:T(8,128)(2,1)}, bf16[128,1536]{1,0:T(8,128)(2,1)}, u32[]{:S(2)}, u32[]{:S(2)}) collective-permute-start(bf16[128,1536]{1,0:T(8,128)(2,1)} %slice.50), channel_id=1, source_target_pairs={{0,24},{8,0},{16,8},{24,16},{1,25},{9,1},{17,9},{25,17},{2,26},{10... | collective-permute-start | bytes 1179656 | tf_op jit(solution)/shard_map/ppermute | solution.py:316
  54.5 0.0 collective-permute-done.1.r_half
  54.5 0.0 copy-start.2
  54.5 0.8 slice.49
  55.3 1.9 %collective-permute-start.3 = (bf16[128,1536]{1,0:T(8,128)(2,1)}, bf16[128,1536]{1,0:T(8,128)(2,1)}, u32[]{:S(2)}, u32[]{:S(2)}) collective-permute-start(bf16[128,1536]{1,0:T(8,128)(2,1)} %slice.49), channel_id=1, source_target_pairs={{0,8},{8,16},{16,24},{24,0},{1,9},{9,17},{17,25},{25,1},{2,10},{10... | collective-permute-start | bytes 1179656 | tf_op jit(solution)/shard_map/ppermute | solution.py:316
  57.2 0.0 copy-done.1
  57.2 5.7 %collective-permute-start.7 = (bf16[256,1536]{1,0:T(8,128)(2,1)S(1)}, bf16[256,1536]{1,0:T(8,128)(2,1)S(1)}, u32[]{:S(2)}, u32[]{:S(2)}) collective-permute-start(bf16[256,1536]{1,0:T(8,128)(2,1)S(1)} %collective-permute-done.2.l_half), channel_id=1, source_target_pairs={{0,1},{1,0},{2,3},{3,2},{4,5},{5,4},{6,7},{7,6},{8,9},{9,8},{10,11... | collective-permute-start | bytes 2359304 | tf_op jit(solution)/shard_map/ppermute | solution.py:316
  62.9 1.9 %collective-permute-start.6 = (bf16[256,1536]{1,0:T(8,128)(2,1)S(1)}, bf16[256,1536]{1,0:T(8,128)(2,1)}, u32[]{:S(2)}, u32[]{:S(2)}) collective-permute-start(bf16[256,1536]{1,0:T(8,128)(2,1)S(1)} %collective-permute-done.1.r_half), channel_id=1, source_target_pairs={{0,1},{1,0},{2,3},{3,2},{4,5},{5,4},{6,7},{7,6},{8,9},{9,8},{10,11... | collective-permute-start | bytes 2359304 | tf_op jit(solution)/shard_map/ppermute | solution.py:316
  64.8 0.0 collective-permute-done.5.z_sibling
  64.9 0.0 all-to-all-done.1.near
  64.9 0.0 copy-start
  64.9 5.0 %collective-permute-start.10 = (bf16[8,304,128]{2,1,0:T(8,128)(2,1)S(1)}, bf16[8,304,128]{2,1,0:T(8,128)(2,1)}, u32[]{:S(2)}, u32[]{:S(2)}) collective-permute-start(bf16[8,304,128]{2,1,0:T(8,128)(2,1)S(1)} %all-to-all-done.1.near), channel_id=1, source_target_pairs={{0,480},{32,64},{64,32},{96,128},{128,96},{160,192},{192,160},{224... | collective-permute-start | bytes 1867784 | tf_op jit(solution)/shard_map/ppermute | solution.py:353
  69.9 0.0 collective-permute-done.4.g_half
  69.9 2.7 %collective-permute-start.9 = (bf16[128,1536]{1,0:T(8,128)(2,1)}, bf16[128,1536]{1,0:T(8,128)(2,1)S(1)}, u32[]{:S(2)}, u32[]{:S(2)}) collective-permute-start(bf16[128,1536]{1,0:T(8,128)(2,1)} %collective-permute-done.4.g_half), channel_id=1, source_target_pairs={{0,1},{1,0},{2,3},{3,2},{4,5},{5,4},{6,7},{7,6},{8,9},{9,8},{10,11... | collective-permute-start | bytes 1179656 | tf_op jit(solution)/shard_map/ppermute | solution.py:316
  72.6 0.0 collective-permute-done.3.f_half
  72.6 1.9 %collective-permute-start.8 = (bf16[128,1536]{1,0:T(8,128)(2,1)}, bf16[128,1536]{1,0:T(8,128)(2,1)}, u32[]{:S(2)}, u32[]{:S(2)}) collective-permute-start(bf16[128,1536]{1,0:T(8,128)(2,1)} %collective-permute-done.3.f_half), channel_id=1, source_target_pairs={{0,1},{1,0},{2,3},{3,2},{4,5},{5,4},{6,7},{7,6},{8,9},{9,8},{10,11... | collective-permute-start | bytes 1179656 | tf_op jit(solution)/shard_map/ppermute | solution.py:316
  74.6 0.6 pad_add_fusion.idx
  75.2 0.0 collective-permute-done.9.g_sibling
  75.2 0.0 collective-permute-done.7.l_sibling
  75.2 1.4 %collective-permute-done.8.f_sibling = bf16[128,1536]{1,0:T(8,128)(2,1)} collective-permute-done((bf16[128,1536]{1,0:T(8,128)(2,1)}, bf16[128,1536]{1,0:T(8,128)(2,1)}, u32[]{:S(2)}, u32[]{:S(2)}) %collective-permute-start.8) | collective-permute-done | bytes 393248 | tf_op jit(solution)/shard_map/ppermute | solution.py:316
  76.6 0.0 collective-permute-done.6.r_sibling
  76.6 7.4 %collective-permute-done.10.other = bf16[8,304,128]{2,1,0:T(8,128)(2,1)} collective-permute-done((bf16[8,304,128]{2,1,0:T(8,128)(2,1)S(1)}, bf16[8,304,128]{2,1,0:T(8,128)(2,1)}, u32[]{:S(2)}, u32[]{:S(2)}) %collective-permute-start.10) | collective-permute-done | bytes 622624 | tf_op jit(solution)/shard_map/ppermute | solution.py:353
  84.0 0.0 copy-done.2
  84.0 0.0 copy-done.5
  84.0 22.3 %clip_head.1 = f32[8,64,128]{2,1,0:T(8,128)} custom-call(s32[4]{0:T(128)} %pad_add_fusion.idx, f32[6]{0:T(128)} %rate0.1, bf16[128,3072]{1,0:T(8,128)(2,1)} %own.1, bf16[128,1536]{1,0:T(8,128)(2,1)} %copy-done.3, bf16[256,1536]{1,0:T(8,128)(2,1)} %copy-done.2, bf16[256,1536]{1,0:T(8,128)(2,1)} %copy-done.1, bf16[128,1536]{1,0:T(8,128)(2,1)} %collective-permute-done.3.f_half, ...), custom_call_target="tpu_custom_call" | custom-call | tf_op jit(solution)/shard_map/clip_head/pallas_call | solution.py:269
  106.3 4.2 %all-to-all-start.2 = ((f32[8,64,128]{2,1,0:T(8,128)}), f32[8,64,128]{2,1,0:T(8,128)S(1)}, u32[]{:S(2)}, u32[]{:S(2)}) async-start(f32[8,64,128]{2,1,0:T(8,128)} %clip_head.1), calls=%async_computation.2 | async-start | bytes 524288 | tf_op jit(solution)/shard_map/all_to_all | solution.py:362
  110.6 6.1 %all-to-all-done.2 = f32[8,64,128]{2,1,0:T(8,128)S(1)} async-done(((f32[8,64,128]{2,1,0:T(8,128)}), f32[8,64,128]{2,1,0:T(8,128)S(1)}, u32[]{:S(2)}, u32[]{:S(2)}) %all-to-all-start.2) | async-done | bytes 262176 | tf_op jit(solution)/shard_map/all_to_all | solution.py:362
  116.7 0.1 multiply_reduce_fusion
  116.8 0.6 broadcast_in_dim.5
  117.4 6.9 %all-to-all-start.3 = ((f32[8,2,128]{2,1,0:T(2,128)}), f32[8,2,128]{2,1,0:T(2,128)S(1)}, u32[]{:S(2)}, u32[]{:S(2)}) async-start(f32[8,2,128]{2,1,0:T(2,128)} %broadcast_in_dim.5), calls=%async_computation.3 | async-start | bytes 16384 | tf_op jit(solution)/shard_map/all_to_all | solution.py:372
  124.3 0.7 copy.15
  125.0 1.7 %by_token.1 = f32[128,384]{1,0:T(8,128)} custom-call(f32[6,64,128]{2,1,0:T(8,128)} %bitcast.37), custom_call_target="tpu_custom_call" | custom-call | tf_op jit(solution)/shard_map/by_token/pallas_call | solution.py:307
  126.7 2.2 %all-to-all-done.3 = f32[8,2,128]{2,1,0:T(2,128)S(1)} async-done(((f32[8,2,128]{2,1,0:T(2,128)}), f32[8,2,128]{2,1,0:T(2,128)S(1)}, u32[]{:S(2)}, u32[]{:S(2)}) %all-to-all-start.3) | async-done | bytes 8224 | tf_op jit(solution)/shard_map/all_to_all | solution.py:372
  129.0 1.7 %multiply_convert_fusion = bf16[128,384]{1,0:T(8,128)(2,1)} fusion(f32[128,384]{1,0:T(8,128)} %by_token.1, f32[384]{0:T(512)S(1)} %copy-done.6, f32[128]{0:T(128)S(1)} %add_rsqrt_fusion, f32[128]{0:T(128)S(1)} %broadcast_multiply_fusion), kind=kLoop, calls=%fused_computation.2 | loop fusion | flops 196608 | bytes 297472 | tf_op jit(solution)/shard_map/convert_element_type | solution.py:377
  (26 shorter events, 0.2 us)
Async XLA Ops:
  1.0 15.1 %collective-permute-start = (bf16[128,1536]{1,0:T(8,128)(2,1)S(1)}, bf16[128,1536]{1,0:T(8,128)(2,1)S(1)}, u32[]{:S(2)}, u32[]{:S(2)}) collective-permute-start(bf16[128,1536]{1,0:T(8,128)(2,1)S(1)} %constant_dynamic-slice_fusion), channel_id=1, source_target_pairs={{0,32},{32,0},{1,33},{33,1},{2,34},{34,2},{3,35},{35,3},{4,36},{36... | collective-permute-start | bytes 1179656 | tf_op jit(solution)/shard_map/ppermute | solution.py:316
  7.1 9.0 %all-to-all-start = ((bf16[4,160,128]{2,1,0:T(8,128)(2,1)}), bf16[4,160,128]{2,1,0:T(8,128)(2,1)S(1)}, u32[]{:S(2)}, u32[]{:S(2)}) async-start(bf16[4,160,128]{2,1,0:T(8,128)(2,1)} %bitcast.39), calls=%async_computation | async-start | bytes 327680 | tf_op jit(solution)/shard_map/all_to_all | solution.py:335
  16.1 20.3 %copy-start.3 = (bf16[128,1536]{1,0:T(8,128)(2,1)}, bf16[128,1536]{1,0:T(8,128)(2,1)S(1)}, u32[]{:S(2)}) copy-start(bf16[128,1536]{1,0:T(8,128)(2,1)S(1)} %collective-permute-done.z_half) | copy-start | bytes 1179652
  17.2 47.7 %all-to-all-start.1 = ((bf16[8,304,128]{2,1,0:T(8,128)(2,1)}), bf16[8,304,128]{2,1,0:T(8,128)(2,1)S(1)}, u32[]{:S(2)}, u32[]{:S(2)}) async-start(bf16[8,304,128]{2,1,0:T(8,128)(2,1)} %bitcast.18), calls=%async_computation.1 | async-start | bytes 1245184 | tf_op jit(solution)/shard_map/all_to_all | solution.py:347
  31.1 18.3 %collective-permute-start.2 = (bf16[256,1536]{1,0:T(8,128)(2,1)S(1)}, bf16[256,1536]{1,0:T(8,128)(2,1)S(1)}, u32[]{:S(2)}, u32[]{:S(2)}) collective-permute-start(bf16[256,1536]{1,0:T(8,128)(2,1)S(1)} %pad_maximum_fusion), channel_id=1, source_target_pairs={{0,24},{8,0},{16,8},{24,16},{1,25},{9,1},{17,9},{25,17},{2,26},{10... | collective-permute-start | bytes 2359304 | tf_op jit(solution)/shard_map/ppermute | solution.py:316
  34.0 20.4 %collective-permute-start.1 = (bf16[256,1536]{1,0:T(8,128)(2,1)S(1)}, bf16[256,1536]{1,0:T(8,128)(2,1)S(1)}, u32[]{:S(2)}, u32[]{:S(2)}) collective-permute-start(bf16[256,1536]{1,0:T(8,128)(2,1)S(1)} %pad_maximum_fusion), channel_id=1, source_target_pairs={{0,8},{8,16},{16,24},{24,0},{1,9},{9,17},{17,25},{25,1},{2,10},{10... | collective-permute-start | bytes 2359304 | tf_op jit(solution)/shard_map/ppermute | solution.py:316
  36.4 28.4 %collective-permute-start.5 = (bf16[128,1536]{1,0:T(8,128)(2,1)S(1)}, bf16[128,1536]{1,0:T(8,128)(2,1)}, u32[]{:S(2)}, u32[]{:S(2)}) collective-permute-start(bf16[128,1536]{1,0:T(8,128)(2,1)S(1)} %collective-permute-done.z_half), channel_id=1, source_target_pairs={{0,1},{1,0},{2,3},{3,2},{4,5},{5,4},{6,7},{7,6},{8,9},{9,8},{10,11... | collective-permute-start | bytes 1179656 | tf_op jit(solution)/shard_map/ppermute | solution.py:316
  49.4 7.9 %copy-start.1 = (bf16[256,1536]{1,0:T(8,128)(2,1)}, bf16[256,1536]{1,0:T(8,128)(2,1)S(1)}, u32[]{:S(2)}) copy-start(bf16[256,1536]{1,0:T(8,128)(2,1)S(1)} %collective-permute-done.2.l_half) | copy-start | bytes 2359300
  50.2 19.7 %collective-permute-start.4 = (bf16[128,1536]{1,0:T(8,128)(2,1)}, bf16[128,1536]{1,0:T(8,128)(2,1)}, u32[]{:S(2)}, u32[]{:S(2)}) collective-permute-start(bf16[128,1536]{1,0:T(8,128)(2,1)} %slice.50), channel_id=1, source_target_pairs={{0,24},{8,0},{16,8},{24,16},{1,25},{9,1},{17,9},{25,17},{2,26},{10... | collective-permute-start | bytes 1179656 | tf_op jit(solution)/shard_map/ppermute | solution.py:316
  54.5 29.5 %copy-start.2 = (bf16[256,1536]{1,0:T(8,128)(2,1)}, bf16[256,1536]{1,0:T(8,128)(2,1)S(1)}, u32[]{:S(2)}) copy-start(bf16[256,1536]{1,0:T(8,128)(2,1)S(1)} %collective-permute-done.1.r_half) | copy-start | bytes 2359300
  55.3 17.3 %collective-permute-start.3 = (bf16[128,1536]{1,0:T(8,128)(2,1)}, bf16[128,1536]{1,0:T(8,128)(2,1)}, u32[]{:S(2)}, u32[]{:S(2)}) collective-permute-start(bf16[128,1536]{1,0:T(8,128)(2,1)} %slice.49), channel_id=1, source_target_pairs={{0,8},{8,16},{16,24},{24,0},{1,9},{9,17},{17,25},{25,1},{2,10},{10... | collective-permute-start | bytes 1179656 | tf_op jit(solution)/shard_map/ppermute | solution.py:316
  57.2 18.0 %collective-permute-start.7 = (bf16[256,1536]{1,0:T(8,128)(2,1)S(1)}, bf16[256,1536]{1,0:T(8,128)(2,1)S(1)}, u32[]{:S(2)}, u32[]{:S(2)}) collective-permute-start(bf16[256,1536]{1,0:T(8,128)(2,1)S(1)} %collective-permute-done.2.l_half), channel_id=1, source_target_pairs={{0,1},{1,0},{2,3},{3,2},{4,5},{5,4},{6,7},{7,6},{8,9},{9,8},{10,11... | collective-permute-start | bytes 2359304 | tf_op jit(solution)/shard_map/ppermute | solution.py:316
  62.9 13.7 %collective-permute-start.6 = (bf16[256,1536]{1,0:T(8,128)(2,1)S(1)}, bf16[256,1536]{1,0:T(8,128)(2,1)}, u32[]{:S(2)}, u32[]{:S(2)}) collective-permute-start(bf16[256,1536]{1,0:T(8,128)(2,1)S(1)} %collective-permute-done.1.r_half), channel_id=1, source_target_pairs={{0,1},{1,0},{2,3},{3,2},{4,5},{5,4},{6,7},{7,6},{8,9},{9,8},{10,11... | collective-permute-start | bytes 2359304 | tf_op jit(solution)/shard_map/ppermute | solution.py:316
  64.9 19.1 %copy-start = (bf16[8,304,128]{2,1,0:T(8,128)(2,1)}, bf16[8,304,128]{2,1,0:T(8,128)(2,1)S(1)}, u32[]{:S(2)}) copy-start(bf16[8,304,128]{2,1,0:T(8,128)(2,1)S(1)} %all-to-all-done.1.near) | copy-start | bytes 1867780
  64.9 19.1 %collective-permute-start.10 = (bf16[8,304,128]{2,1,0:T(8,128)(2,1)S(1)}, bf16[8,304,128]{2,1,0:T(8,128)(2,1)}, u32[]{:S(2)}, u32[]{:S(2)}) collective-permute-start(bf16[8,304,128]{2,1,0:T(8,128)(2,1)S(1)} %all-to-all-done.1.near), channel_id=1, source_target_pairs={{0,480},{32,64},{64,32},{96,128},{128,96},{160,192},{192,160},{224... | collective-permute-start | bytes 1867784 | tf_op jit(solution)/shard_map/ppermute | solution.py:353
  69.9 5.3 %collective-permute-start.9 = (bf16[128,1536]{1,0:T(8,128)(2,1)}, bf16[128,1536]{1,0:T(8,128)(2,1)S(1)}, u32[]{:S(2)}, u32[]{:S(2)}) collective-permute-start(bf16[128,1536]{1,0:T(8,128)(2,1)} %collective-permute-done.4.g_half), channel_id=1, source_target_pairs={{0,1},{1,0},{2,3},{3,2},{4,5},{5,4},{6,7},{7,6},{8,9},{9,8},{10,11... | collective-permute-start | bytes 1179656 | tf_op jit(solution)/shard_map/ppermute | solution.py:316
  72.6 4.0 %collective-permute-start.8 = (bf16[128,1536]{1,0:T(8,128)(2,1)}, bf16[128,1536]{1,0:T(8,128)(2,1)}, u32[]{:S(2)}, u32[]{:S(2)}) collective-permute-start(bf16[128,1536]{1,0:T(8,128)(2,1)} %collective-permute-done.3.f_half), channel_id=1, source_target_pairs={{0,1},{1,0},{2,3},{3,2},{4,5},{5,4},{6,7},{7,6},{8,9},{9,8},{10,11... | collective-permute-start | bytes 1179656 | tf_op jit(solution)/shard_map/ppermute | solution.py:316
  75.2 8.8 %copy-start.5 = (bf16[128,1536]{1,0:T(8,128)(2,1)}, bf16[128,1536]{1,0:T(8,128)(2,1)S(1)}, u32[]{:S(2)}) copy-start(bf16[128,1536]{1,0:T(8,128)(2,1)S(1)} %collective-permute-done.9.g_sibling) | copy-start | bytes 1179652
  75.2 8.8 %copy-start.4 = (bf16[256,1536]{1,0:T(8,128)(2,1)}, bf16[256,1536]{1,0:T(8,128)(2,1)S(1)}, u32[]{:S(2)}) copy-start(bf16[256,1536]{1,0:T(8,128)(2,1)S(1)} %collective-permute-done.7.l_sibling) | copy-start | bytes 2359300
  106.3 10.4 %all-to-all-start.2 = ((f32[8,64,128]{2,1,0:T(8,128)}), f32[8,64,128]{2,1,0:T(8,128)S(1)}, u32[]{:S(2)}, u32[]{:S(2)}) async-start(f32[8,64,128]{2,1,0:T(8,128)} %clip_head.1), calls=%async_computation.2 | async-start | bytes 524288 | tf_op jit(solution)/shard_map/all_to_all | solution.py:362
  110.6 18.4 %copy-start.6 = (f32[384]{0:T(512)S(1)}, f32[384]{0:T(512)}, u32[]{:S(2)}) copy-start(f32[384]{0:T(512)} %param.21) | copy-start | bytes 4612
  117.4 11.5 %all-to-all-start.3 = ((f32[8,2,128]{2,1,0:T(2,128)}), f32[8,2,128]{2,1,0:T(2,128)S(1)}, u32[]{:S(2)}, u32[]{:S(2)}) async-start(f32[8,2,128]{2,1,0:T(2,128)} %broadcast_in_dim.5), calls=%async_computation.3 | async-start | bytes 16384 | tf_op jit(solution)/shard_map/all_to_all | solution.py:372
